TPU v7x, 512 devices: a whole 4x8x8 slice. The times are simulated.
512 devices in a mesh: row: 16 (over z, core), col: 8 (over y), depth: 4 (over x).
Axes of the slice: x: 4, y: 8, z: 8, core: 2. Of those that a mesh axis runs over, the one named last changes fastest.
Arguments:
- p_blocks: bfloat16 [256, 32, 128, 128], P('row', ('col', 'depth')), may hold values from -0.8984375 to 0.8984375
- p_cols: int32 [256, 32], P('row', ('col', 'depth')), may hold values from 0 to 255, as said below
Outputs:
- square: bfloat16 [256, 32, 128, 128], P('row', ('col', 'depth'))
Inputs may be any that keep to these rules, and one draw needn't show every extreme that they name: p_cols[i, m] is congruent to m modulo 32 and lies in the cyclic range from i - 32 to i + 32 - 1 modulo 256.
All inputs are finite; a program needn't handle non-finite values.
Results may differ from a plain program's by a relative error of at most 0.001.
Values may be sent and summed in bfloat16 or wider, within the bound.
No kernel may reach another device: no remote copies, remote signals or barrier semaphores. Data moves between devices by JAX's collectives and lax.ppermute only.
A program may use at most 128 MiB of HBM per device.

v0:
```python
import jax
import jax.numpy as jnp
from jax import lax
from jax.sharding import PartitionSpec as P


def passed_along(block, axis, distance):
    devices = range(lax.axis_size(axis))
    route = [((i - distance) % len(devices), i) for i in devices]
    return lax.ppermute(block, axis, route)


def shards(p_blocks, p_cols):
    panel_rows = p_blocks.shape[0]
    classes = lax.axis_size("col") * lax.axis_size("depth")
    matrix_rows = panel_rows * lax.axis_size("row")
    hop_count = (classes + panel_rows - 1) // panel_rows
    own_blocks = p_blocks[:, 0]
    own_cols = p_cols[:, 0]
    anchor = lax.axis_index("row") * panel_rows - hop_count * panel_rows
    below_blocks = []
    below_cols = []
    above_blocks = []
    above_cols = []
    moving_down = (own_blocks, own_cols)
    moving_up = (own_blocks, own_cols)
    for hop_index in range(hop_count):
        moving_down = passed_along((moving_down[0], moving_down[1]), "row", 1)
        moving_up = passed_along((moving_up[0], moving_up[1]), "row", -1)
        below_blocks.append(moving_down[0])
        below_cols.append(moving_down[1])
        above_blocks.append(moving_up[0])
        above_cols.append(moving_up[1])
    window_blocks = jnp.concatenate(below_blocks[::-1] + [own_blocks] + above_blocks, axis=0)
    window_cols = jnp.concatenate(below_cols[::-1] + [own_cols] + above_cols, axis=0)
    piece_blocks = lax.all_gather(p_blocks, ("col", "depth"), axis=1, tiled=True)
    piece_cols = lax.all_gather(p_cols, ("col", "depth"), axis=1, tiled=True)
    position = jnp.mod(piece_cols - anchor, matrix_rows).astype(jnp.int32)
    partner_blocks = window_blocks[position]
    matches = window_cols[position] == own_cols[:, None]
    masked_blocks = jnp.where(matches[:, :, None, None], piece_blocks, jnp.zeros_like(piece_blocks))
    totals = jnp.einsum(
        "itab,itbc->iac", masked_blocks, partner_blocks, preferred_element_type=jnp.float32
    )
    return totals.astype(jnp.bfloat16)[:, None]


def solution(mesh):
    return jax.shard_map(
        shards,
        mesh=mesh,
        in_specs=(P("row", ("col", "depth"), None, None), P("row", ("col", "depth"))),
        out_specs=P("row", ("col", "depth"), None, None),
        check_vma=False,
    )
```

profile of v0, /device:TPU:1, one launch (start us, length us, event | category | flops | bytes accessed | tf_op | source)
XLA Modules:
  0.0 181.8 jit_solution(12480873045619297380)
XLA Ops:
  6.5 0.7 all-gather.3.cloned.1.call-update
  7.3 3.5 %collective-permute-start.4 = (bf16[16,128,128]{2,1,0:T(8,128)(2,1)}, bf16[16,128,128]{2,1,0:T(8,128)(2,1)S(1)}, u32[]{:S(2)}, u32[]{:S(2)}) collective-permute-start(bf16[16,128,128]{2,1,0:T(8,128)(2,1)} %bitcast.23), channel_id=1, source_target_pairs={{480,0},{0,32},{32,64},{64,96},{96,128},{128,160},{160,192},{192,2... | collective-permute-start | bytes 1572872 | tf_op jit(solution)/shard_map/ppermute | solution.py:10
  10.8 0.0 collective-permute-start
  10.8 3.4 %collective-permute-start.2 = (s32[16]{0:T(128)}, s32[16]{0:T(128)S(1)}, u32[]{:S(2)}, u32[]{:S(2)}) collective-permute-start(s32[16]{0:T(128)} %bitcast.28), channel_id=1, source_target_pairs={{32,0},{64,32},{96,64},{128,96},{160,128},{192,160},{224,192},{256... | collective-permute-start | bytes 200 | tf_op jit(solution)/shard_map/ppermute | solution.py:10
  14.2 3.1 %collective-permute-start.6 = (bf16[16,128,128]{2,1,0:T(8,128)(2,1)}, bf16[16,128,128]{2,1,0:T(8,128)(2,1)}, u32[]{:S(2)}, u32[]{:S(2)}) collective-permute-start(bf16[16,128,128]{2,1,0:T(8,128)(2,1)} %bitcast.24), channel_id=1, source_target_pairs={{32,0},{64,32},{96,64},{128,96},{160,128},{192,160},{224,192},{256... | collective-permute-start | bytes 1572872 | tf_op jit(solution)/shard_map/ppermute | solution.py:10
  17.3 32.1 %all-gather = s32[32,1,16]{2,1,0:T(1,128)S(1)} all-gather(s32[1,1,16]{2,1,0:T(1,128)} %bitcast.29), channel_id=1, replica_groups=mesh['row'=16,'col'=8,'depth'=4] {'col','depth'}, dimensions={0}, use_global_device_ids=true | all-gather | bytes 2112 | tf_op jit(solution)/shard_map/all_gather | solution.py:37
  49.4 0.0 collective-permute-done.4
  49.4 0.0 copy-start.1
  49.4 0.0 collective-permute-start.5
  49.4 0.1 copy.6
  49.5 0.1 reshape.21
  49.6 0.0 collective-permute-done
  49.6 0.0 collective-permute-start.1
  49.6 0.0 collective-permute-done.2
  49.6 4.6 %collective-permute-start.3 = (s32[16]{0:T(128)S(1)}, s32[16]{0:T(128)S(1)}, u32[]{:S(2)}, u32[]{:S(2)}) collective-permute-start(s32[16]{0:T(128)S(1)} %collective-permute-done.2), channel_id=1, source_target_pairs={{32,0},{64,32},{96,64},{128,96},{160,128},{192,160},{224,192},{256... | collective-permute-start | bytes 200 | tf_op jit(solution)/shard_map/ppermute | solution.py:10
  54.3 1.3 collective-permute-done.1
  55.6 0.0 collective-permute-done.3
  55.6 0.7 concatenate.6
  56.3 3.3 %gather_fusion = s32[512]{0:T(512)S(1)} fusion(s32[80]{0:T(128)S(1)} %concatenate.6, s32[1024]{0:T(1024)S(1)} %pad_clamp_fusion), kind=kCustom, calls=%fused_computation | custom fusion | bytes 6144 | tf_op jit(solution)/shard_map/gather | solution.py:40
  59.7 0.1 reshape.20
  59.8 0.1 broadcast_compare_fusion
  59.8 0.0 collective-permute-done.6
  59.8 8.4 %collective-permute-start.7 = (bf16[16,128,128]{2,1,0:T(8,128)(2,1)}, bf16[16,128,128]{2,1,0:T(8,128)(2,1)S(1)}, u32[]{:S(2)}, u32[]{:S(2)}) collective-permute-start(bf16[16,128,128]{2,1,0:T(8,128)(2,1)} %collective-permute-done.6), channel_id=1, source_target_pairs={{32,0},{64,32},{96,64},{128,96},{160,128},{192,160},{224,192},{256... | collective-permute-start | bytes 1572872 | tf_op jit(solution)/shard_map/ppermute | solution.py:10
  68.2 0.0 collective-permute-done.5
  68.2 1.1 constant_dynamic-update-slice_fusion.4
  69.3 1.1 constant_dynamic-update-slice_fusion.3
  70.4 0.1 constant_dynamic-update-slice_fusion.2
  70.5 1.1 constant_dynamic-update-slice_fusion.1
  71.6 0.1 constant_dynamic-update-slice_fusion
  71.7 13.4 %gather_fusion.1 = bf16[512,128,128]{2,1,0:T(8,128)(2,1)} fusion(bf16[80,128,128]{2,1,0:T(8,128)(2,1)S(1)} %constant_dynamic-update-slice_fusion, s32[1024]{0:T(1024)S(1)} %pad_clamp_fusion), kind=kCustom, calls=%fused_computation.1 | custom fusion | bytes 33556480 | tf_op jit(solution)/shard_map/gather | solution.py:39
  85.1 76.2 %all-gather.3.cloned.1.call-done = bf16[16,32,128,128]{3,2,1,0:T(8,128)(2,1)} async-done(((bf16[16,1,128,128]{3,2,1,0:T(8,128)(2,1)}), bf16[16,32,128,128]{3,2,1,0:T(8,128)(2,1)}) %all-gather.3.cloned.1.call-update) | async-done | bytes 16777232 | tf_op jit(solution)/shard_map/all_gather | solution.py:36
  161.3 13.7 %fusion.10 = bf16[16,1,128,128]{3,2,1,0:T(8,128)(2,1)} fusion(bf16[16,32,128,128]{3,2,1,0:T(8,128)(2,1)} %bitcast.22, bf16[16,32,128,128]{3,2,1,0:T(8,128)(2,1)} %all-gather.3.cloned.1.call-done, pred[16,32]{1,0:T(8,128)(4,1)S(1)} %broadcast_compare_fusion), kind=kOutput, calls=%fused_computation.8 | convolution fusion | flops 2156134400 | bytes 34079232 | tf_op jit(solution)/shard_map/itab,itbc->iac/dot_general | solution.py:42
  (10 shorter events, 0.0 us)
Async XLA Ops:
  6.5 154.7 %all-gather.3.cloned.1.call-start = ((), (), s32[]{:S(2)}) async-start(), calls=%async_computation | async-start | bytes 17301504 | tf_op jit(solution)/shard_map/all_gather | solution.py:36
  7.3 42.1 %collective-permute-start.4 = (bf16[16,128,128]{2,1,0:T(8,128)(2,1)}, bf16[16,128,128]{2,1,0:T(8,128)(2,1)S(1)}, u32[]{:S(2)}, u32[]{:S(2)}) collective-permute-start(bf16[16,128,128]{2,1,0:T(8,128)(2,1)} %bitcast.23), channel_id=1, source_target_pairs={{480,0},{0,32},{32,64},{64,96},{96,128},{128,160},{160,192},{192,2... | collective-permute-start | bytes 1572872 | tf_op jit(solution)/shard_map/ppermute | solution.py:10
  10.8 38.8 %collective-permute-start = (s32[16]{0:T(128)}, s32[16]{0:T(128)S(1)}, u32[]{:S(2)}, u32[]{:S(2)}) collective-permute-start(s32[16]{0:T(128)} %bitcast.27), channel_id=1, source_target_pairs={{480,0},{0,32},{32,64},{64,96},{96,128},{128,160},{160,192},{192,2... | collective-permute-start | bytes 200 | tf_op jit(solution)/shard_map/ppermute | solution.py:10
  10.8 38.8 %collective-permute-start.2 = (s32[16]{0:T(128)}, s32[16]{0:T(128)S(1)}, u32[]{:S(2)}, u32[]{:S(2)}) collective-permute-start(s32[16]{0:T(128)} %bitcast.28), channel_id=1, source_target_pairs={{32,0},{64,32},{96,64},{128,96},{160,128},{192,160},{224,192},{256... | collective-permute-start | bytes 200 | tf_op jit(solution)/shard_map/ppermute | solution.py:10
  14.2 45.6 %collective-permute-start.6 = (bf16[16,128,128]{2,1,0:T(8,128)(2,1)}, bf16[16,128,128]{2,1,0:T(8,128)(2,1)}, u32[]{:S(2)}, u32[]{:S(2)}) collective-permute-start(bf16[16,128,128]{2,1,0:T(8,128)(2,1)} %bitcast.24), channel_id=1, source_target_pairs={{32,0},{64,32},{96,64},{128,96},{160,128},{192,160},{224,192},{256... | collective-permute-start | bytes 1572872 | tf_op jit(solution)/shard_map/ppermute | solution.py:10
  49.4 10.3 %copy-start.1 = (bf16[16,128,128]{2,1,0:T(8,128)(2,1)}, bf16[16,128,128]{2,1,0:T(8,128)(2,1)S(1)}, u32[]{:S(2)}) copy-start(bf16[16,128,128]{2,1,0:T(8,128)(2,1)S(1)} %collective-permute-done.4) | copy-start | bytes 1572868
  49.4 18.8 %collective-permute-start.5 = (bf16[16,128,128]{2,1,0:T(8,128)(2,1)S(1)}, bf16[16,128,128]{2,1,0:T(8,128)(2,1)}, u32[]{:S(2)}, u32[]{:S(2)}) collective-permute-start(bf16[16,128,128]{2,1,0:T(8,128)(2,1)S(1)} %collective-permute-done.4), channel_id=1, source_target_pairs={{480,0},{0,32},{32,64},{64,96},{96,128},{128,160},{160,192},{192,2... | collective-permute-start | bytes 1572872 | tf_op jit(solution)/shard_map/ppermute | solution.py:10
  49.6 6.0 %collective-permute-start.1 = (s32[16]{0:T(128)S(1)}, s32[16]{0:T(128)S(1)}, u32[]{:S(2)}, u32[]{:S(2)}) collective-permute-start(s32[16]{0:T(128)S(1)} %collective-permute-done), channel_id=1, source_target_pairs={{480,0},{0,32},{32,64},{64,96},{96,128},{128,160},{160,192},{192,2... | collective-permute-start | bytes 200 | tf_op jit(solution)/shard_map/ppermute | solution.py:10
  49.6 5.9 %collective-permute-start.3 = (s32[16]{0:T(128)S(1)}, s32[16]{0:T(128)S(1)}, u32[]{:S(2)}, u32[]{:S(2)}) collective-permute-start(s32[16]{0:T(128)S(1)} %collective-permute-done.2), channel_id=1, source_target_pairs={{32,0},{64,32},{96,64},{128,96},{160,128},{192,160},{224,192},{256... | collective-permute-start | bytes 200 | tf_op jit(solution)/shard_map/ppermute | solution.py:10
  56.3 3.4 %copy-start.2 = (s32[16,1]{0,1:T(1,128)S(1)}, s32[16,1]{0,1:T(1,128)}, u32[]{:S(2)}) copy-start(s32[16,1]{0,1:T(1,128)} %param.3) | copy-start | bytes 196
  56.3 14.1 %copy-start = (bf16[16,1,128,128]{3,2,1,0:T(8,128)(2,1)S(1)}, bf16[16,1,128,128]{3,2,1,0:T(8,128)(2,1)}, u32[]{:S(2)}) copy-start(bf16[16,1,128,128]{3,2,1,0:T(8,128)(2,1)} %param.2) | copy-start | bytes 1572868
  59.8 11.8 %collective-permute-start.7 = (bf16[16,128,128]{2,1,0:T(8,128)(2,1)}, bf16[16,128,128]{2,1,0:T(8,128)(2,1)S(1)}, u32[]{:S(2)}, u32[]{:S(2)}) collective-permute-start(bf16[16,128,128]{2,1,0:T(8,128)(2,1)} %collective-permute-done.6), channel_id=1, source_target_pairs={{32,0},{64,32},{96,64},{128,96},{160,128},{192,160},{224,192},{256... | collective-permute-start | bytes 1572872 | tf_op jit(solution)/shard_map/ppermute | solution.py:10
Sparse Core Ops, SparseCore 0:
  10.5 150.6 all-gather.2
where the time goes:
time: 182 us
  waiting for transfers between devices  78.2 us (43%)
  blocking collectives  32.1 us (18%)
  starting transfers between devices  23.1 us (13%)
  local copies, waits for them, and re-layouts  21.2 us (12%)
  matrix products  13.7 us (8%)
  between operations  13.5 us (7%)
    all_gather x1, waiting for transfers between devices, shards(): lax.all_gather(p_blocks, ('col', 'depth'), axis=1, tiled=True)  76.2 us
    all_gather x1, blocking collectives, shards(): piece_cols = lax.all_gather(p_cols, ('col', 'depth'), axis=1, tiled=True)  32.1 us
    ppermute x8, starting transfers between devices, passed_along(): return lax.ppermute(block, axis, route)  23.1 us
    dot_general x1, matrix products, shards(): jnp.einsum('itab,itbc->iac', masked_blocks, partner_blocks, preferred_ele...  13.7 us
    gather x1, local copies, waits for them, and re-layouts, shards(): partner_blocks = window_blocks[position]  13.4 us
  transfers between devices with their start and end apart: 9, of which 2 were waited for; matrix products, arithmetic and copies ran while one was open for 12% of the time, Pallas kernels for 0%

commit v1 on v0

v1 whole, which is shorter than its diff:
```python
import functools

import jax
import jax.numpy as jnp
from jax import lax
from jax.experimental import pallas as pl
from jax.experimental.pallas import tpu as pltpu
from jax.sharding import PartitionSpec as P

BS = 128
TAIL = 16
STEP = 2
QMAX = 32700.0
TINY = 2.0**-111


def passed_along(block, axis, distance):
    n = lax.axis_size(axis)
    return lax.ppermute(block, axis, [(i, (i + distance) % n) for i in range(n)])


def product_kernel(
    rows, panels, classes, idx_ref, x_ref, *refs
):
    shards = refs[:7]
    half_a, half_b = refs[7:9]
    windows = refs[9 : 9 + panels]
    q_ref, own_ref, held, codes, sems = refs[9 + panels :]
    step = pl.program_id(0)
    n_steps = rows // STEP
    zero_at = panels * classes * 4 * BS
    span = 4 * BS

    @pl.when(step == 0)
    def _():
        copies = []
        for p in range(panels):
            for m in range(classes):
                slot = p * classes + m
                copies.append(
                    pltpu.make_async_copy(
                        windows[p].at[m, pl.ds(0, span)],
                        held.at[pl.ds(slot * span, span)],
                        sems.at[slot],
                    )
                )
                copies[-1].start()
        held[pl.ds(zero_at, BS), :] = jnp.zeros((BS, BS), held.dtype)
        for copy in copies:
            copy.wait()

    x = x_ref[0]
    slots = [lax.rem(x + d, classes) for d in range(classes)]
    first_half = step < n_steps // 2
    for r in range(STEP):
        at = slice(r * BS, (r + 1) * BS)
        row = step * STEP + r
        left = [shard[0, at, :] for shard in shards]
        left.append(jnp.where(first_half, half_a[at, :], half_b[at, :]))
        left = jnp.concatenate(left, axis=1)
        right = []
        for d in range(classes):
            picked = []
            for s in range(8):
                k = idx_ref[(row * 8 + s) * classes + slots[d]]
                picked.append(held[pl.ds(pl.multiple_of(k * BS, BS), BS), :])
            right.append(jnp.concatenate(picked, axis=0))
        right = jnp.concatenate(right, axis=1)
        sums = jnp.dot(left, right, preferred_element_type=jnp.float32)
        own_ref[at, :] = sums[:, :BS]
        for d in range(1, classes):
            part = sums[:, d * BS : (d + 1) * BS]
            top = jnp.max(jnp.max(jnp.abs(part), axis=0, keepdims=True), axis=1, keepdims=True)
            code = jnp.ceil(jnp.log2(jnp.maximum(top, TINY)) * 16.0)
            scaled = part * (jnp.exp2(code * (-1.0 / 16.0)) * QMAX)
            coded = jnp.round(jnp.clip(scaled, -32767.0, 32767.0)).astype(jnp.int32)
            q_ref[slots[d], pl.ds(pl.multiple_of(row * BS, BS), BS), :] = coded.astype(jnp.int16)
            codes[d, pl.ds(row, 1), :] = jnp.broadcast_to(code.astype(jnp.int32), (1, BS))

    @pl.when(step == n_steps - 1)
    def _():
        for d in range(1, classes):
            q_ref[slots[d], pl.ds(rows * BS, TAIL), :] = codes[d].astype(jnp.int16)


def products(idx, x, shards, halves, windows, rows, classes):
    panels = len(windows)
    n_steps = rows // STEP
    half = n_steps // 2
    block = STEP * BS
    total_rows = rows * BS + TAIL
    shard_spec = pl.BlockSpec((1, block, BS), lambda g, i, x: (g // half, g % half, 0))
    grid_spec = pltpu.PrefetchScalarGridSpec(
        num_scalar_prefetch=2,
        grid=(n_steps,),
        in_specs=[shard_spec] * 7
        + [
            pl.BlockSpec((block, BS), lambda g, i, x: (jnp.minimum(g, half - 1), 0)),
            pl.BlockSpec((block, BS), lambda g, i, x: (jnp.maximum(g - half, 0), 0)),
        ]
        + [pl.BlockSpec(memory_space=pl.ANY)] * panels,
        out_specs=[
            pl.BlockSpec((classes, total_rows, BS), lambda g, i, x: (0, 0, 0)),
            pl.BlockSpec((block, BS), lambda g, i, x: (g, 0)),
        ],
        scratch_shapes=[
            pltpu.VMEM(((panels * classes * 4 + 1) * BS, BS), jnp.bfloat16),
            pltpu.VMEM((classes, TAIL, BS), jnp.int32),
            pltpu.SemaphoreType.DMA((panels * classes,)),
        ],
    )
    return pl.pallas_call(
        functools.partial(product_kernel, rows, panels, classes),
        grid_spec=grid_spec,
        out_shape=[
            jax.ShapeDtypeStruct((classes, total_rows, BS), jnp.int16),
            jax.ShapeDtypeStruct((rows * BS, BS), jnp.float32),
        ],
        compiler_params=pltpu.CompilerParams(vmem_limit_bytes=40 * 2**20),
        cost_estimate=pl.CostEstimate(
            flops=2 * rows * 32 * BS**3, bytes_accessed=12 * 2**20, transcendentals=0
        ),
    )(idx, x, *shards, *halves, *windows)


def sum_kernel(block_rows, x_ref, own_ref, *refs):
    out_ref = refs[-1]
    parts, codes = refs[0:3], refs[3:6]
    step = pl.program_id(0)
    scales = [jnp.exp2(c[0].astype(jnp.int32).astype(jnp.float32) * (1.0 / 16.0)) * (1.0 / QMAX) for c in codes]
    n_steps = TAIL // block_rows
    for r in range(block_rows):
        at = slice(r * BS, (r + 1) * BS)
        total = own_ref[at, :]
        for part, scale in zip(parts, scales):
            line = scale[r : r + 1, :]
            for other in range(1, n_steps):
                row = other * block_rows + r
                line = jnp.where(step == other, scale[row : row + 1, :], line)
            total = total + part[0, at, :].astype(jnp.int32).astype(jnp.float32) * line
        out_ref[at, :] = total.astype(jnp.bfloat16)


def summed(x, own, received, rows, classes):
    block_rows = 4
    block = block_rows * BS

    def part_spec(d):
        return pl.BlockSpec((1, block, BS), lambda g, x: (lax.rem(x[0] + d, classes), g, 0))

    def code_spec(d):
        return pl.BlockSpec((1, TAIL, BS), lambda g, x: (lax.rem(x[0] + d, classes), rows * BS // TAIL, 0))

    grid_spec = pltpu.PrefetchScalarGridSpec(
        num_scalar_prefetch=1,
        grid=(rows // block_rows,),
        in_specs=[pl.BlockSpec((block, BS), lambda g, x: (g, 0))]
        + [part_spec(d) for d in (1, 2, 3)]
        + [code_spec(d) for d in (1, 2, 3)],
        out_specs=pl.BlockSpec((block, BS), lambda g, x: (g, 0)),
    )
    return pl.pallas_call(
        functools.partial(sum_kernel, block_rows),
        grid_spec=grid_spec,
        out_shape=jax.ShapeDtypeStruct((rows * BS, BS), jnp.bfloat16),
        compiler_params=pltpu.CompilerParams(vmem_limit_bytes=24 * 2**20),
    )(x, own, *[received] * 6)


def shards(p_blocks, p_cols):
    rows = p_blocks.shape[0]
    classes = lax.axis_size("depth")
    matrix_rows = rows * lax.axis_size("row")
    x = lax.axis_index("depth")
    anchor = lax.axis_index("row") * rows - 2 * rows
    blocks = p_blocks[:, 0]
    cols = p_cols[:, 0]
    tail = jnp.zeros((TAIL, BS), jnp.bfloat16).at[0, :rows].set(cols.astype(jnp.bfloat16))

    own = jnp.concatenate(
        [blocks.reshape(2, rows // 2 * BS, BS), jnp.broadcast_to(tail, (2, TAIL, BS))], axis=1
    )
    down = up = own
    left = [own]
    for _ in range(3):
        down = passed_along(down, "col", 1)
        up = passed_along(up, "col", -1)
        left += [down, up]
    halves = [passed_along(down[0], "col", 1), passed_along(up[1], "col", -1)]

    pieces = blocks.reshape(rows // classes, classes, BS, BS).swapaxes(0, 1)
    pieces = jnp.concatenate(
        [pieces.reshape(classes, rows // classes * BS, BS), jnp.broadcast_to(tail, (classes, TAIL, BS))], axis=1
    )
    middle = lax.all_to_all(pieces, "depth", 0, 0)
    windows = [passed_along(middle, "row", 2), passed_along(middle, "row", 1), middle]
    windows += [passed_along(middle, "row", -1), passed_along(middle, "row", -2)]

    left_cols = jnp.stack([s[0, -TAIL, :rows] for s in left] + [halves[0][-TAIL, :rows]], axis=1).astype(jnp.int32)
    window_cols = jnp.stack([w[:, -TAIL, :rows] for w in windows]).astype(jnp.int32)
    own_cols = window_cols[2].T
    place = jnp.mod(left_cols - anchor, matrix_rows) // classes
    n_places = 5 * rows // classes
    by_place = window_cols.reshape(5, classes, rows // classes, classes)
    by_place = jnp.sum(jnp.where(jnp.arange(classes) == x, by_place, 0), axis=-1)
    by_place = by_place.swapaxes(1, 2).reshape(n_places, classes)
    found = (place[:, :, None, None] == jnp.arange(n_places)[:, None]) & (
        by_place[None, None] == own_cols[:, None, None, :]
    )
    per_panel = rows // classes
    where = (place // per_panel)[:, :, None] * (classes * per_panel) + jnp.arange(classes) * per_panel
    where = where + (place % per_panel)[:, :, None]
    idx = jnp.where(jnp.any(found, axis=2), where, n_places * classes).astype(jnp.int32).reshape(-1)

    x_operand = jnp.reshape(x, (1,)).astype(jnp.int32)
    coded, mine = products(idx, x_operand, left, halves, windows, rows, classes)
    received = lax.all_to_all(coded, "depth", 0, 0)
    total = summed(x_operand, mine, received, rows, classes)
    return total.reshape(rows, 1, BS, BS)


def solution(mesh):
    return jax.shard_map(
        shards,
        mesh=mesh,
        in_specs=(P("row", ("col", "depth"), None, None), P("row", ("col", "depth"))),
        out_specs=P("row", ("col", "depth"), None, None),
        check_vma=False,
    )
```

time: 182 us -> 132 us (0.73)
  waiting for transfers between devices: 78.2 us -> 26.9 us
  starting transfers between devices: 23.1 us -> 48.7 us
  matrix products: 13.7 us -> 0 us
  between operations: 13.5 us -> 0.28 us
  Pallas kernels: 0 us -> 12.9 us
  local copies, waits for them, and re-layouts: 21.2 us -> 10.7 us
  blocking collectives: 32.1 us -> 27.2 us
  other arithmetic: 0.1 us -> 4.06 us
    all_gather x1 -> x0, waiting for transfers between devices: 76.2 us -> none  [shards(): lax.all_gather(p_blocks, ('col', 'depth'), axis=1, tiled=True)]
    all_gather x1 -> x0, blocking collectives: 32.1 us -> none  [shards(): piece_cols = lax.all_gather(p_cols, ('col', 'depth'), axis=1, tiled=True)]
    all_to_all x0 -> x1, blocking collectives: none -> 27.2 us  [shards(): received = lax.all_to_all(coded, 'depth', 0, 0)]
    ppermute x8 -> x12, waiting for transfers between devices: 1.33 us -> 26.9 us  [passed_along(): lax.ppermute(block, axis, [(i, (i + distance) % n) for i in range(n)])]
    ppermute x8 -> x12, starting transfers between devices: 23.1 us -> 43.9 us  [passed_along(): lax.ppermute(block, axis, [(i, (i + distance) % n) for i in range(n)])]
    gather x3 -> x0, local copies, waits for them, and re-layouts: 16.8 us -> none  [the longest x1 13.4 us: shards(): partner_blocks = window_blocks[position]]
    dot_general x1 -> x0, matrix products: 13.7 us -> none  [shards(): jnp.einsum('itab,itbc->iac', masked_blocks, partner_blocks, preferred_ele...]
    pallas_call x0 -> x2, Pallas kernels: none -> 12.9 us  [the longest x1 11.2 us: products(): pl.pallas_call(functools.partial(product_kernel, rows, panels, classes),...]
  transfers between devices with their start and end apart: 9 -> 13, of which waited for: 2 -> 3; matrix products, arithmetic and copies ran while one was open for 12% -> 7% of each run, Pallas kernels for 0% -> 0%
where the time goes in v1:
time: 132 us; the launch traced here: 131 us
  starting transfers between devices  48.7 us (37%)
  blocking collectives  27.2 us (21%)
  waiting for transfers between devices  26.9 us (20%)
  Pallas kernels  12.9 us (10%)
  local copies, waits for them, and re-layouts  10.7 us (8%)
  other arithmetic  4.06 us (3%)
    ppermute x12, starting transfers between devices, passed_along(): lax.ppermute(block, axis, [(i, (i + distance) % n) for i in range(n)])  43.9 us
    all_to_all x1, blocking collectives, shards(): received = lax.all_to_all(coded, 'depth', 0, 0)  27.2 us
    ppermute x12, waiting for transfers between devices, passed_along(): lax.ppermute(block, axis, [(i, (i + distance) % n) for i in range(n)])  26.9 us
    pallas_call x1, Pallas kernels, products(): pl.pallas_call(functools.partial(product_kernel, rows, panels, classes),...  11.2 us
    all_to_all x1, starting transfers between devices, shards(): middle = lax.all_to_all(pieces, 'depth', 0, 0)  4.84 us
    unnamed x14, local copies, waits for them, and re-layouts  3.54 us
    another operation x8, local copies, waits for them, and re-layouts, shards(): jnp.stack([s[0, -TAIL, :rows] for s in left] + [halves[0][-TAIL, :rows]],...  2.7 us
  transfers between devices with their start and end apart: 13, of which 3 were waited for; matrix products, arithmetic and copies ran while one was open for 7% of the time, Pallas kernels for 0%

profile of v1, /device:TPU:1, one launch (start us, length us, event | category | flops | bytes accessed | tf_op | source)
XLA Modules:
  0.0 130.7 jit_solution(17743914846815774899)
XLA Ops:
  0.7 1.1 copy.26
  1.8 0.8 pad_maximum_fusion
  2.6 4.8 %all-to-all-start = ((bf16[4,528,128]{2,1,0:T(8,128)(2,1)}), bf16[4,528,128]{2,1,0:T(8,128)(2,1)S(1)}, u32[]{:S(2)}, u32[]{:S(2)}) async-start(bf16[4,528,128]{2,1,0:T(8,128)(2,1)} %pad_maximum_fusion), calls=%async_computation | async-start | bytes 1081344 | tf_op jit(solution)/shard_map/all_to_all | solution.py:195
  7.5 5.1 %collective-permute-start.1 = (bf16[2,1040,128]{2,1,0:T(8,128)(2,1)S(1)}, bf16[2,1040,128]{2,1,0:T(8,128)(2,1)}, u32[]{:S(2)}, u32[]{:S(2)}) collective-permute-start(bf16[2,1040,128]{2,1,0:T(8,128)(2,1)S(1)} %pad_maximum_fusion.1.refs_0_), channel_id=1, source_target_pairs={{0,28},{4,0},{8,4},{12,8},{16,12},{20,16},{24,20},{28,24},{1,29},{... | collective-permute-start | bytes 1597448 | tf_op jit(solution)/shard_map/ppermute | solution.py:19
  12.6 1.9 %collective-permute-start = (bf16[2,1040,128]{2,1,0:T(8,128)(2,1)S(1)}, bf16[2,1040,128]{2,1,0:T(8,128)(2,1)}, u32[]{:S(2)}, u32[]{:S(2)}) collective-permute-start(bf16[2,1040,128]{2,1,0:T(8,128)(2,1)S(1)} %pad_maximum_fusion.1.refs_0_), channel_id=1, source_target_pairs={{0,4},{4,8},{8,12},{12,16},{16,20},{20,24},{24,28},{28,0},{1,5},{5... | collective-permute-start | bytes 1597448 | tf_op jit(solution)/shard_map/ppermute | solution.py:19
  14.6 12.0 %collective-permute-start.10 = (bf16[4,528,128]{2,1,0:T(8,128)(2,1)S(1)}, bf16[4,528,128]{2,1,0:T(8,128)(2,1)S(1)}, u32[]{:S(2)}, u32[]{:S(2)}) collective-permute-start(bf16[4,528,128]{2,1,0:T(8,128)(2,1)S(1)} %all-to-all-done.refs_11_), channel_id=1, source_target_pairs={{0,448},{32,480},{64,0},{96,32},{128,64},{160,96},{192,128},{224,1... | collective-permute-start | bytes 1622024 | tf_op jit(solution)/shard_map/ppermute | solution.py:19
  26.8 2.4 %collective-permute-start.9 = (bf16[4,528,128]{2,1,0:T(8,128)(2,1)S(1)}, bf16[4,528,128]{2,1,0:T(8,128)(2,1)S(1)}, u32[]{:S(2)}, u32[]{:S(2)}) collective-permute-start(bf16[4,528,128]{2,1,0:T(8,128)(2,1)S(1)} %all-to-all-done.refs_11_), channel_id=1, source_target_pairs={{0,480},{32,0},{64,32},{96,64},{128,96},{160,128},{192,160},{224,1... | collective-permute-start | bytes 1622024 | tf_op jit(solution)/shard_map/ppermute | solution.py:19
  29.2 1.9 %collective-permute-start.7 = (bf16[4,528,128]{2,1,0:T(8,128)(2,1)S(1)}, bf16[4,528,128]{2,1,0:T(8,128)(2,1)}, u32[]{:S(2)}, u32[]{:S(2)}) collective-permute-start(bf16[4,528,128]{2,1,0:T(8,128)(2,1)S(1)} %all-to-all-done.refs_11_), channel_id=1, source_target_pairs={{0,64},{32,96},{64,128},{96,160},{128,192},{160,224},{192,256},{22... | collective-permute-start | bytes 1622024 | tf_op jit(solution)/shard_map/ppermute | solution.py:19
  31.1 0.7 slice_bitcast_fusion.7
  31.8 5.1 %collective-permute-start.3 = (bf16[2,1040,128]{2,1,0:T(8,128)(2,1)}, bf16[2,1040,128]{2,1,0:T(8,128)(2,1)}, u32[]{:S(2)}, u32[]{:S(2)}) collective-permute-start(bf16[2,1040,128]{2,1,0:T(8,128)(2,1)} %collective-permute-done.1.refs_2_), channel_id=1, source_target_pairs={{0,28},{4,0},{8,4},{12,8},{16,12},{20,16},{24,20},{28,24},{1,29},{... | collective-permute-start | bytes 1597448 | tf_op jit(solution)/shard_map/ppermute | solution.py:19
  36.9 0.7 slice_bitcast_fusion.8
  37.6 1.9 %collective-permute-start.2 = (bf16[2,1040,128]{2,1,0:T(8,128)(2,1)}, bf16[2,1040,128]{2,1,0:T(8,128)(2,1)}, u32[]{:S(2)}, u32[]{:S(2)}) collective-permute-start(bf16[2,1040,128]{2,1,0:T(8,128)(2,1)} %collective-permute-done.refs_1_), channel_id=1, source_target_pairs={{0,4},{4,8},{8,12},{12,16},{16,20},{20,24},{24,28},{28,0},{1,5},{5... | collective-permute-start | bytes 1597448 | tf_op jit(solution)/shard_map/ppermute | solution.py:19
  39.7 0.8 copy-done
  40.6 9.9 %collective-permute-done.7.refs_9_ = bf16[4,528,128]{2,1,0:T(8,128)(2,1)} collective-permute-done((bf16[4,528,128]{2,1,0:T(8,128)(2,1)S(1)}, bf16[4,528,128]{2,1,0:T(8,128)(2,1)}, u32[]{:S(2)}, u32[]{:S(2)}) %collective-permute-start.7) | collective-permute-done | bytes 540704 | tf_op jit(solution)/shard_map/ppermute | solution.py:19
  50.5 0.7 slice_reduce_fusion.3
  51.9 4.8 %collective-permute-start.5 = (bf16[2,1040,128]{2,1,0:T(8,128)(2,1)}, bf16[2,1040,128]{2,1,0:T(8,128)(2,1)S(1)}, u32[]{:S(2)}, u32[]{:S(2)}) collective-permute-start(bf16[2,1040,128]{2,1,0:T(8,128)(2,1)} %collective-permute-done.3.refs_4_), channel_id=1, source_target_pairs={{0,28},{4,0},{8,4},{12,8},{16,12},{20,16},{24,20},{28,24},{1,29},{... | collective-permute-start | bytes 1597448 | tf_op jit(solution)/shard_map/ppermute | solution.py:19
  56.8 1.9 %collective-permute-start.4 = (bf16[2,1040,128]{2,1,0:T(8,128)(2,1)}, bf16[2,1040,128]{2,1,0:T(8,128)(2,1)S(1)}, u32[]{:S(2)}, u32[]{:S(2)}) collective-permute-start(bf16[2,1040,128]{2,1,0:T(8,128)(2,1)} %collective-permute-done.2.refs_3_), channel_id=1, source_target_pairs={{0,4},{4,8},{8,12},{12,16},{16,20},{20,24},{24,28},{28,0},{1,5},{5... | collective-permute-start | bytes 1597448 | tf_op jit(solution)/shard_map/ppermute | solution.py:19
  58.7 0.7 slice_bitcast_fusion.5
  60.0 8.6 %collective-permute-done.5.refs_6_ = bf16[2,1040,128]{2,1,0:T(8,128)(2,1)S(1)} collective-permute-done((bf16[2,1040,128]{2,1,0:T(8,128)(2,1)}, bf16[2,1040,128]{2,1,0:T(8,128)(2,1)S(1)}, u32[]{:S(2)}, u32[]{:S(2)}) %collective-permute-start.5) | collective-permute-done | bytes 532512 | tf_op jit(solution)/shard_map/ppermute | solution.py:19
  68.6 0.7 slice_bitcast_fusion
  69.3 4.9 %collective-permute-start.11 = (bf16[1040,128]{1,0:T(8,128)(2,1)}, bf16[1040,128]{1,0:T(8,128)(2,1)S(1)}, u32[]{:S(2)}, u32[]{:S(2)}) collective-permute-start(bf16[1040,128]{1,0:T(8,128)(2,1)} %slice_bitcast_fusion), channel_id=1, source_target_pairs={{0,28},{4,0},{8,4},{12,8},{16,12},{20,16},{24,20},{28,24},{1,29},{... | collective-permute-start | bytes 798728 | tf_op jit(solution)/shard_map/ppermute | solution.py:19
  74.3 1.9 %collective-permute-start.6 = (bf16[1040,128]{1,0:T(8,128)(2,1)S(1)}, bf16[1040,128]{1,0:T(8,128)(2,1)S(1)}, u32[]{:S(2)}, u32[]{:S(2)}) collective-permute-start(bf16[1040,128]{1,0:T(8,128)(2,1)S(1)} %slice_bitcast_fusion.1), channel_id=1, source_target_pairs={{0,4},{4,8},{8,12},{12,16},{16,20},{20,24},{24,28},{28,0},{1,5},{5... | collective-permute-start | bytes 798728 | tf_op jit(solution)/shard_map/ppermute | solution.py:19
  76.3 8.4 %collective-permute-done.6.refs_7_ = bf16[1040,128]{1,0:T(8,128)(2,1)S(1)} collective-permute-done((bf16[1040,128]{1,0:T(8,128)(2,1)S(1)}, bf16[1040,128]{1,0:T(8,128)(2,1)S(1)}, u32[]{:S(2)}, u32[]{:S(2)}) %collective-permute-start.6) | collective-permute-done | bytes 266272 | tf_op jit(solution)/shard_map/ppermute | solution.py:19
  84.7 0.7 copy-done.2
  85.6 1.2 and_reduce_fusion
  87.0 0.7 add_select_fusion
  87.6 0.9 copy.31
  88.7 1.0 copy-done.1
  89.7 0.9 copy-done.3
  90.7 11.2 %shard_map.28 = (s16[4,2064,128]{2,1,0:T(8,128)(2,1)S(1)}, f32[2048,128]{1,0:T(8,128)S(1)}) custom-call(s32[512]{0:T(512)S(1)} %select_n.67.idx_ref, s32[1]{0:T(128)} %bitcast.x_ref, bf16[2,1040,128]{2,1,0:T(8,128)(2,1)S(1)} %pad_maximum_fusion.1.refs_0_, bf16[2,1040,128]{2,1,0:T(8,128)(2,1)} %collective-permute-done.refs_1_, ...), custom_call_target="tpu_custom_call" | custom-call | flops 2147483648 | bytes 12582912 | tf_op jit(solution)/shard_map/pallas_call | solution.py:112
  101.8 27.2 %all_to_all.10.refs_0_.refs_1_.refs_2_.refs_3_.refs_4_.refs_5_ = s16[4,2064,128]{2,1,0:T(8,128)(2,1)S(1)} all-to-all(s16[4,2064,128]{2,1,0:T(8,128)(2,1)S(1)} %get-tuple-element.20), channel_id=1, replica_groups=mesh['row'=16,'col'=8,'depth'=4] {'depth'}, dimensions={0} | all-to-all | bytes 4227072 | tf_op jit(solution)/shard_map/all_to_all | solution.py:217
  129.0 1.7 %shard_map.29 = bf16[2048,128]{1,0:T(8,128)(2,1)} custom-call(s32[1]{0:T(128)} %bitcast.x_ref, f32[2048,128]{1,0:T(8,128)S(1)} %get-tuple-element.19.own_ref, s16[4,2064,128]{2,1,0:T(8,128)(2,1)S(1)} %all_to_all.10.refs_0_.refs_1_.refs_2_.refs_3_.refs_4_.refs_5_, s16[4,2064,128]{2,1,0:T(8,128)(2,1)S(1)} %all_to_all.10.refs_0_.refs_1_.refs_2_.refs_3_.refs_4_.refs_5_, ...), custom_call_target="tpu_custom_call" | custom-call | tf_op jit(solution)/shard_map/pallas_call | solution.py:162
  (56 shorter events, 3.2 us)
Async XLA Ops:
  1.8 5.7 %copy-start.4 = (bf16[16,1,128,128]{3,2,1,0:T(8,128)(2,1)S(1)}, bf16[16,1,128,128]{3,2,1,0:T(8,128)(2,1)}, u32[]{:S(2)}) copy-start(bf16[16,1,128,128]{3,2,1,0:T(8,128)(2,1)} %param.4) | copy-start | bytes 1572868
  2.6 12.0 %all-to-all-start = ((bf16[4,528,128]{2,1,0:T(8,128)(2,1)}), bf16[4,528,128]{2,1,0:T(8,128)(2,1)S(1)}, u32[]{:S(2)}, u32[]{:S(2)}) async-start(bf16[4,528,128]{2,1,0:T(8,128)(2,1)} %pad_maximum_fusion), calls=%async_computation | async-start | bytes 1081344 | tf_op jit(solution)/shard_map/all_to_all | solution.py:195
  7.5 21.7 %collective-permute-start.1 = (bf16[2,1040,128]{2,1,0:T(8,128)(2,1)S(1)}, bf16[2,1040,128]{2,1,0:T(8,128)(2,1)}, u32[]{:S(2)}, u32[]{:S(2)}) collective-permute-start(bf16[2,1040,128]{2,1,0:T(8,128)(2,1)S(1)} %pad_maximum_fusion.1.refs_0_), channel_id=1, source_target_pairs={{0,28},{4,0},{8,4},{12,8},{16,12},{20,16},{24,20},{28,24},{1,29},{... | collective-permute-start | bytes 1597448 | tf_op jit(solution)/shard_map/ppermute | solution.py:19
  12.6 19.2 %collective-permute-start = (bf16[2,1040,128]{2,1,0:T(8,128)(2,1)S(1)}, bf16[2,1040,128]{2,1,0:T(8,128)(2,1)}, u32[]{:S(2)}, u32[]{:S(2)}) collective-permute-start(bf16[2,1040,128]{2,1,0:T(8,128)(2,1)S(1)} %pad_maximum_fusion.1.refs_0_), channel_id=1, source_target_pairs={{0,4},{4,8},{8,12},{12,16},{16,20},{20,24},{24,28},{28,0},{1,5},{5... | collective-permute-start | bytes 1597448 | tf_op jit(solution)/shard_map/ppermute | solution.py:19
  14.6 23.0 %collective-permute-start.10 = (bf16[4,528,128]{2,1,0:T(8,128)(2,1)S(1)}, bf16[4,528,128]{2,1,0:T(8,128)(2,1)S(1)}, u32[]{:S(2)}, u32[]{:S(2)}) collective-permute-start(bf16[4,528,128]{2,1,0:T(8,128)(2,1)S(1)} %all-to-all-done.refs_11_), channel_id=1, source_target_pairs={{0,448},{32,480},{64,0},{96,32},{128,64},{160,96},{192,128},{224,1... | collective-permute-start | bytes 1622024 | tf_op jit(solution)/shard_map/ppermute | solution.py:19
  26.8 12.8 %collective-permute-start.9 = (bf16[4,528,128]{2,1,0:T(8,128)(2,1)S(1)}, bf16[4,528,128]{2,1,0:T(8,128)(2,1)S(1)}, u32[]{:S(2)}, u32[]{:S(2)}) collective-permute-start(bf16[4,528,128]{2,1,0:T(8,128)(2,1)S(1)} %all-to-all-done.refs_11_), channel_id=1, source_target_pairs={{0,480},{32,0},{64,32},{96,64},{128,96},{160,128},{192,160},{224,1... | collective-permute-start | bytes 1622024 | tf_op jit(solution)/shard_map/ppermute | solution.py:19
  29.2 10.5 %collective-permute-start.8 = (bf16[4,528,128]{2,1,0:T(8,128)(2,1)S(1)}, bf16[4,528,128]{2,1,0:T(8,128)(2,1)S(1)}, u32[]{:S(2)}, u32[]{:S(2)}) collective-permute-start(bf16[4,528,128]{2,1,0:T(8,128)(2,1)S(1)} %all-to-all-done.refs_11_), channel_id=1, source_target_pairs={{0,32},{32,64},{64,96},{96,128},{128,160},{160,192},{192,224},{224... | collective-permute-start | bytes 1622024 | tf_op jit(solution)/shard_map/ppermute | solution.py:19
  29.2 21.3 %collective-permute-start.7 = (bf16[4,528,128]{2,1,0:T(8,128)(2,1)S(1)}, bf16[4,528,128]{2,1,0:T(8,128)(2,1)}, u32[]{:S(2)}, u32[]{:S(2)}) collective-permute-start(bf16[4,528,128]{2,1,0:T(8,128)(2,1)S(1)} %all-to-all-done.refs_11_), channel_id=1, source_target_pairs={{0,64},{32,96},{64,128},{96,160},{128,192},{160,224},{192,256},{22... | collective-permute-start | bytes 1622024 | tf_op jit(solution)/shard_map/ppermute | solution.py:19
  31.8 20.1 %collective-permute-start.3 = (bf16[2,1040,128]{2,1,0:T(8,128)(2,1)}, bf16[2,1040,128]{2,1,0:T(8,128)(2,1)}, u32[]{:S(2)}, u32[]{:S(2)}) collective-permute-start(bf16[2,1040,128]{2,1,0:T(8,128)(2,1)} %collective-permute-done.1.refs_2_), channel_id=1, source_target_pairs={{0,28},{4,0},{8,4},{12,8},{16,12},{20,16},{24,20},{28,24},{1,29},{... | collective-permute-start | bytes 1597448 | tf_op jit(solution)/shard_map/ppermute | solution.py:19
  37.6 19.2 %collective-permute-start.2 = (bf16[2,1040,128]{2,1,0:T(8,128)(2,1)}, bf16[2,1040,128]{2,1,0:T(8,128)(2,1)}, u32[]{:S(2)}, u32[]{:S(2)}) collective-permute-start(bf16[2,1040,128]{2,1,0:T(8,128)(2,1)} %collective-permute-done.refs_1_), channel_id=1, source_target_pairs={{0,4},{4,8},{8,12},{12,16},{16,20},{20,24},{24,28},{28,0},{1,5},{5... | collective-permute-start | bytes 1597448 | tf_op jit(solution)/shard_map/ppermute | solution.py:19
  39.7 0.8 copy-start
  51.9 16.7 %collective-permute-start.5 = (bf16[2,1040,128]{2,1,0:T(8,128)(2,1)}, bf16[2,1040,128]{2,1,0:T(8,128)(2,1)S(1)}, u32[]{:S(2)}, u32[]{:S(2)}) collective-permute-start(bf16[2,1040,128]{2,1,0:T(8,128)(2,1)} %collective-permute-done.3.refs_4_), channel_id=1, source_target_pairs={{0,28},{4,0},{8,4},{12,8},{16,12},{20,16},{24,20},{28,24},{1,29},{... | collective-permute-start | bytes 1597448 | tf_op jit(solution)/shard_map/ppermute | solution.py:19
  56.8 17.5 %collective-permute-start.4 = (bf16[2,1040,128]{2,1,0:T(8,128)(2,1)}, bf16[2,1040,128]{2,1,0:T(8,128)(2,1)S(1)}, u32[]{:S(2)}, u32[]{:S(2)}) collective-permute-start(bf16[2,1040,128]{2,1,0:T(8,128)(2,1)} %collective-permute-done.2.refs_3_), channel_id=1, source_target_pairs={{0,4},{4,8},{8,12},{12,16},{16,20},{20,24},{24,28},{28,0},{1,5},{5... | collective-permute-start | bytes 1597448 | tf_op jit(solution)/shard_map/ppermute | solution.py:19
  69.3 19.3 %collective-permute-start.11 = (bf16[1040,128]{1,0:T(8,128)(2,1)}, bf16[1040,128]{1,0:T(8,128)(2,1)S(1)}, u32[]{:S(2)}, u32[]{:S(2)}) collective-permute-start(bf16[1040,128]{1,0:T(8,128)(2,1)} %slice_bitcast_fusion), channel_id=1, source_target_pairs={{0,28},{4,0},{8,4},{12,8},{16,12},{20,16},{24,20},{28,24},{1,29},{... | collective-permute-start | bytes 798728 | tf_op jit(solution)/shard_map/ppermute | solution.py:19
  74.3 10.4 %collective-permute-start.6 = (bf16[1040,128]{1,0:T(8,128)(2,1)S(1)}, bf16[1040,128]{1,0:T(8,128)(2,1)S(1)}, u32[]{:S(2)}, u32[]{:S(2)}) collective-permute-start(bf16[1040,128]{1,0:T(8,128)(2,1)S(1)} %slice_bitcast_fusion.1), channel_id=1, source_target_pairs={{0,4},{4,8},{8,12},{12,16},{16,20},{20,24},{24,28},{28,0},{1,5},{5... | collective-permute-start | bytes 798728 | tf_op jit(solution)/shard_map/ppermute | solution.py:19
  84.7 0.7 copy-start.2
  88.7 1.0 copy-start.1
  89.7 1.0 copy-start.3

commit v2 on v1

v2 whole, which is shorter than its diff:
```python
import functools

import jax
import jax.numpy as jnp
from jax import lax
from jax.experimental import pallas as pl
from jax.experimental.pallas import tpu as pltpu
from jax.sharding import PartitionSpec as P

BS = 128
TAIL = 16
STEP = 4
PANELS = 5
SPAN = 4 * BS + TAIL
QMAX = 32700.0
TINY = 2.0**-111


def passed_along(block, axis, distance):
    n = lax.axis_size(axis)
    return lax.ppermute(block, axis, [(i, (i + distance) % n) for i in range(n)])


def offsets(left_tails, held, x, anchor, matrix_rows, classes, zero_at):
    sub = lax.broadcasted_iota(jnp.int32, (8, BS), 0)
    lane = lax.broadcasted_iota(jnp.int32, (8, BS), 1)

    def numbers(tile):
        return tile.astype(jnp.float32)[:8].astype(jnp.int32)

    cols = jnp.zeros((8, BS), jnp.int32)
    for s in range(8):
        cols = jnp.where(sub == s, numbers(left_tails[s]), cols)
    place = lax.shift_right_logical((cols - anchor + 2 * matrix_rows) & (matrix_rows - 1), 2)
    base = lax.shift_right_logical(place, 2) * (classes * SPAN) + (place & 3) * BS
    result = []
    for m in range(classes):
        tails = [numbers(held[pl.ds((p * classes + m) * SPAN + 4 * BS, TAIL), :]) for p in range(PANELS)]
        found = jnp.zeros((8, BS), jnp.int32)
        for p in range(PANELS):
            for a in range(4):
                column = jnp.sum(jnp.where(lane == 4 * a + x, tails[p], 0), axis=1, keepdims=True)
                hit = (place == 4 * p + a) & (tails[PANELS // 2] == column)
                found = jnp.where(hit, 1, found)
        result.append(jnp.where(found == 1, base + m * SPAN, zero_at))
    return result


def product_kernel(rows, classes, matrix_rows, here_ref, *refs):
    shards = refs[:7]
    half_a, half_b = refs[7:9]
    tail_sources = refs[9:17]
    pair, far, cross = refs[17:20]
    q_ref, own_ref, held, tails, wide, idx_ref, sems = refs[20:]
    step = pl.program_id(0)
    n_steps = rows // STEP
    panel = classes * SPAN
    zero_at = PANELS * panel
    x, core, anchor = here_ref[0], here_ref[1], here_ref[2]

    @pl.when(step == 0)
    def _():
        pieces = [
            (pair.at[pl.ds(0, panel)], 2 - core),
            (pair.at[pl.ds(panel, panel)], 3 - core),
            (far.at[pl.ds(0, panel)], 3 * core),
            (far.at[pl.ds(panel, panel)], 1 + 3 * core),
            (cross, 4 - 4 * core),
        ]
        copies = []
        for n, (source, p) in enumerate(pieces):
            at = pl.ds(pl.multiple_of(p * panel, TAIL), panel)
            copies.append(pltpu.make_async_copy(source, held.at[at], sems.at[n]))
        for s in range(8):
            if s < 7:
                source = tail_sources[s].at[0, pl.ds(rows // 2 * BS, TAIL)]
            else:
                source = tail_sources[s].at[pl.ds(rows // 2 * BS, TAIL)]
            copies.append(pltpu.make_async_copy(source, tails.at[s], sems.at[len(pieces) + s]))
        for copy in copies:
            copy.start()
        held[pl.ds(zero_at, BS), :] = jnp.zeros((BS, BS), held.dtype)
        for copy in copies:
            copy.wait()
        found = offsets([tails[s] for s in range(8)], held, x, anchor, matrix_rows, classes, zero_at)
        for m in range(classes):
            wide[pl.ds(m * 8, 8), :] = found[m]
        copy = pltpu.make_async_copy(wide, idx_ref, sems.at[len(copies)])
        copy.start()
        copy.wait()

    slots = [lax.rem(x + d, classes) for d in range(classes)]
    first_half = step < n_steps // 2
    codes = [[] for _ in range(classes)]
    for r in range(STEP):
        at = slice(r * BS, (r + 1) * BS)
        row = step * STEP + r
        left = [shard[0, at, :] for shard in shards]
        left.append(jnp.where(first_half, half_a[at, :], half_b[at, :]))
        left = jnp.concatenate(left, axis=1)
        right = []
        for d in range(classes):
            picked = []
            for s in range(8):
                k = idx_ref[slots[d] * 8 + s, row]
                picked.append(held[pl.ds(pl.multiple_of(k, TAIL), BS), :])
            right.append(jnp.concatenate(picked, axis=0))
        right = jnp.concatenate(right, axis=1)
        sums = jnp.dot(left, right, preferred_element_type=jnp.float32)
        own_ref[at, :] = sums[:, :BS]
        for d in range(1, classes):
            part = sums[:, d * BS : (d + 1) * BS]
            top = jnp.max(jnp.max(jnp.abs(part), axis=0, keepdims=True), axis=1, keepdims=True)
            code = jnp.ceil(jnp.log2(jnp.maximum(top, TINY)) * 16.0)
            scaled = part * (jnp.exp2(code * (-1.0 / 16.0)) * QMAX)
            coded = jnp.round(jnp.clip(scaled, -32767.0, 32767.0)).astype(jnp.int32)
            q_ref[slots[d], 0, at, :] = coded.astype(jnp.int16)
            codes[d].append(code)
    sub = lax.broadcasted_iota(jnp.int32, (TAIL, BS), 0)
    for d in range(1, classes):
        lines = jnp.zeros((TAIL, BS), jnp.float32)
        for r in range(STEP):
            lines = jnp.where(sub == r, codes[d][r], lines)
        q_ref[slots[d], 0, pl.ds(STEP * BS, TAIL), :] = lines.astype(jnp.int32).astype(jnp.int16)


def products(here, shards, halves, windows, rows, classes, matrix_rows):
    n_steps = rows // STEP
    half = n_steps // 2
    block = STEP * BS
    shard_spec = pl.BlockSpec((1, block, BS), lambda g, h: (g // half, g % half, 0))
    anywhere = pl.BlockSpec(memory_space=pl.ANY)
    grid_spec = pltpu.PrefetchScalarGridSpec(
        num_scalar_prefetch=1,
        grid=(n_steps,),
        in_specs=[shard_spec] * 7
        + [
            pl.BlockSpec((block, BS), lambda g, h: (jnp.minimum(g, half - 1), 0)),
            pl.BlockSpec((block, BS), lambda g, h: (jnp.maximum(g - half, 0), 0)),
        ]
        + [anywhere] * 11,
        out_specs=[
            pl.BlockSpec((classes, 1, block + TAIL, BS), lambda g, h: (0, g, 0, 0)),
            pl.BlockSpec((block, BS), lambda g, h: (g, 0)),
        ],
        scratch_shapes=[
            pltpu.VMEM((PANELS * classes * SPAN + BS, BS), jnp.bfloat16),
            pltpu.VMEM((8, TAIL, BS), jnp.bfloat16),
            pltpu.VMEM((classes * 8, BS), jnp.int32),
            pltpu.SMEM((classes * 8, BS), jnp.int32),
            pltpu.SemaphoreType.DMA((14,)),
        ],
    )
    return pl.pallas_call(
        functools.partial(product_kernel, rows, classes, matrix_rows),
        grid_spec=grid_spec,
        out_shape=[
            jax.ShapeDtypeStruct((classes, n_steps, block + TAIL, BS), jnp.int16),
            jax.ShapeDtypeStruct((rows * BS, BS), jnp.float32),
        ],
        compiler_params=pltpu.CompilerParams(vmem_limit_bytes=24 * 2**20),
        cost_estimate=pl.CostEstimate(
            flops=2 * rows * 32 * BS**3, bytes_accessed=12 * 2**20, transcendentals=0
        ),
    )(here, *shards, *halves, *shards, halves[0], *windows)


def sum_kernel(here_ref, own_ref, *refs):
    out_ref = refs[-1]
    scales = []
    for part in refs[:-1]:
        code = part[0, 0, pl.ds(STEP * BS, TAIL), :].astype(jnp.int32).astype(jnp.float32)
        scales.append(jnp.exp2(code * (1.0 / 16.0)) * (1.0 / QMAX))
    for r in range(STEP):
        at = slice(r * BS, (r + 1) * BS)
        total = own_ref[at, :]
        for part, scale in zip(refs[:-1], scales):
            total = total + part[0, 0, at, :].astype(jnp.int32).astype(jnp.float32) * scale[r : r + 1, :]
        out_ref[at, :] = total.astype(jnp.bfloat16)


def summed(here, own, received, rows, classes):
    block = STEP * BS

    def part_spec(d):
        return pl.BlockSpec((1, 1, block + TAIL, BS), lambda g, h: (lax.rem(h[0] + d, classes), g, 0, 0))

    grid_spec = pltpu.PrefetchScalarGridSpec(
        num_scalar_prefetch=1,
        grid=(rows // STEP,),
        in_specs=[pl.BlockSpec((block, BS), lambda g, h: (g, 0))] + [part_spec(d) for d in (1, 2, 3)],
        out_specs=pl.BlockSpec((block, BS), lambda g, h: (g, 0)),
    )
    return pl.pallas_call(
        sum_kernel,
        grid_spec=grid_spec,
        out_shape=jax.ShapeDtypeStruct((rows * BS, BS), jnp.bfloat16),
        compiler_params=pltpu.CompilerParams(vmem_limit_bytes=16 * 2**20),
    )(here, own, received, received, received)


def shards(p_blocks, p_cols):
    rows = p_blocks.shape[0]
    classes = lax.axis_size("depth")
    n_panels = lax.axis_size("row")
    matrix_rows = rows * n_panels
    r = lax.axis_index("row")
    core = lax.rem(r, 2)
    here = jnp.stack([lax.axis_index("depth"), core, (r - PANELS // 2) * rows]).astype(jnp.int32)
    blocks = p_blocks[:, 0]
    line = jnp.zeros((1, BS), jnp.bfloat16).at[0, :rows].set(p_cols[:, 0].astype(jnp.bfloat16))
    tail = jnp.broadcast_to(line, (TAIL, BS))

    own = jnp.concatenate(
        [blocks.reshape(2, rows // 2 * BS, BS), jnp.broadcast_to(tail, (2, TAIL, BS))], axis=1
    )
    down = up = own
    left = [own]
    for hop in range(3):
        down = passed_along(down, "col", 1)
        up = passed_along(up, "col", -1)
        left += [down, up]
        if hop == 0:
            after_first = (down, up)
    halves = [passed_along(down[0], "col", 1), passed_along(up[1], "col", -1)]

    pieces = blocks.reshape(rows // classes, classes, BS, BS).swapaxes(0, 1)
    pieces = jnp.concatenate(
        [pieces.reshape(classes, rows // classes * BS, BS), jnp.broadcast_to(tail, (classes, TAIL, BS))], axis=1
    )
    pieces = jnp.concatenate([pieces, pieces], axis=0)
    groups = [[(2 * z + c) * classes + x for c in range(2) for x in range(classes)] for z in range(n_panels // 2)]
    pair = lax.all_to_all(pieces, ("row", "depth"), 0, 0, axis_index_groups=groups)
    pair = pair.reshape(2 * classes * SPAN, BS)
    pair, *_ = lax.optimization_barrier((pair,) + after_first)
    far = lax.ppermute(pair, "row", [(i, (i + (2 if i % 2 == 0 else -2)) % n_panels) for i in range(n_panels)])
    panel = classes * SPAN
    cross = jnp.where(core == 0, pair[:panel], pair[panel:])
    cross = lax.ppermute(cross, "row", [(i, (i + (-2 if i % 2 == 0 else 2)) % n_panels) for i in range(n_panels)])

    coded, mine = products(here, left, halves, (pair, far, cross), rows, classes, matrix_rows)
    received = lax.all_to_all(coded, "depth", 0, 0)
    return summed(here, mine, received, rows, classes).reshape(rows, 1, BS, BS)


def solution(mesh):
    return jax.shard_map(
        shards,
        mesh=mesh,
        in_specs=(P("row", ("col", "depth"), None, None), P("row", ("col", "depth"))),
        out_specs=P("row", ("col", "depth"), None, None),
        check_vma=False,
    )
```

time: 132 us -> 114 us (0.86)
  waiting for transfers between devices: 26.9 us -> 19.1 us
  local copies, waits for them, and re-layouts: 10.7 us -> 3.34 us
  starting transfers between devices: 48.7 us -> 44.9 us
  Pallas kernels: 12.9 us -> 11.1 us
    ppermute x12 -> x8, waiting for transfers between devices: 26.9 us -> 9.49 us  [passed_along(): lax.ppermute(block, axis, [(i, (i + distance) % n) for i in range(n)])]
    ppermute x12 -> x8, starting transfers between devices: 43.9 us -> 27.5 us  [passed_along(): lax.ppermute(block, axis, [(i, (i + distance) % n) for i in range(n)])]
    all_to_all x1, waiting for transfers between devices: 0.01 us -> 9.64 us  [shards(): lax.all_to_all(pieces, ('row', 'depth'), 0, 0, axis_index_groups=groups)]
    ppermute x0 -> x2, starting transfers between devices: none -> 9.06 us  [the longest x1 7.15 us: shards(): lax.ppermute(pair, 'row', [(i, (i + (2 if i % 2 == 0 else -2)) % n_panels...]
    another operation x15 -> x2, local copies, waits for them, and re-layouts: 4.22 us -> 0.01 us  [the longest x1 0.01 us: shards(): jnp.broadcast_to(tail, (2, TAIL, BS))]
    all_to_all x1, starting transfers between devices: 4.84 us -> 8.35 us  [shards(): lax.all_to_all(pieces, ('row', 'depth'), 0, 0, axis_index_groups=groups)]
    another operation x0 -> x3, other arithmetic: none -> 2.02 us
    pallas_call x2, Pallas kernels: 12.9 us -> 11.1 us  [the longest x1 8.82 us: products(): pl.pallas_call(functools.partial(product_kernel, rows, classes, matrix_ro...]
  transfers between devices with their start and end apart: 13 -> 11, of which waited for: 3 -> 4; matrix products, arithmetic and copies ran while one was open for 7% -> 3% of each run, Pallas kernels for 0% -> 0%
where the time goes in v2:
time: 114 us; the launch traced here: 112 us
  starting transfers between devices  44.9 us (39%)
  blocking collectives  28.4 us (25%)
  waiting for transfers between devices  19.1 us (17%)
  Pallas kernels  11.1 us (10%)
  other arithmetic  5.11 us (4%)
  local copies, waits for them, and re-layouts  3.34 us (3%)
    all_to_all x1, blocking collectives, shards(): received = lax.all_to_all(coded, 'depth', 0, 0)  28.4 us
    ppermute x8, starting transfers between devices, passed_along(): lax.ppermute(block, axis, [(i, (i + distance) % n) for i in range(n)])  27.5 us
    all_to_all x1, waiting for transfers between devices, shards(): lax.all_to_all(pieces, ('row', 'depth'), 0, 0, axis_index_groups=groups)  9.64 us
    ppermute x8, waiting for transfers between devices, passed_along(): lax.ppermute(block, axis, [(i, (i + distance) % n) for i in range(n)])  9.49 us
    pallas_call x1, Pallas kernels, products(): pl.pallas_call(functools.partial(product_kernel, rows, classes, matrix_ro...  8.82 us
    all_to_all x1, starting transfers between devices, shards(): lax.all_to_all(pieces, ('row', 'depth'), 0, 0, axis_index_groups=groups)  8.35 us
    ppermute x1, starting transfers between devices, shards(): lax.ppermute(pair, 'row', [(i, (i + (2 if i % 2 == 0 else -2)) % n_panels...  7.15 us
  transfers between devices with their start and end apart: 11, of which 4 were waited for; matrix products, arithmetic and copies ran while one was open for 3% of the time, Pallas kernels for 0%

profile of v2, /device:TPU:1, one launch (start us, length us, event | category | flops | bytes accessed | tf_op | source)
XLA Modules:
  0.0 112.2 jit_solution(7687218494637208238)
XLA Ops:
  0.0 0.6 compare_reduce_fusion
  0.6 1.3 %fusion = bf16[1,16]{1,0:T(2,128)(2,1)S(1)} fusion(pred[]{:T(512)} %compare_reduce_fusion, s32[16,1]{0,1:T(1,128)} %param.5), kind=kLoop, calls=%fused_computation.7 | loop fusion | flops 32 | bytes 97 | tf_op jit(solution)/shard_map/reshape.45
  2.0 1.1 pad_maximum_fusion.refs_0_.refs_9_
  3.0 5.9 %collective-permute-start.1 = (bf16[2,1040,128]{2,1,0:T(8,128)(2,1)S(1)}, bf16[2,1040,128]{2,1,0:T(8,128)(2,1)S(1)}, u32[]{:S(2)}, u32[]{:S(2)}) collective-permute-start(bf16[2,1040,128]{2,1,0:T(8,128)(2,1)S(1)} %pad_maximum_fusion.refs_0_.refs_9_), channel_id=1, source_target_pairs={{0,28},{4,0},{8,4},{12,8},{16,12},{20,16},{24,20},{28,24},{1,29},{... | collective-permute-start | bytes 1597448 | tf_op jit(solution)/shard_map/ppermute | solution.py:21
  9.0 1.9 %collective-permute-start = (bf16[2,1040,128]{2,1,0:T(8,128)(2,1)S(1)}, bf16[2,1040,128]{2,1,0:T(8,128)(2,1)S(1)}, u32[]{:S(2)}, u32[]{:S(2)}) collective-permute-start(bf16[2,1040,128]{2,1,0:T(8,128)(2,1)S(1)} %pad_maximum_fusion.refs_0_.refs_9_), channel_id=1, source_target_pairs={{0,4},{4,8},{8,12},{12,16},{16,20},{20,24},{24,28},{28,0},{1,5},{5... | collective-permute-start | bytes 1597448 | tf_op jit(solution)/shard_map/ppermute | solution.py:21
  11.0 1.1 %maximum_maximum_fusion = bf16[8,528,128]{2,1,0:T(8,128)(2,1)} fusion(bf16[4,16,128]{2,1,0:T(8,128)(2,1)S(1)} %broadcast_in_dim_broadcast_in_dim.5, bf16[4,512,128]{2,1,0:T(8,128)(2,1)S(1)} %bitcast.23), kind=kLoop, calls=%fused_computation | loop fusion | flops 4325376 | bytes 1622016 | tf_op jit(solution)/shard_map/concatenate | solution.py:231
  12.1 8.4 %all-to-all-start = ((bf16[8,528,128]{2,1,0:T(8,128)(2,1)}), bf16[8,528,128]{2,1,0:T(8,128)(2,1)S(1)}, u32[]{:S(2)}, u32[]{:S(2)}) async-start(bf16[8,528,128]{2,1,0:T(8,128)(2,1)} %maximum_maximum_fusion), calls=%async_computation | async-start | bytes 2162688 | tf_op jit(solution)/shard_map/all_to_all | solution.py:233
  20.5 0.0 collective-permute-done.1.refs_2_.refs_11_
  20.5 2.8 %collective-permute-start.3 = (bf16[2,1040,128]{2,1,0:T(8,128)(2,1)S(1)}, bf16[2,1040,128]{2,1,0:T(8,128)(2,1)}, u32[]{:S(2)}, u32[]{:S(2)}) collective-permute-start(bf16[2,1040,128]{2,1,0:T(8,128)(2,1)S(1)} %collective-permute-done.1.refs_2_.refs_11_), channel_id=1, source_target_pairs={{0,28},{4,0},{8,4},{12,8},{16,12},{20,16},{24,20},{28,24},{1,29},{... | collective-permute-start | bytes 1597448 | tf_op jit(solution)/shard_map/ppermute | solution.py:21
  23.3 0.0 collective-permute-done.refs_1_.refs_10_
  23.3 2.4 %collective-permute-start.2 = (bf16[2,1040,128]{2,1,0:T(8,128)(2,1)S(1)}, bf16[2,1040,128]{2,1,0:T(8,128)(2,1)}, u32[]{:S(2)}, u32[]{:S(2)}) collective-permute-start(bf16[2,1040,128]{2,1,0:T(8,128)(2,1)S(1)} %collective-permute-done.refs_1_.refs_10_), channel_id=1, source_target_pairs={{0,4},{4,8},{8,12},{12,16},{16,20},{20,24},{24,28},{28,0},{1,5},{5... | collective-permute-start | bytes 1597448 | tf_op jit(solution)/shard_map/ppermute | solution.py:21
  25.8 0.8 copy-done
  26.6 9.6 %all-to-all-done = bf16[8,528,128]{2,1,0:T(8,128)(2,1)S(1)} async-done(((bf16[8,528,128]{2,1,0:T(8,128)(2,1)}), bf16[8,528,128]{2,1,0:T(8,128)(2,1)S(1)}, u32[]{:S(2)}, u32[]{:S(2)}) %all-to-all-start) | async-done | bytes 1081376 | tf_op jit(solution)/shard_map/all_to_all | solution.py:233
  36.2 7.2 %collective-permute-start.8 = (bf16[4224,128]{1,0:T(8,128)(2,1)S(1)}, bf16[4224,128]{1,0:T(8,128)(2,1)}, u32[]{:S(2)}, u32[]{:S(2)}) collective-permute-start(bf16[4224,128]{1,0:T(8,128)(2,1)S(1)} %bitcast.20), channel_id=1, source_target_pairs={{0,64},{32,480},{64,128},{96,32},{128,192},{160,96},{192,256},{224... | collective-permute-start | bytes 3244040 | tf_op jit(solution)/shard_map/ppermute | solution.py:236
  43.4 0.0 collective-permute-done.3.refs_4_.refs_13_
  43.4 5.3 %collective-permute-start.5 = (bf16[2,1040,128]{2,1,0:T(8,128)(2,1)}, bf16[2,1040,128]{2,1,0:T(8,128)(2,1)S(1)}, u32[]{:S(2)}, u32[]{:S(2)}) collective-permute-start(bf16[2,1040,128]{2,1,0:T(8,128)(2,1)} %collective-permute-done.3.refs_4_.refs_13_), channel_id=1, source_target_pairs={{0,28},{4,0},{8,4},{12,8},{16,12},{20,16},{24,20},{28,24},{1,29},{... | collective-permute-start | bytes 1597448 | tf_op jit(solution)/shard_map/ppermute | solution.py:21
  48.6 0.0 collective-permute-done.2.refs_3_.refs_12_
  48.6 1.9 %collective-permute-start.4 = (bf16[2,1040,128]{2,1,0:T(8,128)(2,1)}, bf16[2,1040,128]{2,1,0:T(8,128)(2,1)S(1)}, u32[]{:S(2)}, u32[]{:S(2)}) collective-permute-start(bf16[2,1040,128]{2,1,0:T(8,128)(2,1)} %collective-permute-done.2.refs_3_.refs_12_), channel_id=1, source_target_pairs={{0,4},{4,8},{8,12},{12,16},{16,20},{20,24},{24,28},{28,0},{1,5},{5... | collective-permute-start | bytes 1597448 | tf_op jit(solution)/shard_map/ppermute | solution.py:21
  50.6 0.9 slice_select_fusion
  51.5 1.9 %collective-permute-start.9 = (bf16[2112,128]{1,0:T(8,128)(2,1)}, bf16[2112,128]{1,0:T(8,128)(2,1)}, u32[]{:S(2)}, u32[]{:S(2)}) collective-permute-start(bf16[2112,128]{1,0:T(8,128)(2,1)} %slice_select_fusion), channel_id=1, source_target_pairs={{0,448},{32,96},{64,0},{96,160},{128,64},{160,224},{192,128},{224,... | collective-permute-start | bytes 1622024 | tf_op jit(solution)/shard_map/ppermute | solution.py:239
  53.4 1.8 %collective-permute-done.5.refs_6_.refs_15_ = bf16[2,1040,128]{2,1,0:T(8,128)(2,1)S(1)} collective-permute-done((bf16[2,1040,128]{2,1,0:T(8,128)(2,1)}, bf16[2,1040,128]{2,1,0:T(8,128)(2,1)S(1)}, u32[]{:S(2)}, u32[]{:S(2)}) %collective-permute-start.5) | collective-permute-done | bytes 532512 | tf_op jit(solution)/shard_map/ppermute | solution.py:21
  55.1 0.7 slice_bitcast_fusion
  55.9 5.3 %collective-permute-start.7 = (bf16[1040,128]{1,0:T(8,128)(2,1)}, bf16[1040,128]{1,0:T(8,128)(2,1)}, u32[]{:S(2)}, u32[]{:S(2)}) collective-permute-start(bf16[1040,128]{1,0:T(8,128)(2,1)} %slice_bitcast_fusion), channel_id=1, source_target_pairs={{0,28},{4,0},{8,4},{12,8},{16,12},{20,16},{24,20},{28,24},{1,29},{... | collective-permute-start | bytes 798728 | tf_op jit(solution)/shard_map/ppermute | solution.py:21
  61.2 0.7 slice_bitcast_fusion.1
  61.9 1.9 %collective-permute-start.6 = (bf16[1040,128]{1,0:T(8,128)(2,1)}, bf16[1040,128]{1,0:T(8,128)(2,1)S(1)}, u32[]{:S(2)}, u32[]{:S(2)}) collective-permute-start(bf16[1040,128]{1,0:T(8,128)(2,1)} %slice_bitcast_fusion.1), channel_id=1, source_target_pairs={{0,4},{4,8},{8,12},{12,16},{16,20},{20,24},{24,28},{28,0},{1,5},{5... | collective-permute-start | bytes 798728 | tf_op jit(solution)/shard_map/ppermute | solution.py:21
  63.8 0.1 pad_add_fusion.here_ref
  63.9 2.0 %collective-permute-done.7.refs_8_ = bf16[1040,128]{1,0:T(8,128)(2,1)} collective-permute-done((bf16[1040,128]{1,0:T(8,128)(2,1)}, bf16[1040,128]{1,0:T(8,128)(2,1)}, u32[]{:S(2)}, u32[]{:S(2)}) %collective-permute-start.7) | collective-permute-done | bytes 266272 | tf_op jit(solution)/shard_map/ppermute | solution.py:21
  66.0 5.7 %collective-permute-done.6.refs_7_.refs_16_ = bf16[1040,128]{1,0:T(8,128)(2,1)S(1)} collective-permute-done((bf16[1040,128]{1,0:T(8,128)(2,1)}, bf16[1040,128]{1,0:T(8,128)(2,1)S(1)}, u32[]{:S(2)}, u32[]{:S(2)}) %collective-permute-start.6) | collective-permute-done | bytes 266272 | tf_op jit(solution)/shard_map/ppermute | solution.py:21
  71.6 1.0 copy-done.1
  72.7 8.8 %shard_map.28 = (s16[4,4,528,128]{3,2,1,0:T(8,128)(2,1)S(1)}, f32[2048,128]{1,0:T(8,128)S(1)}) custom-call(s32[3]{0:T(128)S(1)} %pad_add_fusion.here_ref, bf16[2,1040,128]{2,1,0:T(8,128)(2,1)S(1)} %pad_maximum_fusion.refs_0_.refs_9_, bf16[2,1040,128]{2,1,0:T(8,128)(2,1)S(1)} %copy-done.1, bf16[2,1040,128]{2,1,0:T(8,128)(2,1)S(1)} %collective-permute-done.1.refs_2_.refs_11_, ...), custom_call_target="tpu_custom_call" | custom-call | flops 2147483648 | bytes 12582912 | tf_op jit(solution)/shard_map/pallas_call | solution.py:154
  81.5 28.4 %all_to_all.10.refs_0_.refs_1_.refs_2_ = s16[4,4,528,128]{3,2,1,0:T(8,128)(2,1)S(1)} all-to-all(s16[4,4,528,128]{3,2,1,0:T(8,128)(2,1)S(1)} %get-tuple-element.22), channel_id=1, replica_groups=mesh['row'=16,'col'=8,'depth'=4] {'depth'}, dimensions={0} | all-to-all | bytes 4325376 | tf_op jit(solution)/shard_map/all_to_all | solution.py:242
  109.9 2.3 %shard_map.29 = bf16[2048,128]{1,0:T(8,128)(2,1)} custom-call(s32[3]{0:T(128)S(1)} %pad_add_fusion.here_ref, f32[2048,128]{1,0:T(8,128)S(1)} %get-tuple-element.21.own_ref, s16[4,4,528,128]{3,2,1,0:T(8,128)(2,1)S(1)} %all_to_all.10.refs_0_.refs_1_.refs_2_, s16[4,4,528,128]{3,2,1,0:T(8,128)(2,1)S(1)} %all_to_all.10.refs_0_.refs_1_.refs_2_, ...), custom_call_target="tpu_custom_call" | custom-call | tf_op jit(solution)/shard_map/pallas_call | solution.py:194
  (11 shorter events, 0.1 us)
Async XLA Ops:
  0.0 10.9 %copy-start.2 = (bf16[16,1,128,128]{3,2,1,0:T(8,128)(2,1)S(1)}, bf16[16,1,128,128]{3,2,1,0:T(8,128)(2,1)}, u32[]{:S(2)}) copy-start(bf16[16,1,128,128]{3,2,1,0:T(8,128)(2,1)} %param.4) | copy-start | bytes 1572868
  3.0 17.4 %collective-permute-start.1 = (bf16[2,1040,128]{2,1,0:T(8,128)(2,1)S(1)}, bf16[2,1040,128]{2,1,0:T(8,128)(2,1)S(1)}, u32[]{:S(2)}, u32[]{:S(2)}) collective-permute-start(bf16[2,1040,128]{2,1,0:T(8,128)(2,1)S(1)} %pad_maximum_fusion.refs_0_.refs_9_), channel_id=1, source_target_pairs={{0,28},{4,0},{8,4},{12,8},{16,12},{20,16},{24,20},{28,24},{1,29},{... | collective-permute-start | bytes 1597448 | tf_op jit(solution)/shard_map/ppermute | solution.py:21
  9.0 14.3 %collective-permute-start = (bf16[2,1040,128]{2,1,0:T(8,128)(2,1)S(1)}, bf16[2,1040,128]{2,1,0:T(8,128)(2,1)S(1)}, u32[]{:S(2)}, u32[]{:S(2)}) collective-permute-start(bf16[2,1040,128]{2,1,0:T(8,128)(2,1)S(1)} %pad_maximum_fusion.refs_0_.refs_9_), channel_id=1, source_target_pairs={{0,4},{4,8},{8,12},{12,16},{16,20},{20,24},{24,28},{28,0},{1,5},{5... | collective-permute-start | bytes 1597448 | tf_op jit(solution)/shard_map/ppermute | solution.py:21
  12.1 24.1 %all-to-all-start = ((bf16[8,528,128]{2,1,0:T(8,128)(2,1)}), bf16[8,528,128]{2,1,0:T(8,128)(2,1)S(1)}, u32[]{:S(2)}, u32[]{:S(2)}) async-start(bf16[8,528,128]{2,1,0:T(8,128)(2,1)} %maximum_maximum_fusion), calls=%async_computation | async-start | bytes 2162688 | tf_op jit(solution)/shard_map/all_to_all | solution.py:233
  20.5 22.9 %collective-permute-start.3 = (bf16[2,1040,128]{2,1,0:T(8,128)(2,1)S(1)}, bf16[2,1040,128]{2,1,0:T(8,128)(2,1)}, u32[]{:S(2)}, u32[]{:S(2)}) collective-permute-start(bf16[2,1040,128]{2,1,0:T(8,128)(2,1)S(1)} %collective-permute-done.1.refs_2_.refs_11_), channel_id=1, source_target_pairs={{0,28},{4,0},{8,4},{12,8},{16,12},{20,16},{24,20},{28,24},{1,29},{... | collective-permute-start | bytes 1597448 | tf_op jit(solution)/shard_map/ppermute | solution.py:21
  23.3 25.3 %collective-permute-start.2 = (bf16[2,1040,128]{2,1,0:T(8,128)(2,1)S(1)}, bf16[2,1040,128]{2,1,0:T(8,128)(2,1)}, u32[]{:S(2)}, u32[]{:S(2)}) collective-permute-start(bf16[2,1040,128]{2,1,0:T(8,128)(2,1)S(1)} %collective-permute-done.refs_1_.refs_10_), channel_id=1, source_target_pairs={{0,4},{4,8},{8,12},{12,16},{16,20},{20,24},{24,28},{28,0},{1,5},{5... | collective-permute-start | bytes 1597448 | tf_op jit(solution)/shard_map/ppermute | solution.py:21
  25.8 0.8 copy-start
  36.2 35.4 %collective-permute-start.8 = (bf16[4224,128]{1,0:T(8,128)(2,1)S(1)}, bf16[4224,128]{1,0:T(8,128)(2,1)}, u32[]{:S(2)}, u32[]{:S(2)}) collective-permute-start(bf16[4224,128]{1,0:T(8,128)(2,1)S(1)} %bitcast.20), channel_id=1, source_target_pairs={{0,64},{32,480},{64,128},{96,32},{128,192},{160,96},{192,256},{224... | collective-permute-start | bytes 3244040 | tf_op jit(solution)/shard_map/ppermute | solution.py:236
  43.4 11.8 %collective-permute-start.5 = (bf16[2,1040,128]{2,1,0:T(8,128)(2,1)}, bf16[2,1040,128]{2,1,0:T(8,128)(2,1)S(1)}, u32[]{:S(2)}, u32[]{:S(2)}) collective-permute-start(bf16[2,1040,128]{2,1,0:T(8,128)(2,1)} %collective-permute-done.3.refs_4_.refs_13_), channel_id=1, source_target_pairs={{0,28},{4,0},{8,4},{12,8},{16,12},{20,16},{24,20},{28,24},{1,29},{... | collective-permute-start | bytes 1597448 | tf_op jit(solution)/shard_map/ppermute | solution.py:21
  48.6 12.5 %collective-permute-start.4 = (bf16[2,1040,128]{2,1,0:T(8,128)(2,1)}, bf16[2,1040,128]{2,1,0:T(8,128)(2,1)S(1)}, u32[]{:S(2)}, u32[]{:S(2)}) collective-permute-start(bf16[2,1040,128]{2,1,0:T(8,128)(2,1)} %collective-permute-done.2.refs_3_.refs_12_), channel_id=1, source_target_pairs={{0,4},{4,8},{8,12},{12,16},{16,20},{20,24},{24,28},{28,0},{1,5},{5... | collective-permute-start | bytes 1597448 | tf_op jit(solution)/shard_map/ppermute | solution.py:21
  51.5 12.5 %collective-permute-start.9 = (bf16[2112,128]{1,0:T(8,128)(2,1)}, bf16[2112,128]{1,0:T(8,128)(2,1)}, u32[]{:S(2)}, u32[]{:S(2)}) collective-permute-start(bf16[2112,128]{1,0:T(8,128)(2,1)} %slice_select_fusion), channel_id=1, source_target_pairs={{0,448},{32,96},{64,0},{96,160},{128,64},{160,224},{192,128},{224,... | collective-permute-start | bytes 1622024 | tf_op jit(solution)/shard_map/ppermute | solution.py:239
  55.9 10.1 %collective-permute-start.7 = (bf16[1040,128]{1,0:T(8,128)(2,1)}, bf16[1040,128]{1,0:T(8,128)(2,1)}, u32[]{:S(2)}, u32[]{:S(2)}) collective-permute-start(bf16[1040,128]{1,0:T(8,128)(2,1)} %slice_bitcast_fusion), channel_id=1, source_target_pairs={{0,28},{4,0},{8,4},{12,8},{16,12},{20,16},{24,20},{28,24},{1,29},{... | collective-permute-start | bytes 798728 | tf_op jit(solution)/shard_map/ppermute | solution.py:21
  61.9 9.7 %collective-permute-start.6 = (bf16[1040,128]{1,0:T(8,128)(2,1)}, bf16[1040,128]{1,0:T(8,128)(2,1)S(1)}, u32[]{:S(2)}, u32[]{:S(2)}) collective-permute-start(bf16[1040,128]{1,0:T(8,128)(2,1)} %slice_bitcast_fusion.1), channel_id=1, source_target_pairs={{0,4},{4,8},{8,12},{12,16},{16,20},{20,24},{24,28},{28,0},{1,5},{5... | collective-permute-start | bytes 798728 | tf_op jit(solution)/shard_map/ppermute | solution.py:21
  71.6 1.0 copy-start.1

commit v3 on v2

v3 whole, which is shorter than its diff:
```python
import functools

import jax
import jax.numpy as jnp
from jax import lax
from jax.experimental import pallas as pl
from jax.experimental.pallas import tpu as pltpu
from jax.sharding import PartitionSpec as P

BS = 128
TAIL = 16
STEP = 4
PART_ROWS = 16
PANELS = 5
SPAN = 4 * BS + TAIL
QMAX = 32700.0
TINY = 2.0**-111


def passed_along(block, axis, distance):
    n = lax.axis_size(axis)
    return lax.ppermute(block, axis, [(i, (i + distance) % n) for i in range(n)])


def offsets(left_tails, window_tails, x, anchor, matrix_rows, classes, zero_at):
    sub = lax.broadcasted_iota(jnp.int32, (8, BS), 0)
    lane = lax.broadcasted_iota(jnp.int32, (8, BS), 1)

    def numbers(tile):
        return tile.astype(jnp.float32)[:8].astype(jnp.int32)

    cols = jnp.zeros((8, BS), jnp.int32)
    for s in range(8):
        cols = jnp.where(sub == s, numbers(left_tails[s]), cols)
    place = lax.shift_right_logical((cols - anchor + 2 * matrix_rows) & (matrix_rows - 1), 2)
    base = lax.shift_right_logical(place, 2) * (classes * SPAN) + (place & 3) * BS
    result = []
    for m in range(classes):
        tails = [numbers(window_tails[p * classes + m]) for p in range(PANELS)]
        found = jnp.zeros((8, BS), jnp.int32)
        for p in range(PANELS):
            for a in range(4):
                column = jnp.sum(jnp.where(lane == 4 * a + x, tails[p], 0), axis=1, keepdims=True)
                hit = (place == 4 * p + a) & (tails[PANELS // 2] == column)
                found = jnp.where(hit, 1, found)
        result.append(jnp.where(found == 1, base + m * SPAN, zero_at))
    return result


def product_kernel(first, start, half_rows, classes, matrix_rows, here_ref, *refs):
    if first:
        lefts, tail_sources, refs = refs[:9], refs[9:17], refs[17:]
        window_pieces, (pair, far, cross), refs = refs[:3], refs[3:6], refs[6:]
        q_ref, own_ref, wide, held, tails, idx_ref, sems = refs
    else:
        idx_ref, *refs = refs
        lefts, (pair, far, cross), refs = refs[:9], refs[9:12], refs[12:]
        q_ref, own_ref, held, sems = refs
    step = pl.program_id(0)
    panel = classes * SPAN
    zero_at = PANELS * panel
    x, core, anchor = here_ref[0], here_ref[1], here_ref[2]

    @pl.when(step == 0)
    def _():
        pieces = ((pair, 2 - core, 2), (far, 3 * core, 2), (cross, 4 - 4 * core, 1))
        copies, tail_copies = [], []
        if first:
            for s in range(8):
                at = pl.ds(half_rows * BS, TAIL)
                source = tail_sources[s].at[0, at] if s < 7 else tail_sources[s].at[at]
                tail_copies.append(pltpu.make_async_copy(source, tails.at[s], sems.at[s]))
            for n, (source, p, count) in enumerate(pieces):
                source = window_pieces[n].at[:, pl.ds(4 * BS, TAIL)]
                at = pl.ds(8 + p * classes, count * classes)
                tail_copies.append(pltpu.make_async_copy(source, tails.at[at], sems.at[8 + n]))
        for n, (source, p, count) in enumerate(pieces):
            at = pl.ds(pl.multiple_of(p * panel, TAIL), count * panel)
            copies.append(pltpu.make_async_copy(source, held.at[at], sems.at[11 + n]))
        for copy in tail_copies + copies:
            copy.start()
        held[pl.ds(zero_at, BS), :] = jnp.zeros((BS, BS), held.dtype)
        for copy in tail_copies:
            copy.wait()
        if first:
            left_tails = [tails[s] for s in range(8)]
            window_tails = [tails[8 + n] for n in range(PANELS * classes)]
            found = offsets(left_tails, window_tails, x, anchor, matrix_rows, classes, zero_at)
            for m in range(classes):
                wide[pl.ds(m * 8, 8), :] = found[m]
            copies.append(pltpu.make_async_copy(wide, idx_ref, sems.at[14]))
            copies[-1].start()
        for copy in copies:
            copy.wait()

    slots = [lax.rem(x + d, classes) for d in range(classes)]
    codes = [[] for _ in range(classes)]
    in_first_half = step * STEP + start < half_rows
    for r in range(STEP):
        at = slice(r * BS, (r + 1) * BS)
        row = step * STEP + r + start
        left = [ref[0, at, :] for ref in lefts[:7]]
        left.append(jnp.where(in_first_half, lefts[7][at, :], lefts[8][at, :]))
        left = jnp.concatenate(left, axis=1)
        right = []
        for d in range(classes):
            picked = []
            for s in range(8):
                k = idx_ref[slots[d] * 8 + s, row]
                picked.append(held[pl.ds(pl.multiple_of(k, TAIL), BS), :])
            right.append(jnp.concatenate(picked, axis=0))
        right = jnp.concatenate(right, axis=1)
        sums = jnp.dot(left, right, preferred_element_type=jnp.float32)
        own_ref[at, :] = sums[:, :BS]
        for d in range(1, classes):
            part = sums[:, d * BS : (d + 1) * BS]
            top = jnp.max(jnp.max(jnp.abs(part), axis=0, keepdims=True), axis=1, keepdims=True)
            code = jnp.ceil(jnp.log2(jnp.maximum(top, TINY)) * 16.0)
            scaled = part * (jnp.exp2(code * (-1.0 / 16.0)) * QMAX)
            coded = jnp.round(jnp.clip(scaled, -32767.0, 32767.0)).astype(jnp.int32)
            q_ref[slots[d], 0, at, :] = coded.astype(jnp.int16)
            codes[d].append(code)
    sub = lax.broadcasted_iota(jnp.int32, (TAIL, BS), 0)
    for d in range(1, classes):
        lines = jnp.zeros((TAIL, BS), jnp.float32)
        for r in range(STEP):
            lines = jnp.where(sub == r, codes[d][r], lines)
        q_ref[slots[d], 0, pl.ds(STEP * BS, TAIL), :] = lines.astype(jnp.int32).astype(jnp.int16)


def products(here, idx, lefts, windows, start, rows, half_rows, classes, matrix_rows):
    first = idx is None
    n_steps = rows // STEP
    per_half = half_rows // STEP
    block = STEP * BS
    anywhere = pl.BlockSpec(memory_space=pl.ANY)

    def left_at(g, *_):
        g = g + start // STEP
        return (g // per_half, g % per_half, 0)

    out_specs = [
        pl.BlockSpec((classes, 1, block + TAIL, BS), lambda g, *_: (0, g, 0, 0)),
        pl.BlockSpec((block, BS), lambda g, *_: (g, 0)),
    ]
    out_shape = [
        jax.ShapeDtypeStruct((classes, n_steps, block + TAIL, BS), jnp.int16),
        jax.ShapeDtypeStruct((rows * BS, BS), jnp.float32),
    ]
    scratch = [pltpu.VMEM((PANELS * classes * SPAN + BS, BS), jnp.bfloat16)]
    if first:
        out_specs.append(pl.BlockSpec((classes * 8, BS), lambda g, *_: (0, 0)))
        out_shape.append(jax.ShapeDtypeStruct((classes * 8, BS), jnp.int32))
        scratch += [pltpu.VMEM((8 + PANELS * classes, TAIL, BS), jnp.bfloat16), pltpu.SMEM((classes * 8, BS), jnp.int32)]
        operands = [here, *lefts, *lefts[:8], *(w.reshape(-1, SPAN, BS) for w in windows), *windows]
    else:
        operands = [here, idx, *lefts, *windows]
    grid_spec = pltpu.PrefetchScalarGridSpec(
        num_scalar_prefetch=1 if first else 2,
        grid=(n_steps,),
        in_specs=[pl.BlockSpec((1, block, BS), left_at)] * 7
        + [pl.BlockSpec((block, BS), lambda g, *_: (jnp.minimum(g + start // STEP, per_half - 1), 0))]
        + [pl.BlockSpec((block, BS), lambda g, *_: (jnp.maximum(g + start // STEP - per_half, 0), 0))]
        + [anywhere] * (14 if first else 3),
        out_specs=out_specs,
        scratch_shapes=scratch + [pltpu.SemaphoreType.DMA((15,))],
    )
    return pl.pallas_call(
        functools.partial(product_kernel, first, start, half_rows, classes, matrix_rows),
        grid_spec=grid_spec,
        out_shape=out_shape,
        compiler_params=pltpu.CompilerParams(vmem_limit_bytes=12 * 2**20),
        cost_estimate=pl.CostEstimate(
            flops=2 * rows * 32 * BS**3, bytes_accessed=12 * 2**20, transcendentals=0
        ),
    )(*operands)


def sum_kernel(n_steps, n_parts, here_ref, *refs):
    out_ref = refs[-1]

    def add(own_ref, *received):
        scales = []
        for part in received:
            code = part[0, 0, pl.ds(STEP * BS, TAIL), :].astype(jnp.int32).astype(jnp.float32)
            scales.append(jnp.exp2(code * (1.0 / 16.0)) * (1.0 / QMAX))
        for r in range(STEP):
            at = slice(r * BS, (r + 1) * BS)
            total = own_ref[at, :]
            for part, scale in zip(received, scales):
                total = total + part[0, 0, at, :].astype(jnp.int32).astype(jnp.float32) * scale[r : r + 1, :]
            out_ref[at, :] = total.astype(jnp.bfloat16)

    for n in range(n_parts):
        pl.when(pl.program_id(0) // n_steps == n)(functools.partial(add, *refs[4 * n : 4 * n + 4]))


def summed(here, parts, rows, classes):
    block = STEP * BS
    n_steps = rows // STEP
    specs, operands = [], []
    for n, (own, received) in enumerate(parts):

        def at(g, n=n):
            return jnp.clip(g - n * n_steps, 0, n_steps - 1)

        specs.append(pl.BlockSpec((block, BS), lambda g, h, at=at: (at(g), 0)))
        for d in (1, 2, 3):
            specs.append(
                pl.BlockSpec(
                    (1, 1, block + TAIL, BS), lambda g, h, at=at, d=d: (lax.rem(h[0] + d, classes), at(g), 0, 0)
                )
            )
        operands += [own, received, received, received]
    grid_spec = pltpu.PrefetchScalarGridSpec(
        num_scalar_prefetch=1,
        grid=(len(parts) * n_steps,),
        in_specs=specs,
        out_specs=pl.BlockSpec((block, BS), lambda g, h: (g, 0)),
    )
    return pl.pallas_call(
        functools.partial(sum_kernel, n_steps, len(parts)),
        grid_spec=grid_spec,
        out_shape=jax.ShapeDtypeStruct((len(parts) * rows * BS, BS), jnp.bfloat16),
        compiler_params=pltpu.CompilerParams(vmem_limit_bytes=12 * 2**20),
    )(here, *operands)


def own_payload_kernel(half_rows, cols_ref, blocks_ref, out_ref):
    shape = (cols_ref.shape[0], BS)
    own_lane = lax.broadcasted_iota(jnp.int32, shape, 0) == lax.broadcasted_iota(jnp.int32, shape, 1)
    numbers = jnp.broadcast_to(cols_ref[...], shape).astype(jnp.float32)
    line = jnp.sum(jnp.where(own_lane, numbers, 0.0), axis=0, keepdims=True)
    tail = jnp.broadcast_to(line, (TAIL, BS)).astype(jnp.bfloat16)
    span = half_rows * BS
    for half in range(2):
        out_ref[half, pl.ds(0, span), :] = blocks_ref[pl.ds(half * span, span), :]
        out_ref[half, pl.ds(span, TAIL), :] = tail


def own_payload(blocks, cols, half_rows):
    return pl.pallas_call(
        functools.partial(own_payload_kernel, half_rows),
        out_shape=jax.ShapeDtypeStruct((2, half_rows * BS + TAIL, BS), jnp.bfloat16),
        compiler_params=pltpu.CompilerParams(vmem_limit_bytes=8 * 2**20),
    )(cols, blocks)


def pieces_kernel(classes, payload_ref, out_ref):
    rows = 2 * (payload_ref.shape[1] - TAIL) // BS
    for x in range(classes):
        for n in range(rows // classes):
            row = n * classes + x
            half, at = row // (rows // 2), row % (rows // 2) * BS
            block = payload_ref[half, pl.ds(at, BS), :]
            out_ref[x, pl.ds(n * BS, BS), :] = block
            out_ref[x + classes, pl.ds(n * BS, BS), :] = block
        tail = payload_ref[0, pl.ds(rows // 2 * BS, TAIL), :]
        out_ref[x, pl.ds(4 * BS, TAIL), :] = tail
        out_ref[x + classes, pl.ds(4 * BS, TAIL), :] = tail


def residue_pieces(payload, classes):
    return pl.pallas_call(
        functools.partial(pieces_kernel, classes),
        out_shape=jax.ShapeDtypeStruct((2 * classes, SPAN, BS), jnp.bfloat16),
        compiler_params=pltpu.CompilerParams(vmem_limit_bytes=8 * 2**20),
    )(payload)


def shards(p_blocks, p_cols):
    rows = p_blocks.shape[0]
    classes = lax.axis_size("depth")
    n_panels = lax.axis_size("row")
    matrix_rows = rows * n_panels
    r = lax.axis_index("row")
    core = lax.rem(r, 2)
    here = jnp.stack([lax.axis_index("depth"), core, (r - PANELS // 2) * rows]).astype(jnp.int32)

    own = own_payload(p_blocks.reshape(rows * BS, BS), p_cols, rows // 2)
    down = up = own
    left = [own]
    for hop in range(3):
        down = passed_along(down, "col", 1)
        up = passed_along(up, "col", -1)
        left += [down, up]
        if hop == 0:
            after_first = (down, up)
    halves = [passed_along(down[0], "col", 1), passed_along(up[1], "col", -1)]

    pieces = residue_pieces(own, classes)
    groups = [[(2 * z + c) * classes + x for c in range(2) for x in range(classes)] for z in range(n_panels // 2)]
    pair = lax.all_to_all(pieces, ("row", "depth"), 0, 0, axis_index_groups=groups)
    pair = pair.reshape(2 * classes * SPAN, BS)
    pair, *_ = lax.optimization_barrier((pair,) + after_first)
    far = lax.ppermute(pair, "row", [(i, (i + (2 if i % 2 == 0 else -2)) % n_panels) for i in range(n_panels)])
    panel = classes * SPAN
    cross = jnp.where(core == 0, pair[:panel], pair[panel:])
    cross = lax.ppermute(cross, "row", [(i, (i + (-2 if i % 2 == 0 else 2)) % n_panels) for i in range(n_panels)])

    windows = (pair, far, cross)
    left[1:7] = [pltpu.with_memory_space_constraint(shard, pltpu.HBM) for shard in left[1:7]]
    idx, parts = None, []
    for start in range(0, rows, PART_ROWS):
        coded, mine, *found = products(
            here, idx, left + halves, windows, start, PART_ROWS, rows // 2, classes, matrix_rows
        )
        idx = found[0] if found else idx
        parts.append((mine, lax.all_to_all(coded, "depth", 0, 0)))
    return summed(here, parts, PART_ROWS, classes).reshape(rows, 1, BS, BS)


def solution(mesh):
    return jax.shard_map(
        shards,
        mesh=mesh,
        in_specs=(P("row", ("col", "depth"), None, None), P("row", ("col", "depth"))),
        out_specs=P("row", ("col", "depth"), None, None),
        check_vma=False,
    )
```

time: 114 us -> 112 us (0.982)
  other arithmetic: 5.11 us -> 0.93 us
  Pallas kernels: 11.1 us -> 12.4 us
    concatenate x2 -> x0, other arithmetic: 2.21 us -> none  [the longest x1 1.13 us: shards(): pieces = jnp.concatenate([pieces, pieces], axis=0)]
    another operation x2 -> x0, other arithmetic: 1.94 us -> none
    pallas_call x2 -> x4, Pallas kernels: 11.1 us -> 12.4 us  [the longest x1 8.94 us: products(): pl.pallas_call(functools.partial(product_kernel, first, start, half_rows,...]
  transfers between devices with their start and end apart: 11 -> 11, of which waited for: 4 -> 4; matrix products, arithmetic and copies ran while one was open for 3% -> 2% of each run, Pallas kernels for 0% -> 1%
where the time goes in v3:
time: 112 us; the launch traced here: 110 us
  starting transfers between devices  44.8 us (40%)
  blocking collectives  28.6 us (26%)
  waiting for transfers between devices  19.7 us (18%)
  Pallas kernels  12.4 us (11%)
  local copies, waits for them, and re-layouts  3.43 us (3%)
    all_to_all x1, blocking collectives, shards(): parts.append((mine, lax.all_to_all(coded, 'depth', 0, 0)))  28.6 us
    ppermute x8, starting transfers between devices, passed_along(): lax.ppermute(block, axis, [(i, (i + distance) % n) for i in range(n)])  27.4 us
    all_to_all x1, waiting for transfers between devices, shards(): lax.all_to_all(pieces, ('row', 'depth'), 0, 0, axis_index_groups=groups)  10.4 us
    ppermute x8, waiting for transfers between devices, passed_along(): lax.ppermute(block, axis, [(i, (i + distance) % n) for i in range(n)])  9.33 us
    pallas_call x1, Pallas kernels, products(): pl.pallas_call(functools.partial(product_kernel, first, start, half_rows,...  8.94 us
    all_to_all x1, starting transfers between devices, shards(): lax.all_to_all(pieces, ('row', 'depth'), 0, 0, axis_index_groups=groups)  8.35 us
    ppermute x1, starting transfers between devices, shards(): lax.ppermute(pair, 'row', [(i, (i + (2 if i % 2 == 0 else -2)) % n_panels...  7.15 us
    pallas_call x1, Pallas kernels, summed(): pl.pallas_call(functools.partial(sum_kernel, n_steps, len(parts)), grid_s...  2.29 us
  transfers between devices with their start and end apart: 11, of which 4 were waited for; matrix products, arithmetic and copies ran while one was open for 2% of the time, Pallas kernels for 1%

profile of v3, /device:TPU:1, one launch (start us, length us, event | category | flops | bytes accessed | tf_op | source)
XLA Modules:
  0.0 110.1 jit_solution(4969543927941914037)
XLA Ops:
  0.0 0.7 copy.3.cols_ref
  0.7 1.0 copy-done
  1.8 0.1 shard_map.28.payload_ref.refs_0_.refs_9_
  1.9 5.9 %collective-permute-start.1 = (bf16[2,1040,128]{2,1,0:T(8,128)(2,1)S(1)}, bf16[2,1040,128]{2,1,0:T(8,128)(2,1)S(1)}, u32[]{:S(2)}, u32[]{:S(2)}) collective-permute-start(bf16[2,1040,128]{2,1,0:T(8,128)(2,1)S(1)} %shard_map.28.payload_ref.refs_0_.refs_9_), channel_id=1, source_target_pairs={{0,28},{4,0},{8,4},{12,8},{16,12},{20,16},{24,20},{28,24},{1,29},{... | collective-permute-start | bytes 1597448 | tf_op jit(solution)/shard_map/ppermute | solution.py:22
  7.8 1.9 %collective-permute-start = (bf16[2,1040,128]{2,1,0:T(8,128)(2,1)S(1)}, bf16[2,1040,128]{2,1,0:T(8,128)(2,1)}, u32[]{:S(2)}, u32[]{:S(2)}) collective-permute-start(bf16[2,1040,128]{2,1,0:T(8,128)(2,1)S(1)} %shard_map.28.payload_ref.refs_0_.refs_9_), channel_id=1, source_target_pairs={{0,4},{4,8},{8,12},{12,16},{16,20},{20,24},{24,28},{28,0},{1,5},{5... | collective-permute-start | bytes 1597448 | tf_op jit(solution)/shard_map/ppermute | solution.py:22
  9.7 1.1 %shard_map.29 = bf16[8,528,128]{2,1,0:T(8,128)(2,1)} custom-call(bf16[2,1040,128]{2,1,0:T(8,128)(2,1)S(1)} %shard_map.28.payload_ref.refs_0_.refs_9_), custom_call_target="tpu_custom_call" | custom-call | tf_op jit(solution)/shard_map/pallas_call | solution.py:264
  10.8 8.4 %all-to-all-start = ((bf16[8,528,128]{2,1,0:T(8,128)(2,1)}), bf16[8,528,128]{2,1,0:T(8,128)(2,1)S(1)}, u32[]{:S(2)}, u32[]{:S(2)}) async-start(bf16[8,528,128]{2,1,0:T(8,128)(2,1)} %shard_map.29), calls=%async_computation | async-start | bytes 2162688 | tf_op jit(solution)/shard_map/all_to_all | solution.py:293
  19.2 0.0 collective-permute-done.1.refs_2_.refs_11_
  19.2 2.9 %collective-permute-start.3 = (bf16[2,1040,128]{2,1,0:T(8,128)(2,1)S(1)}, bf16[2,1040,128]{2,1,0:T(8,128)(2,1)}, u32[]{:S(2)}, u32[]{:S(2)}) collective-permute-start(bf16[2,1040,128]{2,1,0:T(8,128)(2,1)S(1)} %collective-permute-done.1.refs_2_.refs_11_), channel_id=1, source_target_pairs={{0,28},{4,0},{8,4},{12,8},{16,12},{20,16},{24,20},{28,24},{1,29},{... | collective-permute-start | bytes 1597448 | tf_op jit(solution)/shard_map/ppermute | solution.py:22
  22.1 0.0 collective-permute-done.refs_1_.refs_10_
  22.1 2.4 %collective-permute-start.2 = (bf16[2,1040,128]{2,1,0:T(8,128)(2,1)}, bf16[2,1040,128]{2,1,0:T(8,128)(2,1)}, u32[]{:S(2)}, u32[]{:S(2)}) collective-permute-start(bf16[2,1040,128]{2,1,0:T(8,128)(2,1)} %collective-permute-done.refs_1_.refs_10_), channel_id=1, source_target_pairs={{0,4},{4,8},{8,12},{12,16},{16,20},{20,24},{24,28},{28,0},{1,5},{5... | collective-permute-start | bytes 1597448 | tf_op jit(solution)/shard_map/ppermute | solution.py:22
  24.5 10.4 %all-to-all-done = bf16[8,528,128]{2,1,0:T(8,128)(2,1)S(1)} async-done(((bf16[8,528,128]{2,1,0:T(8,128)(2,1)}), bf16[8,528,128]{2,1,0:T(8,128)(2,1)S(1)}, u32[]{:S(2)}, u32[]{:S(2)}) %all-to-all-start) | async-done | bytes 1081376 | tf_op jit(solution)/shard_map/all_to_all | solution.py:293
  34.9 7.2 %collective-permute-start.8 = (bf16[4224,128]{1,0:T(8,128)(2,1)S(1)}, bf16[4224,128]{1,0:T(8,128)(2,1)S(1)}, u32[]{:S(2)}, u32[]{:S(2)}) collective-permute-start(bf16[4224,128]{1,0:T(8,128)(2,1)S(1)} %bitcast.15), channel_id=1, source_target_pairs={{0,64},{32,480},{64,128},{96,32},{128,192},{160,96},{192,256},{224... | collective-permute-start | bytes 3244040 | tf_op jit(solution)/shard_map/ppermute | solution.py:296
  42.1 0.0 collective-permute-done.3.refs_4_.refs_13_
  42.1 5.3 %collective-permute-start.5 = (bf16[2,1040,128]{2,1,0:T(8,128)(2,1)}, bf16[2,1040,128]{2,1,0:T(8,128)(2,1)S(1)}, u32[]{:S(2)}, u32[]{:S(2)}) collective-permute-start(bf16[2,1040,128]{2,1,0:T(8,128)(2,1)} %collective-permute-done.3.refs_4_.refs_13_), channel_id=1, source_target_pairs={{0,28},{4,0},{8,4},{12,8},{16,12},{20,16},{24,20},{28,24},{1,29},{... | collective-permute-start | bytes 1597448 | tf_op jit(solution)/shard_map/ppermute | solution.py:22
  47.4 1.9 %collective-permute-start.4 = (bf16[2,1040,128]{2,1,0:T(8,128)(2,1)}, bf16[2,1040,128]{2,1,0:T(8,128)(2,1)S(1)}, u32[]{:S(2)}, u32[]{:S(2)}) collective-permute-start(bf16[2,1040,128]{2,1,0:T(8,128)(2,1)} %collective-permute-done.2.refs_3_.refs_12_), channel_id=1, source_target_pairs={{0,4},{4,8},{8,12},{12,16},{16,20},{20,24},{24,28},{28,0},{1,5},{5... | collective-permute-start | bytes 1597448 | tf_op jit(solution)/shard_map/ppermute | solution.py:22
  49.3 0.9 slice_select_fusion
  50.2 1.9 %collective-permute-start.9 = (bf16[2112,128]{1,0:T(8,128)(2,1)}, bf16[2112,128]{1,0:T(8,128)(2,1)S(1)}, u32[]{:S(2)}, u32[]{:S(2)}) collective-permute-start(bf16[2112,128]{1,0:T(8,128)(2,1)} %slice_select_fusion), channel_id=1, source_target_pairs={{0,448},{32,96},{64,0},{96,160},{128,64},{160,224},{192,128},{224,... | collective-permute-start | bytes 1622024 | tf_op jit(solution)/shard_map/ppermute | solution.py:299
  52.1 1.8 %collective-permute-done.5.refs_6_.refs_15_ = bf16[2,1040,128]{2,1,0:T(8,128)(2,1)S(1)} collective-permute-done((bf16[2,1040,128]{2,1,0:T(8,128)(2,1)}, bf16[2,1040,128]{2,1,0:T(8,128)(2,1)S(1)}, u32[]{:S(2)}, u32[]{:S(2)}) %collective-permute-start.5) | collective-permute-done | bytes 532512 | tf_op jit(solution)/shard_map/ppermute | solution.py:22
  53.9 0.8 slice_bitcast_fusion
  54.6 5.2 %collective-permute-start.7 = (bf16[1040,128]{1,0:T(8,128)(2,1)}, bf16[1040,128]{1,0:T(8,128)(2,1)}, u32[]{:S(2)}, u32[]{:S(2)}) collective-permute-start(bf16[1040,128]{1,0:T(8,128)(2,1)} %slice_bitcast_fusion), channel_id=1, source_target_pairs={{0,28},{4,0},{8,4},{12,8},{16,12},{20,16},{24,20},{28,24},{1,29},{... | collective-permute-start | bytes 798728 | tf_op jit(solution)/shard_map/ppermute | solution.py:22
  59.9 0.8 slice_bitcast_fusion.1
  60.6 0.1 copy-done.2
  60.8 1.9 %collective-permute-start.6 = (bf16[1040,128]{1,0:T(8,128)(2,1)}, bf16[1040,128]{1,0:T(8,128)(2,1)S(1)}, u32[]{:S(2)}, u32[]{:S(2)}) collective-permute-start(bf16[1040,128]{1,0:T(8,128)(2,1)} %slice_bitcast_fusion.1), channel_id=1, source_target_pairs={{0,4},{4,8},{8,12},{12,16},{16,20},{20,24},{24,28},{28,0},{1,5},{5... | collective-permute-start | bytes 798728 | tf_op jit(solution)/shard_map/ppermute | solution.py:22
  62.7 0.1 pad_add_fusion.here_ref
  62.8 0.0 collective-permute-done.9.refs_22_
  62.8 1.7 %collective-permute-done.7.refs_8_ = bf16[1040,128]{1,0:T(8,128)(2,1)} collective-permute-done((bf16[1040,128]{1,0:T(8,128)(2,1)}, bf16[1040,128]{1,0:T(8,128)(2,1)}, u32[]{:S(2)}, u32[]{:S(2)}) %collective-permute-start.7) | collective-permute-done | bytes 266272 | tf_op jit(solution)/shard_map/ppermute | solution.py:22
  64.5 5.9 %collective-permute-done.6.refs_7_.refs_16_ = bf16[1040,128]{1,0:T(8,128)(2,1)S(1)} collective-permute-done((bf16[1040,128]{1,0:T(8,128)(2,1)}, bf16[1040,128]{1,0:T(8,128)(2,1)S(1)}, u32[]{:S(2)}, u32[]{:S(2)}) %collective-permute-start.6) | collective-permute-done | bytes 266272 | tf_op jit(solution)/shard_map/ppermute | solution.py:22
  70.3 0.0 collective-permute-done.8.refs_21_
  70.3 8.9 %shard_map.30 = (s16[4,4,528,128]{3,2,1,0:T(8,128)(2,1)S(1)}, f32[2048,128]{1,0:T(8,128)S(1)}, s32[32,128]{1,0:T(8,128)}) custom-call(s32[3]{0:T(128)S(1)} %pad_add_fusion.here_ref, bf16[2,1040,128]{2,1,0:T(8,128)(2,1)S(1)} %shard_map.28.payload_ref.refs_0_.refs_9_, bf16[2,1040,128]{2,1,0:T(8,128)(2,1)} %collective-permute-done.refs_1_.refs_10_, ...), custom_call_target="tpu_custom_call" | custom-call | flops 2147483648 | bytes 12582912 | tf_op jit(solution)/shard_map/pallas_call | solution.py:168
  79.2 28.6 %all_to_all.10.refs_1_.refs_2_.refs_3_ = s16[4,4,528,128]{3,2,1,0:T(8,128)(2,1)S(1)} all-to-all(s16[4,4,528,128]{3,2,1,0:T(8,128)(2,1)S(1)} %get-tuple-element.10), channel_id=1, replica_groups=mesh['row'=16,'col'=8,'depth'=4] {'depth'}, dimensions={0} | all-to-all | bytes 4325376 | tf_op jit(solution)/shard_map/all_to_all | solution.py:309
  107.8 2.3 %shard_map.31 = bf16[2048,128]{1,0:T(8,128)(2,1)} custom-call(s32[3]{0:T(128)S(1)} %pad_add_fusion.here_ref, f32[2048,128]{1,0:T(8,128)S(1)} %get-tuple-element.9.refs_0_, s16[4,4,528,128]{3,2,1,0:T(8,128)(2,1)S(1)} %all_to_all.10.refs_1_.refs_2_.refs_3_, s16[4,4,528,128]{3,2,1,0:T(8,128)(2,1)S(1)} %all_to_all.10.refs_1_.refs_2_.refs_3_, ...), custom_call_target="tpu_custom_call" | custom-call | tf_op jit(solution)/shard_map/pallas_call | solution.py:221
  (8 shorter events, 0.0 us)
Async XLA Ops:
  0.7 1.0 copy-start
  1.9 17.3 %collective-permute-start.1 = (bf16[2,1040,128]{2,1,0:T(8,128)(2,1)S(1)}, bf16[2,1040,128]{2,1,0:T(8,128)(2,1)S(1)}, u32[]{:S(2)}, u32[]{:S(2)}) collective-permute-start(bf16[2,1040,128]{2,1,0:T(8,128)(2,1)S(1)} %shard_map.28.payload_ref.refs_0_.refs_9_), channel_id=1, source_target_pairs={{0,28},{4,0},{8,4},{12,8},{16,12},{20,16},{24,20},{28,24},{1,29},{... | collective-permute-start | bytes 1597448 | tf_op jit(solution)/shard_map/ppermute | solution.py:22
  7.8 14.3 %collective-permute-start = (bf16[2,1040,128]{2,1,0:T(8,128)(2,1)S(1)}, bf16[2,1040,128]{2,1,0:T(8,128)(2,1)}, u32[]{:S(2)}, u32[]{:S(2)}) collective-permute-start(bf16[2,1040,128]{2,1,0:T(8,128)(2,1)S(1)} %shard_map.28.payload_ref.refs_0_.refs_9_), channel_id=1, source_target_pairs={{0,4},{4,8},{8,12},{12,16},{16,20},{20,24},{24,28},{28,0},{1,5},{5... | collective-permute-start | bytes 1597448 | tf_op jit(solution)/shard_map/ppermute | solution.py:22
  10.8 24.1 %all-to-all-start = ((bf16[8,528,128]{2,1,0:T(8,128)(2,1)}), bf16[8,528,128]{2,1,0:T(8,128)(2,1)S(1)}, u32[]{:S(2)}, u32[]{:S(2)}) async-start(bf16[8,528,128]{2,1,0:T(8,128)(2,1)} %shard_map.29), calls=%async_computation | async-start | bytes 2162688 | tf_op jit(solution)/shard_map/all_to_all | solution.py:293
  19.2 30.1 %copy-start.3 = (bf16[2,1040,128]{2,1,0:T(8,128)(2,1)}, bf16[2,1040,128]{2,1,0:T(8,128)(2,1)S(1)}, u32[]{:S(2)}) copy-start(bf16[2,1040,128]{2,1,0:T(8,128)(2,1)S(1)} %collective-permute-done.1.refs_2_.refs_11_) | copy-start | bytes 1597444
  19.2 22.9 %collective-permute-start.3 = (bf16[2,1040,128]{2,1,0:T(8,128)(2,1)S(1)}, bf16[2,1040,128]{2,1,0:T(8,128)(2,1)}, u32[]{:S(2)}, u32[]{:S(2)}) collective-permute-start(bf16[2,1040,128]{2,1,0:T(8,128)(2,1)S(1)} %collective-permute-done.1.refs_2_.refs_11_), channel_id=1, source_target_pairs={{0,28},{4,0},{8,4},{12,8},{16,12},{20,16},{24,20},{28,24},{1,29},{... | collective-permute-start | bytes 1597448 | tf_op jit(solution)/shard_map/ppermute | solution.py:22
  22.1 25.3 %collective-permute-start.2 = (bf16[2,1040,128]{2,1,0:T(8,128)(2,1)}, bf16[2,1040,128]{2,1,0:T(8,128)(2,1)}, u32[]{:S(2)}, u32[]{:S(2)}) collective-permute-start(bf16[2,1040,128]{2,1,0:T(8,128)(2,1)} %collective-permute-done.refs_1_.refs_10_), channel_id=1, source_target_pairs={{0,4},{4,8},{8,12},{12,16},{16,20},{20,24},{24,28},{28,0},{1,5},{5... | collective-permute-start | bytes 1597448 | tf_op jit(solution)/shard_map/ppermute | solution.py:22
  34.9 35.4 %collective-permute-start.8 = (bf16[4224,128]{1,0:T(8,128)(2,1)S(1)}, bf16[4224,128]{1,0:T(8,128)(2,1)S(1)}, u32[]{:S(2)}, u32[]{:S(2)}) collective-permute-start(bf16[4224,128]{1,0:T(8,128)(2,1)S(1)} %bitcast.15), channel_id=1, source_target_pairs={{0,64},{32,480},{64,128},{96,32},{128,192},{160,96},{192,256},{224... | collective-permute-start | bytes 3244040 | tf_op jit(solution)/shard_map/ppermute | solution.py:296
  42.1 11.8 %collective-permute-start.5 = (bf16[2,1040,128]{2,1,0:T(8,128)(2,1)}, bf16[2,1040,128]{2,1,0:T(8,128)(2,1)S(1)}, u32[]{:S(2)}, u32[]{:S(2)}) collective-permute-start(bf16[2,1040,128]{2,1,0:T(8,128)(2,1)} %collective-permute-done.3.refs_4_.refs_13_), channel_id=1, source_target_pairs={{0,28},{4,0},{8,4},{12,8},{16,12},{20,16},{24,20},{28,24},{1,29},{... | collective-permute-start | bytes 1597448 | tf_op jit(solution)/shard_map/ppermute | solution.py:22
  47.4 12.5 %collective-permute-start.4 = (bf16[2,1040,128]{2,1,0:T(8,128)(2,1)}, bf16[2,1040,128]{2,1,0:T(8,128)(2,1)S(1)}, u32[]{:S(2)}, u32[]{:S(2)}) collective-permute-start(bf16[2,1040,128]{2,1,0:T(8,128)(2,1)} %collective-permute-done.2.refs_3_.refs_12_), channel_id=1, source_target_pairs={{0,4},{4,8},{8,12},{12,16},{16,20},{20,24},{24,28},{28,0},{1,5},{5... | collective-permute-start | bytes 1597448 | tf_op jit(solution)/shard_map/ppermute | solution.py:22
  50.2 12.6 %collective-permute-start.9 = (bf16[2112,128]{1,0:T(8,128)(2,1)}, bf16[2112,128]{1,0:T(8,128)(2,1)S(1)}, u32[]{:S(2)}, u32[]{:S(2)}) collective-permute-start(bf16[2112,128]{1,0:T(8,128)(2,1)} %slice_select_fusion), channel_id=1, source_target_pairs={{0,448},{32,96},{64,0},{96,160},{128,64},{160,224},{192,128},{224,... | collective-permute-start | bytes 1622024 | tf_op jit(solution)/shard_map/ppermute | solution.py:299
  53.9 6.0 %copy-start.1 = (bf16[2,1040,128]{2,1,0:T(8,128)(2,1)}, bf16[2,1040,128]{2,1,0:T(8,128)(2,1)S(1)}, u32[]{:S(2)}) copy-start(bf16[2,1040,128]{2,1,0:T(8,128)(2,1)S(1)} %collective-permute-done.5.refs_6_.refs_15_) | copy-start | bytes 1597444
  54.6 9.8 %collective-permute-start.7 = (bf16[1040,128]{1,0:T(8,128)(2,1)}, bf16[1040,128]{1,0:T(8,128)(2,1)}, u32[]{:S(2)}, u32[]{:S(2)}) collective-permute-start(bf16[1040,128]{1,0:T(8,128)(2,1)} %slice_bitcast_fusion), channel_id=1, source_target_pairs={{0,28},{4,0},{8,4},{12,8},{16,12},{20,16},{24,20},{28,24},{1,29},{... | collective-permute-start | bytes 798728 | tf_op jit(solution)/shard_map/ppermute | solution.py:22
  59.9 0.9 copy-start.2
  60.8 9.5 %collective-permute-start.6 = (bf16[1040,128]{1,0:T(8,128)(2,1)}, bf16[1040,128]{1,0:T(8,128)(2,1)S(1)}, u32[]{:S(2)}, u32[]{:S(2)}) collective-permute-start(bf16[1040,128]{1,0:T(8,128)(2,1)} %slice_bitcast_fusion.1), channel_id=1, source_target_pairs={{0,4},{4,8},{8,12},{12,16},{16,20},{20,24},{24,28},{28,0},{1,5},{5... | collective-permute-start | bytes 798728 | tf_op jit(solution)/shard_map/ppermute | solution.py:22

commit v4 on v3

--- a/solution.py
+++ b/solution.py
@@ -9,7 +9,7 @@
 
 BS = 128
 TAIL = 16
-STEP = 4
+STEP = 8
 PART_ROWS = 16
 PANELS = 5
 SPAN = 4 * BS + TAIL
@@ -117,7 +117,7 @@
             top = jnp.max(jnp.max(jnp.abs(part), axis=0, keepdims=True), axis=1, keepdims=True)
             code = jnp.ceil(jnp.log2(jnp.maximum(top, TINY)) * 16.0)
             scaled = part * (jnp.exp2(code * (-1.0 / 16.0)) * QMAX)
-            coded = jnp.round(jnp.clip(scaled, -32767.0, 32767.0)).astype(jnp.int32)
+            coded = jnp.round(scaled).astype(jnp.int32)
             q_ref[slots[d], 0, at, :] = coded.astype(jnp.int16)
             codes[d].append(code)
     sub = lax.broadcasted_iota(jnp.int32, (TAIL, BS), 0)
@@ -169,7 +169,7 @@
         functools.partial(product_kernel, first, start, half_rows, classes, matrix_rows),
         grid_spec=grid_spec,
         out_shape=out_shape,
-        compiler_params=pltpu.CompilerParams(vmem_limit_bytes=12 * 2**20),
+        compiler_params=pltpu.CompilerParams(vmem_limit_bytes=20 * 2**20),
         cost_estimate=pl.CostEstimate(
             flops=2 * rows * 32 * BS**3, bytes_accessed=12 * 2**20, transcendentals=0
         ),

time: 112 us -> 110 us (0.982)
  Pallas kernels: 12.4 us -> 11.2 us
where the time goes in v4:
time: 110 us; the launch traced here: 109 us
  starting transfers between devices  44.8 us (41%)
  blocking collectives  28.5 us (26%)
  waiting for transfers between devices  19.7 us (18%)
  Pallas kernels  11.2 us (10%)
  local copies, waits for them, and re-layouts  3.43 us (3%)
    all_to_all x1, blocking collectives, shards(): parts.append((mine, lax.all_to_all(coded, 'depth', 0, 0)))  28.5 us
    ppermute x8, starting transfers between devices, passed_along(): lax.ppermute(block, axis, [(i, (i + distance) % n) for i in range(n)])  27.4 us
    all_to_all x1, waiting for transfers between devices, shards(): lax.all_to_all(pieces, ('row', 'depth'), 0, 0, axis_index_groups=groups)  10.4 us
    ppermute x8, waiting for transfers between devices, passed_along(): lax.ppermute(block, axis, [(i, (i + distance) % n) for i in range(n)])  9.33 us
    all_to_all x1, starting transfers between devices, shards(): lax.all_to_all(pieces, ('row', 'depth'), 0, 0, axis_index_groups=groups)  8.35 us
    pallas_call x1, Pallas kernels, products(): pl.pallas_call(functools.partial(product_kernel, first, start, half_rows,...  8.18 us
    ppermute x1, starting transfers between devices, shards(): lax.ppermute(pair, 'row', [(i, (i + (2 if i % 2 == 0 else -2)) % n_panels...  7.15 us
  transfers between devices with their start and end apart: 11, of which 4 were waited for; matrix products, arithmetic and copies ran while one was open for 2% of the time, Pallas kernels for 1%

profile of v4, /device:TPU:1, one launch (start us, length us, event | category | flops | bytes accessed | tf_op | source)
XLA Modules:
  0.0 108.8 jit_solution(14711148932873478401)
XLA Ops:
  0.0 0.7 copy.3.cols_ref
  0.7 1.0 copy-done
  1.8 0.1 shard_map.28.payload_ref.refs_0_.refs_9_
  1.9 5.9 %collective-permute-start.1 = (bf16[2,1040,128]{2,1,0:T(8,128)(2,1)S(1)}, bf16[2,1040,128]{2,1,0:T(8,128)(2,1)S(1)}, u32[]{:S(2)}, u32[]{:S(2)}) collective-permute-start(bf16[2,1040,128]{2,1,0:T(8,128)(2,1)S(1)} %shard_map.28.payload_ref.refs_0_.refs_9_), channel_id=1, source_target_pairs={{0,28},{4,0},{8,4},{12,8},{16,12},{20,16},{24,20},{28,24},{1,29},{... | collective-permute-start | bytes 1597448 | tf_op jit(solution)/shard_map/ppermute | solution.py:22
  7.8 1.9 %collective-permute-start = (bf16[2,1040,128]{2,1,0:T(8,128)(2,1)S(1)}, bf16[2,1040,128]{2,1,0:T(8,128)(2,1)}, u32[]{:S(2)}, u32[]{:S(2)}) collective-permute-start(bf16[2,1040,128]{2,1,0:T(8,128)(2,1)S(1)} %shard_map.28.payload_ref.refs_0_.refs_9_), channel_id=1, source_target_pairs={{0,4},{4,8},{8,12},{12,16},{16,20},{20,24},{24,28},{28,0},{1,5},{5... | collective-permute-start | bytes 1597448 | tf_op jit(solution)/shard_map/ppermute | solution.py:22
  9.7 1.1 %shard_map.29 = bf16[8,528,128]{2,1,0:T(8,128)(2,1)} custom-call(bf16[2,1040,128]{2,1,0:T(8,128)(2,1)S(1)} %shard_map.28.payload_ref.refs_0_.refs_9_), custom_call_target="tpu_custom_call" | custom-call | tf_op jit(solution)/shard_map/pallas_call | solution.py:264
  10.8 8.4 %all-to-all-start = ((bf16[8,528,128]{2,1,0:T(8,128)(2,1)}), bf16[8,528,128]{2,1,0:T(8,128)(2,1)S(1)}, u32[]{:S(2)}, u32[]{:S(2)}) async-start(bf16[8,528,128]{2,1,0:T(8,128)(2,1)} %shard_map.29), calls=%async_computation | async-start | bytes 2162688 | tf_op jit(solution)/shard_map/all_to_all | solution.py:293
  19.2 0.0 collective-permute-done.1.refs_2_.refs_11_
  19.2 2.9 %collective-permute-start.3 = (bf16[2,1040,128]{2,1,0:T(8,128)(2,1)S(1)}, bf16[2,1040,128]{2,1,0:T(8,128)(2,1)}, u32[]{:S(2)}, u32[]{:S(2)}) collective-permute-start(bf16[2,1040,128]{2,1,0:T(8,128)(2,1)S(1)} %collective-permute-done.1.refs_2_.refs_11_), channel_id=1, source_target_pairs={{0,28},{4,0},{8,4},{12,8},{16,12},{20,16},{24,20},{28,24},{1,29},{... | collective-permute-start | bytes 1597448 | tf_op jit(solution)/shard_map/ppermute | solution.py:22
  22.1 0.0 collective-permute-done.refs_1_.refs_10_
  22.1 2.4 %collective-permute-start.2 = (bf16[2,1040,128]{2,1,0:T(8,128)(2,1)}, bf16[2,1040,128]{2,1,0:T(8,128)(2,1)}, u32[]{:S(2)}, u32[]{:S(2)}) collective-permute-start(bf16[2,1040,128]{2,1,0:T(8,128)(2,1)} %collective-permute-done.refs_1_.refs_10_), channel_id=1, source_target_pairs={{0,4},{4,8},{8,12},{12,16},{16,20},{20,24},{24,28},{28,0},{1,5},{5... | collective-permute-start | bytes 1597448 | tf_op jit(solution)/shard_map/ppermute | solution.py:22
  24.5 10.4 %all-to-all-done = bf16[8,528,128]{2,1,0:T(8,128)(2,1)S(1)} async-done(((bf16[8,528,128]{2,1,0:T(8,128)(2,1)}), bf16[8,528,128]{2,1,0:T(8,128)(2,1)S(1)}, u32[]{:S(2)}, u32[]{:S(2)}) %all-to-all-start) | async-done | bytes 1081376 | tf_op jit(solution)/shard_map/all_to_all | solution.py:293
  34.9 7.2 %collective-permute-start.8 = (bf16[4224,128]{1,0:T(8,128)(2,1)S(1)}, bf16[4224,128]{1,0:T(8,128)(2,1)S(1)}, u32[]{:S(2)}, u32[]{:S(2)}) collective-permute-start(bf16[4224,128]{1,0:T(8,128)(2,1)S(1)} %bitcast.15), channel_id=1, source_target_pairs={{0,64},{32,480},{64,128},{96,32},{128,192},{160,96},{192,256},{224... | collective-permute-start | bytes 3244040 | tf_op jit(solution)/shard_map/ppermute | solution.py:296
  42.1 0.0 collective-permute-done.3.refs_4_.refs_13_
  42.1 5.3 %collective-permute-start.5 = (bf16[2,1040,128]{2,1,0:T(8,128)(2,1)}, bf16[2,1040,128]{2,1,0:T(8,128)(2,1)S(1)}, u32[]{:S(2)}, u32[]{:S(2)}) collective-permute-start(bf16[2,1040,128]{2,1,0:T(8,128)(2,1)} %collective-permute-done.3.refs_4_.refs_13_), channel_id=1, source_target_pairs={{0,28},{4,0},{8,4},{12,8},{16,12},{20,16},{24,20},{28,24},{1,29},{... | collective-permute-start | bytes 1597448 | tf_op jit(solution)/shard_map/ppermute | solution.py:22
  47.4 1.9 %collective-permute-start.4 = (bf16[2,1040,128]{2,1,0:T(8,128)(2,1)}, bf16[2,1040,128]{2,1,0:T(8,128)(2,1)S(1)}, u32[]{:S(2)}, u32[]{:S(2)}) collective-permute-start(bf16[2,1040,128]{2,1,0:T(8,128)(2,1)} %collective-permute-done.2.refs_3_.refs_12_), channel_id=1, source_target_pairs={{0,4},{4,8},{8,12},{12,16},{16,20},{20,24},{24,28},{28,0},{1,5},{5... | collective-permute-start | bytes 1597448 | tf_op jit(solution)/shard_map/ppermute | solution.py:22
  49.3 0.9 slice_select_fusion
  50.2 1.9 %collective-permute-start.9 = (bf16[2112,128]{1,0:T(8,128)(2,1)}, bf16[2112,128]{1,0:T(8,128)(2,1)S(1)}, u32[]{:S(2)}, u32[]{:S(2)}) collective-permute-start(bf16[2112,128]{1,0:T(8,128)(2,1)} %slice_select_fusion), channel_id=1, source_target_pairs={{0,448},{32,96},{64,0},{96,160},{128,64},{160,224},{192,128},{224,... | collective-permute-start | bytes 1622024 | tf_op jit(solution)/shard_map/ppermute | solution.py:299
  52.1 1.8 %collective-permute-done.5.refs_6_.refs_15_ = bf16[2,1040,128]{2,1,0:T(8,128)(2,1)S(1)} collective-permute-done((bf16[2,1040,128]{2,1,0:T(8,128)(2,1)}, bf16[2,1040,128]{2,1,0:T(8,128)(2,1)S(1)}, u32[]{:S(2)}, u32[]{:S(2)}) %collective-permute-start.5) | collective-permute-done | bytes 532512 | tf_op jit(solution)/shard_map/ppermute | solution.py:22
  53.9 0.8 slice_bitcast_fusion
  54.6 5.2 %collective-permute-start.7 = (bf16[1040,128]{1,0:T(8,128)(2,1)}, bf16[1040,128]{1,0:T(8,128)(2,1)}, u32[]{:S(2)}, u32[]{:S(2)}) collective-permute-start(bf16[1040,128]{1,0:T(8,128)(2,1)} %slice_bitcast_fusion), channel_id=1, source_target_pairs={{0,28},{4,0},{8,4},{12,8},{16,12},{20,16},{24,20},{28,24},{1,29},{... | collective-permute-start | bytes 798728 | tf_op jit(solution)/shard_map/ppermute | solution.py:22
  59.9 0.8 slice_bitcast_fusion.1
  60.6 0.1 copy-done.2
  60.8 1.9 %collective-permute-start.6 = (bf16[1040,128]{1,0:T(8,128)(2,1)}, bf16[1040,128]{1,0:T(8,128)(2,1)S(1)}, u32[]{:S(2)}, u32[]{:S(2)}) collective-permute-start(bf16[1040,128]{1,0:T(8,128)(2,1)} %slice_bitcast_fusion.1), channel_id=1, source_target_pairs={{0,4},{4,8},{8,12},{12,16},{16,20},{20,24},{24,28},{28,0},{1,5},{5... | collective-permute-start | bytes 798728 | tf_op jit(solution)/shard_map/ppermute | solution.py:22
  62.7 0.1 pad_add_fusion.here_ref
  62.8 0.0 collective-permute-done.9.refs_22_
  62.8 1.7 %collective-permute-done.7.refs_8_ = bf16[1040,128]{1,0:T(8,128)(2,1)} collective-permute-done((bf16[1040,128]{1,0:T(8,128)(2,1)}, bf16[1040,128]{1,0:T(8,128)(2,1)}, u32[]{:S(2)}, u32[]{:S(2)}) %collective-permute-start.7) | collective-permute-done | bytes 266272 | tf_op jit(solution)/shard_map/ppermute | solution.py:22
  64.5 5.9 %collective-permute-done.6.refs_7_.refs_16_ = bf16[1040,128]{1,0:T(8,128)(2,1)S(1)} collective-permute-done((bf16[1040,128]{1,0:T(8,128)(2,1)}, bf16[1040,128]{1,0:T(8,128)(2,1)S(1)}, u32[]{:S(2)}, u32[]{:S(2)}) %collective-permute-start.6) | collective-permute-done | bytes 266272 | tf_op jit(solution)/shard_map/ppermute | solution.py:22
  70.3 0.0 collective-permute-done.8.refs_21_
  70.3 8.2 %shard_map.30 = (s16[4,2,1040,128]{3,2,1,0:T(8,128)(2,1)S(1)}, f32[2048,128]{1,0:T(8,128)S(1)}, s32[32,128]{1,0:T(8,128)}) custom-call(s32[3]{0:T(128)S(1)} %pad_add_fusion.here_ref, bf16[2,1040,128]{2,1,0:T(8,128)(2,1)S(1)} %shard_map.28.payload_ref.refs_0_.refs_9_, bf16[2,1040,128]{2,1,0:T(8,128)(2,1)} %collective-permute-done.refs_1_.refs_10_, ...), custom_call_target="tpu_custom_call" | custom-call | flops 2147483648 | bytes 12582912 | tf_op jit(solution)/shard_map/pallas_call | solution.py:168
  78.5 28.5 %all_to_all.10.refs_1_.refs_2_.refs_3_ = s16[4,2,1040,128]{3,2,1,0:T(8,128)(2,1)S(1)} all-to-all(s16[4,2,1040,128]{3,2,1,0:T(8,128)(2,1)S(1)} %get-tuple-element.10), channel_id=1, replica_groups=mesh['row'=16,'col'=8,'depth'=4] {'depth'}, dimensions={0} | all-to-all | bytes 4259840 | tf_op jit(solution)/shard_map/all_to_all | solution.py:309
  107.0 1.8 %shard_map.31 = bf16[2048,128]{1,0:T(8,128)(2,1)} custom-call(s32[3]{0:T(128)S(1)} %pad_add_fusion.here_ref, f32[2048,128]{1,0:T(8,128)S(1)} %get-tuple-element.9.refs_0_, s16[4,2,1040,128]{3,2,1,0:T(8,128)(2,1)S(1)} %all_to_all.10.refs_1_.refs_2_.refs_3_, s16[4,2,1040,128]{3,2,1,0:T(8,128)(2,1)S(1)} %all_to_all.10.refs_1_.refs_2_.refs_3_, ...), custom_call_target="tpu_custom_call" | custom-call | tf_op jit(solution)/shard_map/pallas_call | solution.py:221
  (8 shorter events, 0.0 us)
Async XLA Ops:
  0.7 1.0 copy-start
  1.9 17.3 %collective-permute-start.1 = (bf16[2,1040,128]{2,1,0:T(8,128)(2,1)S(1)}, bf16[2,1040,128]{2,1,0:T(8,128)(2,1)S(1)}, u32[]{:S(2)}, u32[]{:S(2)}) collective-permute-start(bf16[2,1040,128]{2,1,0:T(8,128)(2,1)S(1)} %shard_map.28.payload_ref.refs_0_.refs_9_), channel_id=1, source_target_pairs={{0,28},{4,0},{8,4},{12,8},{16,12},{20,16},{24,20},{28,24},{1,29},{... | collective-permute-start | bytes 1597448 | tf_op jit(solution)/shard_map/ppermute | solution.py:22
  7.8 14.3 %collective-permute-start = (bf16[2,1040,128]{2,1,0:T(8,128)(2,1)S(1)}, bf16[2,1040,128]{2,1,0:T(8,128)(2,1)}, u32[]{:S(2)}, u32[]{:S(2)}) collective-permute-start(bf16[2,1040,128]{2,1,0:T(8,128)(2,1)S(1)} %shard_map.28.payload_ref.refs_0_.refs_9_), channel_id=1, source_target_pairs={{0,4},{4,8},{8,12},{12,16},{16,20},{20,24},{24,28},{28,0},{1,5},{5... | collective-permute-start | bytes 1597448 | tf_op jit(solution)/shard_map/ppermute | solution.py:22
  10.8 24.1 %all-to-all-start = ((bf16[8,528,128]{2,1,0:T(8,128)(2,1)}), bf16[8,528,128]{2,1,0:T(8,128)(2,1)S(1)}, u32[]{:S(2)}, u32[]{:S(2)}) async-start(bf16[8,528,128]{2,1,0:T(8,128)(2,1)} %shard_map.29), calls=%async_computation | async-start | bytes 2162688 | tf_op jit(solution)/shard_map/all_to_all | solution.py:293
  19.2 30.1 %copy-start.3 = (bf16[2,1040,128]{2,1,0:T(8,128)(2,1)}, bf16[2,1040,128]{2,1,0:T(8,128)(2,1)S(1)}, u32[]{:S(2)}) copy-start(bf16[2,1040,128]{2,1,0:T(8,128)(2,1)S(1)} %collective-permute-done.1.refs_2_.refs_11_) | copy-start | bytes 1597444
  19.2 22.9 %collective-permute-start.3 = (bf16[2,1040,128]{2,1,0:T(8,128)(2,1)S(1)}, bf16[2,1040,128]{2,1,0:T(8,128)(2,1)}, u32[]{:S(2)}, u32[]{:S(2)}) collective-permute-start(bf16[2,1040,128]{2,1,0:T(8,128)(2,1)S(1)} %collective-permute-done.1.refs_2_.refs_11_), channel_id=1, source_target_pairs={{0,28},{4,0},{8,4},{12,8},{16,12},{20,16},{24,20},{28,24},{1,29},{... | collective-permute-start | bytes 1597448 | tf_op jit(solution)/shard_map/ppermute | solution.py:22
  22.1 25.3 %collective-permute-start.2 = (bf16[2,1040,128]{2,1,0:T(8,128)(2,1)}, bf16[2,1040,128]{2,1,0:T(8,128)(2,1)}, u32[]{:S(2)}, u32[]{:S(2)}) collective-permute-start(bf16[2,1040,128]{2,1,0:T(8,128)(2,1)} %collective-permute-done.refs_1_.refs_10_), channel_id=1, source_target_pairs={{0,4},{4,8},{8,12},{12,16},{16,20},{20,24},{24,28},{28,0},{1,5},{5... | collective-permute-start | bytes 1597448 | tf_op jit(solution)/shard_map/ppermute | solution.py:22
  34.9 35.4 %collective-permute-start.8 = (bf16[4224,128]{1,0:T(8,128)(2,1)S(1)}, bf16[4224,128]{1,0:T(8,128)(2,1)S(1)}, u32[]{:S(2)}, u32[]{:S(2)}) collective-permute-start(bf16[4224,128]{1,0:T(8,128)(2,1)S(1)} %bitcast.15), channel_id=1, source_target_pairs={{0,64},{32,480},{64,128},{96,32},{128,192},{160,96},{192,256},{224... | collective-permute-start | bytes 3244040 | tf_op jit(solution)/shard_map/ppermute | solution.py:296
  42.1 11.8 %collective-permute-start.5 = (bf16[2,1040,128]{2,1,0:T(8,128)(2,1)}, bf16[2,1040,128]{2,1,0:T(8,128)(2,1)S(1)}, u32[]{:S(2)}, u32[]{:S(2)}) collective-permute-start(bf16[2,1040,128]{2,1,0:T(8,128)(2,1)} %collective-permute-done.3.refs_4_.refs_13_), channel_id=1, source_target_pairs={{0,28},{4,0},{8,4},{12,8},{16,12},{20,16},{24,20},{28,24},{1,29},{... | collective-permute-start | bytes 1597448 | tf_op jit(solution)/shard_map/ppermute | solution.py:22
  47.4 12.5 %collective-permute-start.4 = (bf16[2,1040,128]{2,1,0:T(8,128)(2,1)}, bf16[2,1040,128]{2,1,0:T(8,128)(2,1)S(1)}, u32[]{:S(2)}, u32[]{:S(2)}) collective-permute-start(bf16[2,1040,128]{2,1,0:T(8,128)(2,1)} %collective-permute-done.2.refs_3_.refs_12_), channel_id=1, source_target_pairs={{0,4},{4,8},{8,12},{12,16},{16,20},{20,24},{24,28},{28,0},{1,5},{5... | collective-permute-start | bytes 1597448 | tf_op jit(solution)/shard_map/ppermute | solution.py:22
  50.2 12.6 %collective-permute-start.9 = (bf16[2112,128]{1,0:T(8,128)(2,1)}, bf16[2112,128]{1,0:T(8,128)(2,1)S(1)}, u32[]{:S(2)}, u32[]{:S(2)}) collective-permute-start(bf16[2112,128]{1,0:T(8,128)(2,1)} %slice_select_fusion), channel_id=1, source_target_pairs={{0,448},{32,96},{64,0},{96,160},{128,64},{160,224},{192,128},{224,... | collective-permute-start | bytes 1622024 | tf_op jit(solution)/shard_map/ppermute | solution.py:299
  53.9 6.0 %copy-start.1 = (bf16[2,1040,128]{2,1,0:T(8,128)(2,1)}, bf16[2,1040,128]{2,1,0:T(8,128)(2,1)S(1)}, u32[]{:S(2)}) copy-start(bf16[2,1040,128]{2,1,0:T(8,128)(2,1)S(1)} %collective-permute-done.5.refs_6_.refs_15_) | copy-start | bytes 1597444
  54.6 9.8 %collective-permute-start.7 = (bf16[1040,128]{1,0:T(8,128)(2,1)}, bf16[1040,128]{1,0:T(8,128)(2,1)}, u32[]{:S(2)}, u32[]{:S(2)}) collective-permute-start(bf16[1040,128]{1,0:T(8,128)(2,1)} %slice_bitcast_fusion), channel_id=1, source_target_pairs={{0,28},{4,0},{8,4},{12,8},{16,12},{20,16},{24,20},{28,24},{1,29},{... | collective-permute-start | bytes 798728 | tf_op jit(solution)/shard_map/ppermute | solution.py:22
  59.9 0.9 copy-start.2
  60.8 9.5 %collective-permute-start.6 = (bf16[1040,128]{1,0:T(8,128)(2,1)}, bf16[1040,128]{1,0:T(8,128)(2,1)S(1)}, u32[]{:S(2)}, u32[]{:S(2)}) collective-permute-start(bf16[1040,128]{1,0:T(8,128)(2,1)} %slice_bitcast_fusion.1), channel_id=1, source_target_pairs={{0,4},{4,8},{8,12},{12,16},{16,20},{20,24},{24,28},{28,0},{1,5},{5... | collective-permute-start | bytes 798728 | tf_op jit(solution)/shard_map/ppermute | solution.py:22

commit v5 on v4

--- a/solution.py
+++ b/solution.py
@@ -226,22 +226,28 @@
     )(here, *operands)
 
 
-def own_payload_kernel(half_rows, cols_ref, blocks_ref, out_ref):
-    shape = (cols_ref.shape[0], BS)
-    own_lane = lax.broadcasted_iota(jnp.int32, shape, 0) == lax.broadcasted_iota(jnp.int32, shape, 1)
-    numbers = jnp.broadcast_to(cols_ref[...], shape).astype(jnp.float32)
-    line = jnp.sum(jnp.where(own_lane, numbers, 0.0), axis=0, keepdims=True)
-    tail = jnp.broadcast_to(line, (TAIL, BS)).astype(jnp.bfloat16)
+def own_payload_kernel(half_rows, cols_ref, blocks_ref, out_ref, sems):
     span = half_rows * BS
+    copies = []
     for half in range(2):
-        out_ref[half, pl.ds(0, span), :] = blocks_ref[pl.ds(half * span, span), :]
-        out_ref[half, pl.ds(span, TAIL), :] = tail
+        source, target = blocks_ref.at[pl.ds(half * span, span)], out_ref.at[half, pl.ds(0, span)]
+        copies.append(pltpu.make_async_copy(source, target, sems.at[half]))
+        copies[-1].start()
+    rows = cols_ref.shape[1]
+    numbers = jnp.broadcast_to(cols_ref[...].astype(jnp.float32), (TAIL, rows)).astype(jnp.bfloat16)
+    for half in range(2):
+        out_ref[half, pl.ds(span, TAIL), :] = jnp.zeros((TAIL, BS), jnp.bfloat16)
+        out_ref[half, pl.ds(span, TAIL), pl.ds(0, rows)] = numbers
+    for copy in copies:
+        copy.wait()
 
 
 def own_payload(blocks, cols, half_rows):
     return pl.pallas_call(
         functools.partial(own_payload_kernel, half_rows),
+        in_specs=[pl.BlockSpec(memory_space=pltpu.VMEM), pl.BlockSpec(memory_space=pl.ANY)],
         out_shape=jax.ShapeDtypeStruct((2, half_rows * BS + TAIL, BS), jnp.bfloat16),
+        scratch_shapes=[pltpu.SemaphoreType.DMA((2,))],
         compiler_params=pltpu.CompilerParams(vmem_limit_bytes=8 * 2**20),
     )(cols, blocks)
 
@@ -277,7 +283,8 @@
     core = lax.rem(r, 2)
     here = jnp.stack([lax.axis_index("depth"), core, (r - PANELS // 2) * rows]).astype(jnp.int32)
 
-    own = own_payload(p_blocks.reshape(rows * BS, BS), p_cols, rows // 2)
+    blocks = pltpu.with_memory_space_constraint(p_blocks.reshape(rows * BS, BS), pltpu.HBM)
+    own = own_payload(blocks, p_cols.reshape(1, rows), rows // 2)
     down = up = own
     left = [own]
     for hop in range(3):

time: 110 us -> 110 us (level)
  local copies, waits for them, and re-layouts: 3.43 us -> 2.31 us
    unnamed x9 -> x8, local copies, waits for them, and re-layouts: 1.91 us -> 0.79 us
where the time goes in v5:
time: 110 us; the launch traced here: 109 us
  starting transfers between devices  44.8 us (41%)
  blocking collectives  28.5 us (26%)
  waiting for transfers between devices  19.7 us (18%)
  Pallas kernels  12.2 us (11%)
  local copies, waits for them, and re-layouts  2.31 us (2%)
    all_to_all x1, blocking collectives, shards(): parts.append((mine, lax.all_to_all(coded, 'depth', 0, 0)))  28.5 us
    ppermute x8, starting transfers between devices, passed_along(): lax.ppermute(block, axis, [(i, (i + distance) % n) for i in range(n)])  27.4 us
    all_to_all x1, waiting for transfers between devices, shards(): lax.all_to_all(pieces, ('row', 'depth'), 0, 0, axis_index_groups=groups)  10.4 us
    ppermute x8, waiting for transfers between devices, passed_along(): lax.ppermute(block, axis, [(i, (i + distance) % n) for i in range(n)])  9.33 us
    all_to_all x1, starting transfers between devices, shards(): lax.all_to_all(pieces, ('row', 'depth'), 0, 0, axis_index_groups=groups)  8.35 us
    pallas_call x1, Pallas kernels, products(): pl.pallas_call(functools.partial(product_kernel, first, start, half_rows,...  8.19 us
    ppermute x1, starting transfers between devices, shards(): lax.ppermute(pair, 'row', [(i, (i + (2 if i % 2 == 0 else -2)) % n_panels...  7.15 us
  transfers between devices with their start and end apart: 11, of which 4 were waited for; matrix products, arithmetic and copies ran while one was open for 2% of the time, Pallas kernels for 1%

profile of v5, /device:TPU:1, one launch (start us, length us, event | category | flops | bytes accessed | tf_op | source)
XLA Modules:
  0.0 108.7 jit_solution(3797806897170399987)
XLA Ops:
  0.0 0.7 copy-done
  0.7 1.0 shard_map.28.payload_ref.refs_0_.refs_9_
  1.7 5.9 %collective-permute-start.1 = (bf16[2,1040,128]{2,1,0:T(8,128)(2,1)S(1)}, bf16[2,1040,128]{2,1,0:T(8,128)(2,1)S(1)}, u32[]{:S(2)}, u32[]{:S(2)}) collective-permute-start(bf16[2,1040,128]{2,1,0:T(8,128)(2,1)S(1)} %shard_map.28.payload_ref.refs_0_.refs_9_), channel_id=1, source_target_pairs={{0,28},{4,0},{8,4},{12,8},{16,12},{20,16},{24,20},{28,24},{1,29},{... | collective-permute-start | bytes 1597448 | tf_op jit(solution)/shard_map/ppermute | solution.py:22
  7.6 1.9 %collective-permute-start = (bf16[2,1040,128]{2,1,0:T(8,128)(2,1)S(1)}, bf16[2,1040,128]{2,1,0:T(8,128)(2,1)}, u32[]{:S(2)}, u32[]{:S(2)}) collective-permute-start(bf16[2,1040,128]{2,1,0:T(8,128)(2,1)S(1)} %shard_map.28.payload_ref.refs_0_.refs_9_), channel_id=1, source_target_pairs={{0,4},{4,8},{8,12},{12,16},{16,20},{20,24},{24,28},{28,0},{1,5},{5... | collective-permute-start | bytes 1597448 | tf_op jit(solution)/shard_map/ppermute | solution.py:22
  9.6 1.1 %shard_map.29 = bf16[8,528,128]{2,1,0:T(8,128)(2,1)} custom-call(bf16[2,1040,128]{2,1,0:T(8,128)(2,1)S(1)} %shard_map.28.payload_ref.refs_0_.refs_9_), custom_call_target="tpu_custom_call" | custom-call | tf_op jit(solution)/shard_map/pallas_call | solution.py:270
  10.7 8.4 %all-to-all-start = ((bf16[8,528,128]{2,1,0:T(8,128)(2,1)}), bf16[8,528,128]{2,1,0:T(8,128)(2,1)S(1)}, u32[]{:S(2)}, u32[]{:S(2)}) async-start(bf16[8,528,128]{2,1,0:T(8,128)(2,1)} %shard_map.29), calls=%async_computation | async-start | bytes 2162688 | tf_op jit(solution)/shard_map/all_to_all | solution.py:300
  19.1 0.0 collective-permute-done.1.refs_2_.refs_11_
  19.1 2.9 %collective-permute-start.3 = (bf16[2,1040,128]{2,1,0:T(8,128)(2,1)S(1)}, bf16[2,1040,128]{2,1,0:T(8,128)(2,1)}, u32[]{:S(2)}, u32[]{:S(2)}) collective-permute-start(bf16[2,1040,128]{2,1,0:T(8,128)(2,1)S(1)} %collective-permute-done.1.refs_2_.refs_11_), channel_id=1, source_target_pairs={{0,28},{4,0},{8,4},{12,8},{16,12},{20,16},{24,20},{28,24},{1,29},{... | collective-permute-start | bytes 1597448 | tf_op jit(solution)/shard_map/ppermute | solution.py:22
  21.9 0.0 collective-permute-done.refs_1_.refs_10_
  21.9 2.4 %collective-permute-start.2 = (bf16[2,1040,128]{2,1,0:T(8,128)(2,1)}, bf16[2,1040,128]{2,1,0:T(8,128)(2,1)}, u32[]{:S(2)}, u32[]{:S(2)}) collective-permute-start(bf16[2,1040,128]{2,1,0:T(8,128)(2,1)} %collective-permute-done.refs_1_.refs_10_), channel_id=1, source_target_pairs={{0,4},{4,8},{8,12},{12,16},{16,20},{20,24},{24,28},{28,0},{1,5},{5... | collective-permute-start | bytes 1597448 | tf_op jit(solution)/shard_map/ppermute | solution.py:22
  24.4 10.4 %all-to-all-done = bf16[8,528,128]{2,1,0:T(8,128)(2,1)S(1)} async-done(((bf16[8,528,128]{2,1,0:T(8,128)(2,1)}), bf16[8,528,128]{2,1,0:T(8,128)(2,1)S(1)}, u32[]{:S(2)}, u32[]{:S(2)}) %all-to-all-start) | async-done | bytes 1081376 | tf_op jit(solution)/shard_map/all_to_all | solution.py:300
  34.8 7.2 %collective-permute-start.8 = (bf16[4224,128]{1,0:T(8,128)(2,1)S(1)}, bf16[4224,128]{1,0:T(8,128)(2,1)S(1)}, u32[]{:S(2)}, u32[]{:S(2)}) collective-permute-start(bf16[4224,128]{1,0:T(8,128)(2,1)S(1)} %bitcast.16), channel_id=1, source_target_pairs={{0,64},{32,480},{64,128},{96,32},{128,192},{160,96},{192,256},{224... | collective-permute-start | bytes 3244040 | tf_op jit(solution)/shard_map/ppermute | solution.py:303
  42.0 0.0 collective-permute-done.3.refs_4_.refs_13_
  42.0 5.3 %collective-permute-start.5 = (bf16[2,1040,128]{2,1,0:T(8,128)(2,1)}, bf16[2,1040,128]{2,1,0:T(8,128)(2,1)S(1)}, u32[]{:S(2)}, u32[]{:S(2)}) collective-permute-start(bf16[2,1040,128]{2,1,0:T(8,128)(2,1)} %collective-permute-done.3.refs_4_.refs_13_), channel_id=1, source_target_pairs={{0,28},{4,0},{8,4},{12,8},{16,12},{20,16},{24,20},{28,24},{1,29},{... | collective-permute-start | bytes 1597448 | tf_op jit(solution)/shard_map/ppermute | solution.py:22
  47.2 0.0 collective-permute-done.2.refs_3_.refs_12_
  47.2 1.9 %collective-permute-start.4 = (bf16[2,1040,128]{2,1,0:T(8,128)(2,1)}, bf16[2,1040,128]{2,1,0:T(8,128)(2,1)S(1)}, u32[]{:S(2)}, u32[]{:S(2)}) collective-permute-start(bf16[2,1040,128]{2,1,0:T(8,128)(2,1)} %collective-permute-done.2.refs_3_.refs_12_), channel_id=1, source_target_pairs={{0,4},{4,8},{8,12},{12,16},{16,20},{20,24},{24,28},{28,0},{1,5},{5... | collective-permute-start | bytes 1597448 | tf_op jit(solution)/shard_map/ppermute | solution.py:22
  49.2 0.9 slice_select_fusion
  50.0 1.9 %collective-permute-start.9 = (bf16[2112,128]{1,0:T(8,128)(2,1)}, bf16[2112,128]{1,0:T(8,128)(2,1)S(1)}, u32[]{:S(2)}, u32[]{:S(2)}) collective-permute-start(bf16[2112,128]{1,0:T(8,128)(2,1)} %slice_select_fusion), channel_id=1, source_target_pairs={{0,448},{32,96},{64,0},{96,160},{128,64},{160,224},{192,128},{224,... | collective-permute-start | bytes 1622024 | tf_op jit(solution)/shard_map/ppermute | solution.py:306
  52.0 1.8 %collective-permute-done.5.refs_6_.refs_15_ = bf16[2,1040,128]{2,1,0:T(8,128)(2,1)S(1)} collective-permute-done((bf16[2,1040,128]{2,1,0:T(8,128)(2,1)}, bf16[2,1040,128]{2,1,0:T(8,128)(2,1)S(1)}, u32[]{:S(2)}, u32[]{:S(2)}) %collective-permute-start.5) | collective-permute-done | bytes 532512 | tf_op jit(solution)/shard_map/ppermute | solution.py:22
  53.7 0.8 slice_bitcast_fusion
  54.5 5.2 %collective-permute-start.7 = (bf16[1040,128]{1,0:T(8,128)(2,1)}, bf16[1040,128]{1,0:T(8,128)(2,1)}, u32[]{:S(2)}, u32[]{:S(2)}) collective-permute-start(bf16[1040,128]{1,0:T(8,128)(2,1)} %slice_bitcast_fusion), channel_id=1, source_target_pairs={{0,28},{4,0},{8,4},{12,8},{16,12},{20,16},{24,20},{28,24},{1,29},{... | collective-permute-start | bytes 798728 | tf_op jit(solution)/shard_map/ppermute | solution.py:22
  59.7 0.0 collective-permute-done.4.refs_5_.refs_14_
  59.7 0.8 slice_bitcast_fusion.1
  60.5 0.1 copy-done.2
  60.6 1.9 %collective-permute-start.6 = (bf16[1040,128]{1,0:T(8,128)(2,1)}, bf16[1040,128]{1,0:T(8,128)(2,1)S(1)}, u32[]{:S(2)}, u32[]{:S(2)}) collective-permute-start(bf16[1040,128]{1,0:T(8,128)(2,1)} %slice_bitcast_fusion.1), channel_id=1, source_target_pairs={{0,4},{4,8},{8,12},{12,16},{16,20},{20,24},{24,28},{28,0},{1,5},{5... | collective-permute-start | bytes 798728 | tf_op jit(solution)/shard_map/ppermute | solution.py:22
  62.6 0.1 pad_add_fusion.here_ref
  62.6 0.0 collective-permute-done.9.refs_22_
  62.6 1.7 %collective-permute-done.7.refs_8_ = bf16[1040,128]{1,0:T(8,128)(2,1)} collective-permute-done((bf16[1040,128]{1,0:T(8,128)(2,1)}, bf16[1040,128]{1,0:T(8,128)(2,1)}, u32[]{:S(2)}, u32[]{:S(2)}) %collective-permute-start.7) | collective-permute-done | bytes 266272 | tf_op jit(solution)/shard_map/ppermute | solution.py:22
  64.3 5.9 %collective-permute-done.6.refs_7_.refs_16_ = bf16[1040,128]{1,0:T(8,128)(2,1)S(1)} collective-permute-done((bf16[1040,128]{1,0:T(8,128)(2,1)}, bf16[1040,128]{1,0:T(8,128)(2,1)S(1)}, u32[]{:S(2)}, u32[]{:S(2)}) %collective-permute-start.6) | collective-permute-done | bytes 266272 | tf_op jit(solution)/shard_map/ppermute | solution.py:22
  70.2 8.2 %shard_map.30 = (s16[4,2,1040,128]{3,2,1,0:T(8,128)(2,1)S(1)}, f32[2048,128]{1,0:T(8,128)S(1)}, s32[32,128]{1,0:T(8,128)}) custom-call(s32[3]{0:T(128)S(1)} %pad_add_fusion.here_ref, bf16[2,1040,128]{2,1,0:T(8,128)(2,1)S(1)} %shard_map.28.payload_ref.refs_0_.refs_9_, bf16[2,1040,128]{2,1,0:T(8,128)(2,1)} %collective-permute-done.refs_1_.refs_10_, ...), custom_call_target="tpu_custom_call" | custom-call | flops 2147483648 | bytes 12582912 | tf_op jit(solution)/shard_map/pallas_call | solution.py:168
  78.4 28.5 %all_to_all.10.refs_1_.refs_2_.refs_3_ = s16[4,2,1040,128]{3,2,1,0:T(8,128)(2,1)S(1)} all-to-all(s16[4,2,1040,128]{3,2,1,0:T(8,128)(2,1)S(1)} %get-tuple-element.10), channel_id=1, replica_groups=mesh['row'=16,'col'=8,'depth'=4] {'depth'}, dimensions={0} | all-to-all | bytes 4259840 | tf_op jit(solution)/shard_map/all_to_all | solution.py:316
  106.9 1.8 %shard_map.31 = bf16[2048,128]{1,0:T(8,128)(2,1)} custom-call(s32[3]{0:T(128)S(1)} %pad_add_fusion.here_ref, f32[2048,128]{1,0:T(8,128)S(1)} %get-tuple-element.9.refs_0_, s16[4,2,1040,128]{3,2,1,0:T(8,128)(2,1)S(1)} %all_to_all.10.refs_1_.refs_2_.refs_3_, s16[4,2,1040,128]{3,2,1,0:T(8,128)(2,1)S(1)} %all_to_all.10.refs_1_.refs_2_.refs_3_, ...), custom_call_target="tpu_custom_call" | custom-call | tf_op jit(solution)/shard_map/pallas_call | solution.py:221
  (7 shorter events, 0.0 us)
Async XLA Ops:
  0.0 0.7 copy-start
  1.7 17.4 %collective-permute-start.1 = (bf16[2,1040,128]{2,1,0:T(8,128)(2,1)S(1)}, bf16[2,1040,128]{2,1,0:T(8,128)(2,1)S(1)}, u32[]{:S(2)}, u32[]{:S(2)}) collective-permute-start(bf16[2,1040,128]{2,1,0:T(8,128)(2,1)S(1)} %shard_map.28.payload_ref.refs_0_.refs_9_), channel_id=1, source_target_pairs={{0,28},{4,0},{8,4},{12,8},{16,12},{20,16},{24,20},{28,24},{1,29},{... | collective-permute-start | bytes 1597448 | tf_op jit(solution)/shard_map/ppermute | solution.py:22
  7.6 14.3 %collective-permute-start = (bf16[2,1040,128]{2,1,0:T(8,128)(2,1)S(1)}, bf16[2,1040,128]{2,1,0:T(8,128)(2,1)}, u32[]{:S(2)}, u32[]{:S(2)}) collective-permute-start(bf16[2,1040,128]{2,1,0:T(8,128)(2,1)S(1)} %shard_map.28.payload_ref.refs_0_.refs_9_), channel_id=1, source_target_pairs={{0,4},{4,8},{8,12},{12,16},{16,20},{20,24},{24,28},{28,0},{1,5},{5... | collective-permute-start | bytes 1597448 | tf_op jit(solution)/shard_map/ppermute | solution.py:22
  10.7 24.1 %all-to-all-start = ((bf16[8,528,128]{2,1,0:T(8,128)(2,1)}), bf16[8,528,128]{2,1,0:T(8,128)(2,1)S(1)}, u32[]{:S(2)}, u32[]{:S(2)}) async-start(bf16[8,528,128]{2,1,0:T(8,128)(2,1)} %shard_map.29), calls=%async_computation | async-start | bytes 2162688 | tf_op jit(solution)/shard_map/all_to_all | solution.py:300
  19.1 30.1 %copy-start.3 = (bf16[2,1040,128]{2,1,0:T(8,128)(2,1)}, bf16[2,1040,128]{2,1,0:T(8,128)(2,1)S(1)}, u32[]{:S(2)}) copy-start(bf16[2,1040,128]{2,1,0:T(8,128)(2,1)S(1)} %collective-permute-done.1.refs_2_.refs_11_) | copy-start | bytes 1597444
  19.1 22.9 %collective-permute-start.3 = (bf16[2,1040,128]{2,1,0:T(8,128)(2,1)S(1)}, bf16[2,1040,128]{2,1,0:T(8,128)(2,1)}, u32[]{:S(2)}, u32[]{:S(2)}) collective-permute-start(bf16[2,1040,128]{2,1,0:T(8,128)(2,1)S(1)} %collective-permute-done.1.refs_2_.refs_11_), channel_id=1, source_target_pairs={{0,28},{4,0},{8,4},{12,8},{16,12},{20,16},{24,20},{28,24},{1,29},{... | collective-permute-start | bytes 1597448 | tf_op jit(solution)/shard_map/ppermute | solution.py:22
  21.9 25.3 %collective-permute-start.2 = (bf16[2,1040,128]{2,1,0:T(8,128)(2,1)}, bf16[2,1040,128]{2,1,0:T(8,128)(2,1)}, u32[]{:S(2)}, u32[]{:S(2)}) collective-permute-start(bf16[2,1040,128]{2,1,0:T(8,128)(2,1)} %collective-permute-done.refs_1_.refs_10_), channel_id=1, source_target_pairs={{0,4},{4,8},{8,12},{12,16},{16,20},{20,24},{24,28},{28,0},{1,5},{5... | collective-permute-start | bytes 1597448 | tf_op jit(solution)/shard_map/ppermute | solution.py:22
  34.8 35.4 %collective-permute-start.8 = (bf16[4224,128]{1,0:T(8,128)(2,1)S(1)}, bf16[4224,128]{1,0:T(8,128)(2,1)S(1)}, u32[]{:S(2)}, u32[]{:S(2)}) collective-permute-start(bf16[4224,128]{1,0:T(8,128)(2,1)S(1)} %bitcast.16), channel_id=1, source_target_pairs={{0,64},{32,480},{64,128},{96,32},{128,192},{160,96},{192,256},{224... | collective-permute-start | bytes 3244040 | tf_op jit(solution)/shard_map/ppermute | solution.py:303
  42.0 11.8 %collective-permute-start.5 = (bf16[2,1040,128]{2,1,0:T(8,128)(2,1)}, bf16[2,1040,128]{2,1,0:T(8,128)(2,1)S(1)}, u32[]{:S(2)}, u32[]{:S(2)}) collective-permute-start(bf16[2,1040,128]{2,1,0:T(8,128)(2,1)} %collective-permute-done.3.refs_4_.refs_13_), channel_id=1, source_target_pairs={{0,28},{4,0},{8,4},{12,8},{16,12},{20,16},{24,20},{28,24},{1,29},{... | collective-permute-start | bytes 1597448 | tf_op jit(solution)/shard_map/ppermute | solution.py:22
  47.2 12.5 %collective-permute-start.4 = (bf16[2,1040,128]{2,1,0:T(8,128)(2,1)}, bf16[2,1040,128]{2,1,0:T(8,128)(2,1)S(1)}, u32[]{:S(2)}, u32[]{:S(2)}) collective-permute-start(bf16[2,1040,128]{2,1,0:T(8,128)(2,1)} %collective-permute-done.2.refs_3_.refs_12_), channel_id=1, source_target_pairs={{0,4},{4,8},{8,12},{12,16},{16,20},{20,24},{24,28},{28,0},{1,5},{5... | collective-permute-start | bytes 1597448 | tf_op jit(solution)/shard_map/ppermute | solution.py:22
  50.0 12.6 %collective-permute-start.9 = (bf16[2112,128]{1,0:T(8,128)(2,1)}, bf16[2112,128]{1,0:T(8,128)(2,1)S(1)}, u32[]{:S(2)}, u32[]{:S(2)}) collective-permute-start(bf16[2112,128]{1,0:T(8,128)(2,1)} %slice_select_fusion), channel_id=1, source_target_pairs={{0,448},{32,96},{64,0},{96,160},{128,64},{160,224},{192,128},{224,... | collective-permute-start | bytes 1622024 | tf_op jit(solution)/shard_map/ppermute | solution.py:306
  53.7 6.0 %copy-start.1 = (bf16[2,1040,128]{2,1,0:T(8,128)(2,1)}, bf16[2,1040,128]{2,1,0:T(8,128)(2,1)S(1)}, u32[]{:S(2)}) copy-start(bf16[2,1040,128]{2,1,0:T(8,128)(2,1)S(1)} %collective-permute-done.5.refs_6_.refs_15_) | copy-start | bytes 1597444
  54.5 9.8 %collective-permute-start.7 = (bf16[1040,128]{1,0:T(8,128)(2,1)}, bf16[1040,128]{1,0:T(8,128)(2,1)}, u32[]{:S(2)}, u32[]{:S(2)}) collective-permute-start(bf16[1040,128]{1,0:T(8,128)(2,1)} %slice_bitcast_fusion), channel_id=1, source_target_pairs={{0,28},{4,0},{8,4},{12,8},{16,12},{20,16},{24,20},{28,24},{1,29},{... | collective-permute-start | bytes 798728 | tf_op jit(solution)/shard_map/ppermute | solution.py:22
  59.7 0.9 copy-start.2
  60.6 9.5 %collective-permute-start.6 = (bf16[1040,128]{1,0:T(8,128)(2,1)}, bf16[1040,128]{1,0:T(8,128)(2,1)S(1)}, u32[]{:S(2)}, u32[]{:S(2)}) collective-permute-start(bf16[1040,128]{1,0:T(8,128)(2,1)} %slice_bitcast_fusion.1), channel_id=1, source_target_pairs={{0,4},{4,8},{8,12},{12,16},{16,20},{20,24},{24,28},{28,0},{1,5},{5... | collective-permute-start | bytes 798728 | tf_op jit(solution)/shard_map/ppermute | solution.py:22

commit v6 on v5

--- a/solution.py
+++ b/solution.py
@@ -226,15 +226,18 @@
     )(here, *operands)
 
 
-def own_payload_kernel(half_rows, cols_ref, blocks_ref, out_ref, sems):
+def own_payload_kernel(half_rows, cols_ref, blocks_ref, out_ref, line_ref, sems):
     span = half_rows * BS
+    cols_copy = pltpu.make_async_copy(cols_ref, line_ref, sems.at[2])
+    cols_copy.start()
     copies = []
     for half in range(2):
         source, target = blocks_ref.at[pl.ds(half * span, span)], out_ref.at[half, pl.ds(0, span)]
         copies.append(pltpu.make_async_copy(source, target, sems.at[half]))
         copies[-1].start()
     rows = cols_ref.shape[1]
-    numbers = jnp.broadcast_to(cols_ref[...].astype(jnp.float32), (TAIL, rows)).astype(jnp.bfloat16)
+    cols_copy.wait()
+    numbers = jnp.broadcast_to(line_ref[...].astype(jnp.float32), (TAIL, rows)).astype(jnp.bfloat16)
     for half in range(2):
         out_ref[half, pl.ds(span, TAIL), :] = jnp.zeros((TAIL, BS), jnp.bfloat16)
         out_ref[half, pl.ds(span, TAIL), pl.ds(0, rows)] = numbers
@@ -245,9 +248,9 @@
 def own_payload(blocks, cols, half_rows):
     return pl.pallas_call(
         functools.partial(own_payload_kernel, half_rows),
-        in_specs=[pl.BlockSpec(memory_space=pltpu.VMEM), pl.BlockSpec(memory_space=pl.ANY)],
+        in_specs=[pl.BlockSpec(memory_space=pl.ANY)] * 2,
         out_shape=jax.ShapeDtypeStruct((2, half_rows * BS + TAIL, BS), jnp.bfloat16),
-        scratch_shapes=[pltpu.SemaphoreType.DMA((2,))],
+        scratch_shapes=[pltpu.VMEM(cols.shape, cols.dtype), pltpu.SemaphoreType.DMA((3,))],
         compiler_params=pltpu.CompilerParams(vmem_limit_bytes=8 * 2**20),
     )(cols, blocks)
 
@@ -284,7 +287,8 @@
     here = jnp.stack([lax.axis_index("depth"), core, (r - PANELS // 2) * rows]).astype(jnp.int32)
 
     blocks = pltpu.with_memory_space_constraint(p_blocks.reshape(rows * BS, BS), pltpu.HBM)
-    own = own_payload(blocks, p_cols.reshape(1, rows), rows // 2)
+    cols = pltpu.with_memory_space_constraint(p_cols.reshape(1, rows), pltpu.HBM)
+    own = own_payload(blocks, cols, rows // 2)
     down = up = own
     left = [own]
     for hop in range(3):

time: 110 us -> 109 us (level)
  no operation moved by 1% of the time
where the time goes in v6:
time: 109 us; the launch traced here: 108 us
  starting transfers between devices  44.8 us (41%)
  blocking collectives  28.4 us (26%)
  waiting for transfers between devices  19.8 us (18%)
  Pallas kernels  12.2 us (11%)
  local copies, waits for them, and re-layouts  1.67 us (2%)
    all_to_all x1, blocking collectives, shards(): parts.append((mine, lax.all_to_all(coded, 'depth', 0, 0)))  28.4 us
    ppermute x8, starting transfers between devices, passed_along(): lax.ppermute(block, axis, [(i, (i + distance) % n) for i in range(n)])  27.4 us
    all_to_all x1, waiting for transfers between devices, shards(): lax.all_to_all(pieces, ('row', 'depth'), 0, 0, axis_index_groups=groups)  10.4 us
    ppermute x8, waiting for transfers between devices, passed_along(): lax.ppermute(block, axis, [(i, (i + distance) % n) for i in range(n)])  9.35 us
    all_to_all x1, starting transfers between devices, shards(): lax.all_to_all(pieces, ('row', 'depth'), 0, 0, axis_index_groups=groups)  8.35 us
    pallas_call x1, Pallas kernels, products(): pl.pallas_call(functools.partial(product_kernel, first, start, half_rows,...  8.19 us
    ppermute x1, starting transfers between devices, shards(): lax.ppermute(pair, 'row', [(i, (i + (2 if i % 2 == 0 else -2)) % n_panels...  7.15 us
  transfers between devices with their start and end apart: 11, of which 4 were waited for; matrix products, arithmetic and copies ran while one was open for 2% of the time, Pallas kernels for 1%

profile of v6, /device:TPU:1, one launch (start us, length us, event | category | flops | bytes accessed | tf_op | source)
XLA Modules:
  0.0 108.0 jit_solution(17556846125630226301)
XLA Ops:
  0.0 1.1 shard_map.28.payload_ref.refs_0_.refs_9_
  1.1 5.9 %collective-permute-start.1 = (bf16[2,1040,128]{2,1,0:T(8,128)(2,1)S(1)}, bf16[2,1040,128]{2,1,0:T(8,128)(2,1)S(1)}, u32[]{:S(2)}, u32[]{:S(2)}) collective-permute-start(bf16[2,1040,128]{2,1,0:T(8,128)(2,1)S(1)} %shard_map.28.payload_ref.refs_0_.refs_9_), channel_id=1, source_target_pairs={{0,28},{4,0},{8,4},{12,8},{16,12},{20,16},{24,20},{28,24},{1,29},{... | collective-permute-start | bytes 1597448 | tf_op jit(solution)/shard_map/ppermute | solution.py:22
  7.0 1.9 %collective-permute-start = (bf16[2,1040,128]{2,1,0:T(8,128)(2,1)S(1)}, bf16[2,1040,128]{2,1,0:T(8,128)(2,1)}, u32[]{:S(2)}, u32[]{:S(2)}) collective-permute-start(bf16[2,1040,128]{2,1,0:T(8,128)(2,1)S(1)} %shard_map.28.payload_ref.refs_0_.refs_9_), channel_id=1, source_target_pairs={{0,4},{4,8},{8,12},{12,16},{16,20},{20,24},{24,28},{28,0},{1,5},{5... | collective-permute-start | bytes 1597448 | tf_op jit(solution)/shard_map/ppermute | solution.py:22
  8.9 1.1 %shard_map.29 = bf16[8,528,128]{2,1,0:T(8,128)(2,1)} custom-call(bf16[2,1040,128]{2,1,0:T(8,128)(2,1)S(1)} %shard_map.28.payload_ref.refs_0_.refs_9_), custom_call_target="tpu_custom_call" | custom-call | tf_op jit(solution)/shard_map/pallas_call | solution.py:273
  10.1 8.4 %all-to-all-start = ((bf16[8,528,128]{2,1,0:T(8,128)(2,1)}), bf16[8,528,128]{2,1,0:T(8,128)(2,1)S(1)}, u32[]{:S(2)}, u32[]{:S(2)}) async-start(bf16[8,528,128]{2,1,0:T(8,128)(2,1)} %shard_map.29), calls=%async_computation | async-start | bytes 2162688 | tf_op jit(solution)/shard_map/all_to_all | solution.py:304
  18.4 0.0 collective-permute-done.1.refs_2_.refs_11_
  18.4 2.9 %collective-permute-start.3 = (bf16[2,1040,128]{2,1,0:T(8,128)(2,1)S(1)}, bf16[2,1040,128]{2,1,0:T(8,128)(2,1)}, u32[]{:S(2)}, u32[]{:S(2)}) collective-permute-start(bf16[2,1040,128]{2,1,0:T(8,128)(2,1)S(1)} %collective-permute-done.1.refs_2_.refs_11_), channel_id=1, source_target_pairs={{0,28},{4,0},{8,4},{12,8},{16,12},{20,16},{24,20},{28,24},{1,29},{... | collective-permute-start | bytes 1597448 | tf_op jit(solution)/shard_map/ppermute | solution.py:22
  21.3 0.0 collective-permute-done.refs_1_.refs_10_
  21.3 2.4 %collective-permute-start.2 = (bf16[2,1040,128]{2,1,0:T(8,128)(2,1)}, bf16[2,1040,128]{2,1,0:T(8,128)(2,1)}, u32[]{:S(2)}, u32[]{:S(2)}) collective-permute-start(bf16[2,1040,128]{2,1,0:T(8,128)(2,1)} %collective-permute-done.refs_1_.refs_10_), channel_id=1, source_target_pairs={{0,4},{4,8},{8,12},{12,16},{16,20},{20,24},{24,28},{28,0},{1,5},{5... | collective-permute-start | bytes 1597448 | tf_op jit(solution)/shard_map/ppermute | solution.py:22
  23.8 10.4 %all-to-all-done = bf16[8,528,128]{2,1,0:T(8,128)(2,1)S(1)} async-done(((bf16[8,528,128]{2,1,0:T(8,128)(2,1)}), bf16[8,528,128]{2,1,0:T(8,128)(2,1)S(1)}, u32[]{:S(2)}, u32[]{:S(2)}) %all-to-all-start) | async-done | bytes 1081376 | tf_op jit(solution)/shard_map/all_to_all | solution.py:304
  34.2 7.2 %collective-permute-start.8 = (bf16[4224,128]{1,0:T(8,128)(2,1)S(1)}, bf16[4224,128]{1,0:T(8,128)(2,1)S(1)}, u32[]{:S(2)}, u32[]{:S(2)}) collective-permute-start(bf16[4224,128]{1,0:T(8,128)(2,1)S(1)} %bitcast.16), channel_id=1, source_target_pairs={{0,64},{32,480},{64,128},{96,32},{128,192},{160,96},{192,256},{224... | collective-permute-start | bytes 3244040 | tf_op jit(solution)/shard_map/ppermute | solution.py:307
  41.3 0.0 collective-permute-done.3.refs_4_.refs_13_
  41.3 5.3 %collective-permute-start.5 = (bf16[2,1040,128]{2,1,0:T(8,128)(2,1)}, bf16[2,1040,128]{2,1,0:T(8,128)(2,1)S(1)}, u32[]{:S(2)}, u32[]{:S(2)}) collective-permute-start(bf16[2,1040,128]{2,1,0:T(8,128)(2,1)} %collective-permute-done.3.refs_4_.refs_13_), channel_id=1, source_target_pairs={{0,28},{4,0},{8,4},{12,8},{16,12},{20,16},{24,20},{28,24},{1,29},{... | collective-permute-start | bytes 1597448 | tf_op jit(solution)/shard_map/ppermute | solution.py:22
  46.6 0.0 collective-permute-done.2.refs_3_.refs_12_
  46.6 1.9 %collective-permute-start.4 = (bf16[2,1040,128]{2,1,0:T(8,128)(2,1)}, bf16[2,1040,128]{2,1,0:T(8,128)(2,1)S(1)}, u32[]{:S(2)}, u32[]{:S(2)}) collective-permute-start(bf16[2,1040,128]{2,1,0:T(8,128)(2,1)} %collective-permute-done.2.refs_3_.refs_12_), channel_id=1, source_target_pairs={{0,4},{4,8},{8,12},{12,16},{16,20},{20,24},{24,28},{28,0},{1,5},{5... | collective-permute-start | bytes 1597448 | tf_op jit(solution)/shard_map/ppermute | solution.py:22
  48.6 0.9 slice_select_fusion
  49.4 1.9 %collective-permute-start.9 = (bf16[2112,128]{1,0:T(8,128)(2,1)}, bf16[2112,128]{1,0:T(8,128)(2,1)S(1)}, u32[]{:S(2)}, u32[]{:S(2)}) collective-permute-start(bf16[2112,128]{1,0:T(8,128)(2,1)} %slice_select_fusion), channel_id=1, source_target_pairs={{0,448},{32,96},{64,0},{96,160},{128,64},{160,224},{192,128},{224,... | collective-permute-start | bytes 1622024 | tf_op jit(solution)/shard_map/ppermute | solution.py:310
  51.3 1.8 %collective-permute-done.5.refs_6_.refs_15_ = bf16[2,1040,128]{2,1,0:T(8,128)(2,1)S(1)} collective-permute-done((bf16[2,1040,128]{2,1,0:T(8,128)(2,1)}, bf16[2,1040,128]{2,1,0:T(8,128)(2,1)S(1)}, u32[]{:S(2)}, u32[]{:S(2)}) %collective-permute-start.5) | collective-permute-done | bytes 532512 | tf_op jit(solution)/shard_map/ppermute | solution.py:22
  53.1 0.8 slice_bitcast_fusion
  53.9 5.2 %collective-permute-start.7 = (bf16[1040,128]{1,0:T(8,128)(2,1)}, bf16[1040,128]{1,0:T(8,128)(2,1)}, u32[]{:S(2)}, u32[]{:S(2)}) collective-permute-start(bf16[1040,128]{1,0:T(8,128)(2,1)} %slice_bitcast_fusion), channel_id=1, source_target_pairs={{0,28},{4,0},{8,4},{12,8},{16,12},{20,16},{24,20},{28,24},{1,29},{... | collective-permute-start | bytes 798728 | tf_op jit(solution)/shard_map/ppermute | solution.py:22
  59.1 0.0 collective-permute-done.4.refs_5_.refs_14_
  59.1 0.8 slice_bitcast_fusion.1
  59.9 0.1 copy-done.1
  60.0 1.9 %collective-permute-start.6 = (bf16[1040,128]{1,0:T(8,128)(2,1)}, bf16[1040,128]{1,0:T(8,128)(2,1)S(1)}, u32[]{:S(2)}, u32[]{:S(2)}) collective-permute-start(bf16[1040,128]{1,0:T(8,128)(2,1)} %slice_bitcast_fusion.1), channel_id=1, source_target_pairs={{0,4},{4,8},{8,12},{12,16},{16,20},{20,24},{24,28},{28,0},{1,5},{5... | collective-permute-start | bytes 798728 | tf_op jit(solution)/shard_map/ppermute | solution.py:22
  61.9 0.1 pad_add_fusion.here_ref
  62.0 0.0 collective-permute-done.9.refs_22_
  62.0 1.7 %collective-permute-done.7.refs_8_ = bf16[1040,128]{1,0:T(8,128)(2,1)} collective-permute-done((bf16[1040,128]{1,0:T(8,128)(2,1)}, bf16[1040,128]{1,0:T(8,128)(2,1)}, u32[]{:S(2)}, u32[]{:S(2)}) %collective-permute-start.7) | collective-permute-done | bytes 266272 | tf_op jit(solution)/shard_map/ppermute | solution.py:22
  63.7 5.8 %collective-permute-done.6.refs_7_.refs_16_ = bf16[1040,128]{1,0:T(8,128)(2,1)S(1)} collective-permute-done((bf16[1040,128]{1,0:T(8,128)(2,1)}, bf16[1040,128]{1,0:T(8,128)(2,1)S(1)}, u32[]{:S(2)}, u32[]{:S(2)}) %collective-permute-start.6) | collective-permute-done | bytes 266272 | tf_op jit(solution)/shard_map/ppermute | solution.py:22
  69.6 0.0 collective-permute-done.8.refs_21_
  69.6 8.2 %shard_map.30 = (s16[4,2,1040,128]{3,2,1,0:T(8,128)(2,1)S(1)}, f32[2048,128]{1,0:T(8,128)S(1)}, s32[32,128]{1,0:T(8,128)}) custom-call(s32[3]{0:T(128)S(1)} %pad_add_fusion.here_ref, bf16[2,1040,128]{2,1,0:T(8,128)(2,1)S(1)} %shard_map.28.payload_ref.refs_0_.refs_9_, bf16[2,1040,128]{2,1,0:T(8,128)(2,1)} %collective-permute-done.refs_1_.refs_10_, ...), custom_call_target="tpu_custom_call" | custom-call | flops 2147483648 | bytes 12582912 | tf_op jit(solution)/shard_map/pallas_call | solution.py:168
  77.8 28.4 %all_to_all.10.refs_1_.refs_2_.refs_3_ = s16[4,2,1040,128]{3,2,1,0:T(8,128)(2,1)S(1)} all-to-all(s16[4,2,1040,128]{3,2,1,0:T(8,128)(2,1)S(1)} %get-tuple-element.10), channel_id=1, replica_groups=mesh['row'=16,'col'=8,'depth'=4] {'depth'}, dimensions={0} | all-to-all | bytes 4259840 | tf_op jit(solution)/shard_map/all_to_all | solution.py:320
  106.2 1.8 %shard_map.31 = bf16[2048,128]{1,0:T(8,128)(2,1)} custom-call(s32[3]{0:T(128)S(1)} %pad_add_fusion.here_ref, f32[2048,128]{1,0:T(8,128)S(1)} %get-tuple-element.9.refs_0_, s16[4,2,1040,128]{3,2,1,0:T(8,128)(2,1)S(1)} %all_to_all.10.refs_1_.refs_2_.refs_3_, s16[4,2,1040,128]{3,2,1,0:T(8,128)(2,1)S(1)} %all_to_all.10.refs_1_.refs_2_.refs_3_, ...), custom_call_target="tpu_custom_call" | custom-call | tf_op jit(solution)/shard_map/pallas_call | solution.py:221
  (5 shorter events, 0.0 us)
Async XLA Ops:
  1.1 17.4 %collective-permute-start.1 = (bf16[2,1040,128]{2,1,0:T(8,128)(2,1)S(1)}, bf16[2,1040,128]{2,1,0:T(8,128)(2,1)S(1)}, u32[]{:S(2)}, u32[]{:S(2)}) collective-permute-start(bf16[2,1040,128]{2,1,0:T(8,128)(2,1)S(1)} %shard_map.28.payload_ref.refs_0_.refs_9_), channel_id=1, source_target_pairs={{0,28},{4,0},{8,4},{12,8},{16,12},{20,16},{24,20},{28,24},{1,29},{... | collective-permute-start | bytes 1597448 | tf_op jit(solution)/shard_map/ppermute | solution.py:22
  7.0 14.3 %collective-permute-start = (bf16[2,1040,128]{2,1,0:T(8,128)(2,1)S(1)}, bf16[2,1040,128]{2,1,0:T(8,128)(2,1)}, u32[]{:S(2)}, u32[]{:S(2)}) collective-permute-start(bf16[2,1040,128]{2,1,0:T(8,128)(2,1)S(1)} %shard_map.28.payload_ref.refs_0_.refs_9_), channel_id=1, source_target_pairs={{0,4},{4,8},{8,12},{12,16},{16,20},{20,24},{24,28},{28,0},{1,5},{5... | collective-permute-start | bytes 1597448 | tf_op jit(solution)/shard_map/ppermute | solution.py:22
  10.1 24.1 %all-to-all-start = ((bf16[8,528,128]{2,1,0:T(8,128)(2,1)}), bf16[8,528,128]{2,1,0:T(8,128)(2,1)S(1)}, u32[]{:S(2)}, u32[]{:S(2)}) async-start(bf16[8,528,128]{2,1,0:T(8,128)(2,1)} %shard_map.29), calls=%async_computation | async-start | bytes 2162688 | tf_op jit(solution)/shard_map/all_to_all | solution.py:304
  18.4 30.1 %copy-start.2 = (bf16[2,1040,128]{2,1,0:T(8,128)(2,1)}, bf16[2,1040,128]{2,1,0:T(8,128)(2,1)S(1)}, u32[]{:S(2)}) copy-start(bf16[2,1040,128]{2,1,0:T(8,128)(2,1)S(1)} %collective-permute-done.1.refs_2_.refs_11_) | copy-start | bytes 1597444
  18.4 22.9 %collective-permute-start.3 = (bf16[2,1040,128]{2,1,0:T(8,128)(2,1)S(1)}, bf16[2,1040,128]{2,1,0:T(8,128)(2,1)}, u32[]{:S(2)}, u32[]{:S(2)}) collective-permute-start(bf16[2,1040,128]{2,1,0:T(8,128)(2,1)S(1)} %collective-permute-done.1.refs_2_.refs_11_), channel_id=1, source_target_pairs={{0,28},{4,0},{8,4},{12,8},{16,12},{20,16},{24,20},{28,24},{1,29},{... | collective-permute-start | bytes 1597448 | tf_op jit(solution)/shard_map/ppermute | solution.py:22
  21.3 25.3 %collective-permute-start.2 = (bf16[2,1040,128]{2,1,0:T(8,128)(2,1)}, bf16[2,1040,128]{2,1,0:T(8,128)(2,1)}, u32[]{:S(2)}, u32[]{:S(2)}) collective-permute-start(bf16[2,1040,128]{2,1,0:T(8,128)(2,1)} %collective-permute-done.refs_1_.refs_10_), channel_id=1, source_target_pairs={{0,4},{4,8},{8,12},{12,16},{16,20},{20,24},{24,28},{28,0},{1,5},{5... | collective-permute-start | bytes 1597448 | tf_op jit(solution)/shard_map/ppermute | solution.py:22
  34.2 35.4 %collective-permute-start.8 = (bf16[4224,128]{1,0:T(8,128)(2,1)S(1)}, bf16[4224,128]{1,0:T(8,128)(2,1)S(1)}, u32[]{:S(2)}, u32[]{:S(2)}) collective-permute-start(bf16[4224,128]{1,0:T(8,128)(2,1)S(1)} %bitcast.16), channel_id=1, source_target_pairs={{0,64},{32,480},{64,128},{96,32},{128,192},{160,96},{192,256},{224... | collective-permute-start | bytes 3244040 | tf_op jit(solution)/shard_map/ppermute | solution.py:307
  41.3 11.8 %collective-permute-start.5 = (bf16[2,1040,128]{2,1,0:T(8,128)(2,1)}, bf16[2,1040,128]{2,1,0:T(8,128)(2,1)S(1)}, u32[]{:S(2)}, u32[]{:S(2)}) collective-permute-start(bf16[2,1040,128]{2,1,0:T(8,128)(2,1)} %collective-permute-done.3.refs_4_.refs_13_), channel_id=1, source_target_pairs={{0,28},{4,0},{8,4},{12,8},{16,12},{20,16},{24,20},{28,24},{1,29},{... | collective-permute-start | bytes 1597448 | tf_op jit(solution)/shard_map/ppermute | solution.py:22
  46.6 12.5 %collective-permute-start.4 = (bf16[2,1040,128]{2,1,0:T(8,128)(2,1)}, bf16[2,1040,128]{2,1,0:T(8,128)(2,1)S(1)}, u32[]{:S(2)}, u32[]{:S(2)}) collective-permute-start(bf16[2,1040,128]{2,1,0:T(8,128)(2,1)} %collective-permute-done.2.refs_3_.refs_12_), channel_id=1, source_target_pairs={{0,4},{4,8},{8,12},{12,16},{16,20},{20,24},{24,28},{28,0},{1,5},{5... | collective-permute-start | bytes 1597448 | tf_op jit(solution)/shard_map/ppermute | solution.py:22
  49.4 12.6 %collective-permute-start.9 = (bf16[2112,128]{1,0:T(8,128)(2,1)}, bf16[2112,128]{1,0:T(8,128)(2,1)S(1)}, u32[]{:S(2)}, u32[]{:S(2)}) collective-permute-start(bf16[2112,128]{1,0:T(8,128)(2,1)} %slice_select_fusion), channel_id=1, source_target_pairs={{0,448},{32,96},{64,0},{96,160},{128,64},{160,224},{192,128},{224,... | collective-permute-start | bytes 1622024 | tf_op jit(solution)/shard_map/ppermute | solution.py:310
  53.1 6.0 %copy-start = (bf16[2,1040,128]{2,1,0:T(8,128)(2,1)}, bf16[2,1040,128]{2,1,0:T(8,128)(2,1)S(1)}, u32[]{:S(2)}) copy-start(bf16[2,1040,128]{2,1,0:T(8,128)(2,1)S(1)} %collective-permute-done.5.refs_6_.refs_15_) | copy-start | bytes 1597444
  53.9 9.8 %collective-permute-start.7 = (bf16[1040,128]{1,0:T(8,128)(2,1)}, bf16[1040,128]{1,0:T(8,128)(2,1)}, u32[]{:S(2)}, u32[]{:S(2)}) collective-permute-start(bf16[1040,128]{1,0:T(8,128)(2,1)} %slice_bitcast_fusion), channel_id=1, source_target_pairs={{0,28},{4,0},{8,4},{12,8},{16,12},{20,16},{24,20},{28,24},{1,29},{... | collective-permute-start | bytes 798728 | tf_op jit(solution)/shard_map/ppermute | solution.py:22
  59.1 0.9 copy-start.1
  60.0 9.6 %collective-permute-start.6 = (bf16[1040,128]{1,0:T(8,128)(2,1)}, bf16[1040,128]{1,0:T(8,128)(2,1)S(1)}, u32[]{:S(2)}, u32[]{:S(2)}) collective-permute-start(bf16[1040,128]{1,0:T(8,128)(2,1)} %slice_bitcast_fusion.1), channel_id=1, source_target_pairs={{0,4},{4,8},{8,12},{12,16},{16,20},{20,24},{24,28},{28,0},{1,5},{5... | collective-permute-start | bytes 798728 | tf_op jit(solution)/shard_map/ppermute | solution.py:22

commit v7 on v6

--- a/solution.py
+++ b/solution.py
@@ -77,7 +77,7 @@
         for n, (source, p, count) in enumerate(pieces):
             at = pl.ds(pl.multiple_of(p * panel, TAIL), count * panel)
             copies.append(pltpu.make_async_copy(source, held.at[at], sems.at[11 + n]))
-        for copy in tail_copies + copies:
+        for copy in copies + tail_copies:
             copy.start()
         held[pl.ds(zero_at, BS), :] = jnp.zeros((BS, BS), held.dtype)
         for copy in tail_copies:

time: 109 us -> 110 us (level)
  no operation moved by 1% of the time
where the time goes in v7:
time: 110 us; the launch traced here: 108 us
  starting transfers between devices  44.8 us (41%)
  blocking collectives  28.4 us (26%)
  waiting for transfers between devices  19.8 us (18%)
  Pallas kernels  12.4 us (11%)
  local copies, waits for them, and re-layouts  1.67 us (2%)
    all_to_all x1, blocking collectives, shards(): parts.append((mine, lax.all_to_all(coded, 'depth', 0, 0)))  28.4 us
    ppermute x8, starting transfers between devices, passed_along(): lax.ppermute(block, axis, [(i, (i + distance) % n) for i in range(n)])  27.4 us
    all_to_all x1, waiting for transfers between devices, shards(): lax.all_to_all(pieces, ('row', 'depth'), 0, 0, axis_index_groups=groups)  10.4 us
    ppermute x8, waiting for transfers between devices, passed_along(): lax.ppermute(block, axis, [(i, (i + distance) % n) for i in range(n)])  9.35 us
    pallas_call x1, Pallas kernels, products(): pl.pallas_call(functools.partial(product_kernel, first, start, half_rows,...  8.43 us
    all_to_all x1, starting transfers between devices, shards(): lax.all_to_all(pieces, ('row', 'depth'), 0, 0, axis_index_groups=groups)  8.35 us
    ppermute x1, starting transfers between devices, shards(): lax.ppermute(pair, 'row', [(i, (i + (2 if i % 2 == 0 else -2)) % n_panels...  7.15 us
  transfers between devices with their start and end apart: 11, of which 4 were waited for; matrix products, arithmetic and copies ran while one was open for 2% of the time, Pallas kernels for 1%

profile of v7, /device:TPU:1, one launch (start us, length us, event | category | flops | bytes accessed | tf_op | source)
XLA Modules:
  0.0 108.2 jit_solution(13005561363174160359)
XLA Ops:
  0.0 1.1 shard_map.28.payload_ref.refs_0_.refs_9_
  1.1 5.9 %collective-permute-start.1 = (bf16[2,1040,128]{2,1,0:T(8,128)(2,1)S(1)}, bf16[2,1040,128]{2,1,0:T(8,128)(2,1)S(1)}, u32[]{:S(2)}, u32[]{:S(2)}) collective-permute-start(bf16[2,1040,128]{2,1,0:T(8,128)(2,1)S(1)} %shard_map.28.payload_ref.refs_0_.refs_9_), channel_id=1, source_target_pairs={{0,28},{4,0},{8,4},{12,8},{16,12},{20,16},{24,20},{28,24},{1,29},{... | collective-permute-start | bytes 1597448 | tf_op jit(solution)/shard_map/ppermute | solution.py:22
  7.0 1.9 %collective-permute-start = (bf16[2,1040,128]{2,1,0:T(8,128)(2,1)S(1)}, bf16[2,1040,128]{2,1,0:T(8,128)(2,1)}, u32[]{:S(2)}, u32[]{:S(2)}) collective-permute-start(bf16[2,1040,128]{2,1,0:T(8,128)(2,1)S(1)} %shard_map.28.payload_ref.refs_0_.refs_9_), channel_id=1, source_target_pairs={{0,4},{4,8},{8,12},{12,16},{16,20},{20,24},{24,28},{28,0},{1,5},{5... | collective-permute-start | bytes 1597448 | tf_op jit(solution)/shard_map/ppermute | solution.py:22
  8.9 1.1 %shard_map.29 = bf16[8,528,128]{2,1,0:T(8,128)(2,1)} custom-call(bf16[2,1040,128]{2,1,0:T(8,128)(2,1)S(1)} %shard_map.28.payload_ref.refs_0_.refs_9_), custom_call_target="tpu_custom_call" | custom-call | tf_op jit(solution)/shard_map/pallas_call | solution.py:273
  10.1 8.4 %all-to-all-start = ((bf16[8,528,128]{2,1,0:T(8,128)(2,1)}), bf16[8,528,128]{2,1,0:T(8,128)(2,1)S(1)}, u32[]{:S(2)}, u32[]{:S(2)}) async-start(bf16[8,528,128]{2,1,0:T(8,128)(2,1)} %shard_map.29), calls=%async_computation | async-start | bytes 2162688 | tf_op jit(solution)/shard_map/all_to_all | solution.py:304
  18.4 0.0 collective-permute-done.1.refs_2_.refs_11_
  18.4 2.9 %collective-permute-start.3 = (bf16[2,1040,128]{2,1,0:T(8,128)(2,1)S(1)}, bf16[2,1040,128]{2,1,0:T(8,128)(2,1)}, u32[]{:S(2)}, u32[]{:S(2)}) collective-permute-start(bf16[2,1040,128]{2,1,0:T(8,128)(2,1)S(1)} %collective-permute-done.1.refs_2_.refs_11_), channel_id=1, source_target_pairs={{0,28},{4,0},{8,4},{12,8},{16,12},{20,16},{24,20},{28,24},{1,29},{... | collective-permute-start | bytes 1597448 | tf_op jit(solution)/shard_map/ppermute | solution.py:22
  21.3 0.0 collective-permute-done.refs_1_.refs_10_
  21.3 2.4 %collective-permute-start.2 = (bf16[2,1040,128]{2,1,0:T(8,128)(2,1)}, bf16[2,1040,128]{2,1,0:T(8,128)(2,1)}, u32[]{:S(2)}, u32[]{:S(2)}) collective-permute-start(bf16[2,1040,128]{2,1,0:T(8,128)(2,1)} %collective-permute-done.refs_1_.refs_10_), channel_id=1, source_target_pairs={{0,4},{4,8},{8,12},{12,16},{16,20},{20,24},{24,28},{28,0},{1,5},{5... | collective-permute-start | bytes 1597448 | tf_op jit(solution)/shard_map/ppermute | solution.py:22
  23.8 10.4 %all-to-all-done = bf16[8,528,128]{2,1,0:T(8,128)(2,1)S(1)} async-done(((bf16[8,528,128]{2,1,0:T(8,128)(2,1)}), bf16[8,528,128]{2,1,0:T(8,128)(2,1)S(1)}, u32[]{:S(2)}, u32[]{:S(2)}) %all-to-all-start) | async-done | bytes 1081376 | tf_op jit(solution)/shard_map/all_to_all | solution.py:304
  34.2 7.2 %collective-permute-start.8 = (bf16[4224,128]{1,0:T(8,128)(2,1)S(1)}, bf16[4224,128]{1,0:T(8,128)(2,1)S(1)}, u32[]{:S(2)}, u32[]{:S(2)}) collective-permute-start(bf16[4224,128]{1,0:T(8,128)(2,1)S(1)} %bitcast.16), channel_id=1, source_target_pairs={{0,64},{32,480},{64,128},{96,32},{128,192},{160,96},{192,256},{224... | collective-permute-start | bytes 3244040 | tf_op jit(solution)/shard_map/ppermute | solution.py:307
  41.3 0.0 collective-permute-done.3.refs_4_.refs_13_
  41.3 5.3 %collective-permute-start.5 = (bf16[2,1040,128]{2,1,0:T(8,128)(2,1)}, bf16[2,1040,128]{2,1,0:T(8,128)(2,1)S(1)}, u32[]{:S(2)}, u32[]{:S(2)}) collective-permute-start(bf16[2,1040,128]{2,1,0:T(8,128)(2,1)} %collective-permute-done.3.refs_4_.refs_13_), channel_id=1, source_target_pairs={{0,28},{4,0},{8,4},{12,8},{16,12},{20,16},{24,20},{28,24},{1,29},{... | collective-permute-start | bytes 1597448 | tf_op jit(solution)/shard_map/ppermute | solution.py:22
  46.6 0.0 collective-permute-done.2.refs_3_.refs_12_
  46.6 1.9 %collective-permute-start.4 = (bf16[2,1040,128]{2,1,0:T(8,128)(2,1)}, bf16[2,1040,128]{2,1,0:T(8,128)(2,1)S(1)}, u32[]{:S(2)}, u32[]{:S(2)}) collective-permute-start(bf16[2,1040,128]{2,1,0:T(8,128)(2,1)} %collective-permute-done.2.refs_3_.refs_12_), channel_id=1, source_target_pairs={{0,4},{4,8},{8,12},{12,16},{16,20},{20,24},{24,28},{28,0},{1,5},{5... | collective-permute-start | bytes 1597448 | tf_op jit(solution)/shard_map/ppermute | solution.py:22
  48.6 0.9 slice_select_fusion
  49.4 1.9 %collective-permute-start.9 = (bf16[2112,128]{1,0:T(8,128)(2,1)}, bf16[2112,128]{1,0:T(8,128)(2,1)S(1)}, u32[]{:S(2)}, u32[]{:S(2)}) collective-permute-start(bf16[2112,128]{1,0:T(8,128)(2,1)} %slice_select_fusion), channel_id=1, source_target_pairs={{0,448},{32,96},{64,0},{96,160},{128,64},{160,224},{192,128},{224,... | collective-permute-start | bytes 1622024 | tf_op jit(solution)/shard_map/ppermute | solution.py:310
  51.3 1.8 %collective-permute-done.5.refs_6_.refs_15_ = bf16[2,1040,128]{2,1,0:T(8,128)(2,1)S(1)} collective-permute-done((bf16[2,1040,128]{2,1,0:T(8,128)(2,1)}, bf16[2,1040,128]{2,1,0:T(8,128)(2,1)S(1)}, u32[]{:S(2)}, u32[]{:S(2)}) %collective-permute-start.5) | collective-permute-done | bytes 532512 | tf_op jit(solution)/shard_map/ppermute | solution.py:22
  53.1 0.8 slice_bitcast_fusion
  53.9 5.2 %collective-permute-start.7 = (bf16[1040,128]{1,0:T(8,128)(2,1)}, bf16[1040,128]{1,0:T(8,128)(2,1)}, u32[]{:S(2)}, u32[]{:S(2)}) collective-permute-start(bf16[1040,128]{1,0:T(8,128)(2,1)} %slice_bitcast_fusion), channel_id=1, source_target_pairs={{0,28},{4,0},{8,4},{12,8},{16,12},{20,16},{24,20},{28,24},{1,29},{... | collective-permute-start | bytes 798728 | tf_op jit(solution)/shard_map/ppermute | solution.py:22
  59.1 0.0 collective-permute-done.4.refs_5_.refs_14_
  59.1 0.8 slice_bitcast_fusion.1
  59.9 0.1 copy-done.1
  60.0 1.9 %collective-permute-start.6 = (bf16[1040,128]{1,0:T(8,128)(2,1)}, bf16[1040,128]{1,0:T(8,128)(2,1)S(1)}, u32[]{:S(2)}, u32[]{:S(2)}) collective-permute-start(bf16[1040,128]{1,0:T(8,128)(2,1)} %slice_bitcast_fusion.1), channel_id=1, source_target_pairs={{0,4},{4,8},{8,12},{12,16},{16,20},{20,24},{24,28},{28,0},{1,5},{5... | collective-permute-start | bytes 798728 | tf_op jit(solution)/shard_map/ppermute | solution.py:22
  61.9 0.1 pad_add_fusion.here_ref
  62.0 0.0 collective-permute-done.9.refs_22_
  62.0 1.7 %collective-permute-done.7.refs_8_ = bf16[1040,128]{1,0:T(8,128)(2,1)} collective-permute-done((bf16[1040,128]{1,0:T(8,128)(2,1)}, bf16[1040,128]{1,0:T(8,128)(2,1)}, u32[]{:S(2)}, u32[]{:S(2)}) %collective-permute-start.7) | collective-permute-done | bytes 266272 | tf_op jit(solution)/shard_map/ppermute | solution.py:22
  63.7 5.8 %collective-permute-done.6.refs_7_.refs_16_ = bf16[1040,128]{1,0:T(8,128)(2,1)S(1)} collective-permute-done((bf16[1040,128]{1,0:T(8,128)(2,1)}, bf16[1040,128]{1,0:T(8,128)(2,1)S(1)}, u32[]{:S(2)}, u32[]{:S(2)}) %collective-permute-start.6) | collective-permute-done | bytes 266272 | tf_op jit(solution)/shard_map/ppermute | solution.py:22
  69.6 0.0 collective-permute-done.8.refs_21_
  69.6 8.4 %shard_map.30 = (s16[4,2,1040,128]{3,2,1,0:T(8,128)(2,1)S(1)}, f32[2048,128]{1,0:T(8,128)S(1)}, s32[32,128]{1,0:T(8,128)}) custom-call(s32[3]{0:T(128)S(1)} %pad_add_fusion.here_ref, bf16[2,1040,128]{2,1,0:T(8,128)(2,1)S(1)} %shard_map.28.payload_ref.refs_0_.refs_9_, bf16[2,1040,128]{2,1,0:T(8,128)(2,1)} %collective-permute-done.refs_1_.refs_10_, ...), custom_call_target="tpu_custom_call" | custom-call | flops 2147483648 | bytes 12582912 | tf_op jit(solution)/shard_map/pallas_call | solution.py:168
  78.0 28.4 %all_to_all.10.refs_1_.refs_2_.refs_3_ = s16[4,2,1040,128]{3,2,1,0:T(8,128)(2,1)S(1)} all-to-all(s16[4,2,1040,128]{3,2,1,0:T(8,128)(2,1)S(1)} %get-tuple-element.10), channel_id=1, replica_groups=mesh['row'=16,'col'=8,'depth'=4] {'depth'}, dimensions={0} | all-to-all | bytes 4259840 | tf_op jit(solution)/shard_map/all_to_all | solution.py:320
  106.5 1.8 %shard_map.31 = bf16[2048,128]{1,0:T(8,128)(2,1)} custom-call(s32[3]{0:T(128)S(1)} %pad_add_fusion.here_ref, f32[2048,128]{1,0:T(8,128)S(1)} %get-tuple-element.9.refs_0_, s16[4,2,1040,128]{3,2,1,0:T(8,128)(2,1)S(1)} %all_to_all.10.refs_1_.refs_2_.refs_3_, s16[4,2,1040,128]{3,2,1,0:T(8,128)(2,1)S(1)} %all_to_all.10.refs_1_.refs_2_.refs_3_, ...), custom_call_target="tpu_custom_call" | custom-call | tf_op jit(solution)/shard_map/pallas_call | solution.py:221
  (5 shorter events, 0.0 us)
Async XLA Ops:
  1.1 17.4 %collective-permute-start.1 = (bf16[2,1040,128]{2,1,0:T(8,128)(2,1)S(1)}, bf16[2,1040,128]{2,1,0:T(8,128)(2,1)S(1)}, u32[]{:S(2)}, u32[]{:S(2)}) collective-permute-start(bf16[2,1040,128]{2,1,0:T(8,128)(2,1)S(1)} %shard_map.28.payload_ref.refs_0_.refs_9_), channel_id=1, source_target_pairs={{0,28},{4,0},{8,4},{12,8},{16,12},{20,16},{24,20},{28,24},{1,29},{... | collective-permute-start | bytes 1597448 | tf_op jit(solution)/shard_map/ppermute | solution.py:22
  7.0 14.3 %collective-permute-start = (bf16[2,1040,128]{2,1,0:T(8,128)(2,1)S(1)}, bf16[2,1040,128]{2,1,0:T(8,128)(2,1)}, u32[]{:S(2)}, u32[]{:S(2)}) collective-permute-start(bf16[2,1040,128]{2,1,0:T(8,128)(2,1)S(1)} %shard_map.28.payload_ref.refs_0_.refs_9_), channel_id=1, source_target_pairs={{0,4},{4,8},{8,12},{12,16},{16,20},{20,24},{24,28},{28,0},{1,5},{5... | collective-permute-start | bytes 1597448 | tf_op jit(solution)/shard_map/ppermute | solution.py:22
  10.1 24.1 %all-to-all-start = ((bf16[8,528,128]{2,1,0:T(8,128)(2,1)}), bf16[8,528,128]{2,1,0:T(8,128)(2,1)S(1)}, u32[]{:S(2)}, u32[]{:S(2)}) async-start(bf16[8,528,128]{2,1,0:T(8,128)(2,1)} %shard_map.29), calls=%async_computation | async-start | bytes 2162688 | tf_op jit(solution)/shard_map/all_to_all | solution.py:304
  18.4 30.1 %copy-start.2 = (bf16[2,1040,128]{2,1,0:T(8,128)(2,1)}, bf16[2,1040,128]{2,1,0:T(8,128)(2,1)S(1)}, u32[]{:S(2)}) copy-start(bf16[2,1040,128]{2,1,0:T(8,128)(2,1)S(1)} %collective-permute-done.1.refs_2_.refs_11_) | copy-start | bytes 1597444
  18.4 22.9 %collective-permute-start.3 = (bf16[2,1040,128]{2,1,0:T(8,128)(2,1)S(1)}, bf16[2,1040,128]{2,1,0:T(8,128)(2,1)}, u32[]{:S(2)}, u32[]{:S(2)}) collective-permute-start(bf16[2,1040,128]{2,1,0:T(8,128)(2,1)S(1)} %collective-permute-done.1.refs_2_.refs_11_), channel_id=1, source_target_pairs={{0,28},{4,0},{8,4},{12,8},{16,12},{20,16},{24,20},{28,24},{1,29},{... | collective-permute-start | bytes 1597448 | tf_op jit(solution)/shard_map/ppermute | solution.py:22
  21.3 25.3 %collective-permute-start.2 = (bf16[2,1040,128]{2,1,0:T(8,128)(2,1)}, bf16[2,1040,128]{2,1,0:T(8,128)(2,1)}, u32[]{:S(2)}, u32[]{:S(2)}) collective-permute-start(bf16[2,1040,128]{2,1,0:T(8,128)(2,1)} %collective-permute-done.refs_1_.refs_10_), channel_id=1, source_target_pairs={{0,4},{4,8},{8,12},{12,16},{16,20},{20,24},{24,28},{28,0},{1,5},{5... | collective-permute-start | bytes 1597448 | tf_op jit(solution)/shard_map/ppermute | solution.py:22
  34.2 35.4 %collective-permute-start.8 = (bf16[4224,128]{1,0:T(8,128)(2,1)S(1)}, bf16[4224,128]{1,0:T(8,128)(2,1)S(1)}, u32[]{:S(2)}, u32[]{:S(2)}) collective-permute-start(bf16[4224,128]{1,0:T(8,128)(2,1)S(1)} %bitcast.16), channel_id=1, source_target_pairs={{0,64},{32,480},{64,128},{96,32},{128,192},{160,96},{192,256},{224... | collective-permute-start | bytes 3244040 | tf_op jit(solution)/shard_map/ppermute | solution.py:307
  41.3 11.8 %collective-permute-start.5 = (bf16[2,1040,128]{2,1,0:T(8,128)(2,1)}, bf16[2,1040,128]{2,1,0:T(8,128)(2,1)S(1)}, u32[]{:S(2)}, u32[]{:S(2)}) collective-permute-start(bf16[2,1040,128]{2,1,0:T(8,128)(2,1)} %collective-permute-done.3.refs_4_.refs_13_), channel_id=1, source_target_pairs={{0,28},{4,0},{8,4},{12,8},{16,12},{20,16},{24,20},{28,24},{1,29},{... | collective-permute-start | bytes 1597448 | tf_op jit(solution)/shard_map/ppermute | solution.py:22
  46.6 12.5 %collective-permute-start.4 = (bf16[2,1040,128]{2,1,0:T(8,128)(2,1)}, bf16[2,1040,128]{2,1,0:T(8,128)(2,1)S(1)}, u32[]{:S(2)}, u32[]{:S(2)}) collective-permute-start(bf16[2,1040,128]{2,1,0:T(8,128)(2,1)} %collective-permute-done.2.refs_3_.refs_12_), channel_id=1, source_target_pairs={{0,4},{4,8},{8,12},{12,16},{16,20},{20,24},{24,28},{28,0},{1,5},{5... | collective-permute-start | bytes 1597448 | tf_op jit(solution)/shard_map/ppermute | solution.py:22
  49.4 12.6 %collective-permute-start.9 = (bf16[2112,128]{1,0:T(8,128)(2,1)}, bf16[2112,128]{1,0:T(8,128)(2,1)S(1)}, u32[]{:S(2)}, u32[]{:S(2)}) collective-permute-start(bf16[2112,128]{1,0:T(8,128)(2,1)} %slice_select_fusion), channel_id=1, source_target_pairs={{0,448},{32,96},{64,0},{96,160},{128,64},{160,224},{192,128},{224,... | collective-permute-start | bytes 1622024 | tf_op jit(solution)/shard_map/ppermute | solution.py:310
  53.1 6.0 %copy-start = (bf16[2,1040,128]{2,1,0:T(8,128)(2,1)}, bf16[2,1040,128]{2,1,0:T(8,128)(2,1)S(1)}, u32[]{:S(2)}) copy-start(bf16[2,1040,128]{2,1,0:T(8,128)(2,1)S(1)} %collective-permute-done.5.refs_6_.refs_15_) | copy-start | bytes 1597444
  53.9 9.8 %collective-permute-start.7 = (bf16[1040,128]{1,0:T(8,128)(2,1)}, bf16[1040,128]{1,0:T(8,128)(2,1)}, u32[]{:S(2)}, u32[]{:S(2)}) collective-permute-start(bf16[1040,128]{1,0:T(8,128)(2,1)} %slice_bitcast_fusion), channel_id=1, source_target_pairs={{0,28},{4,0},{8,4},{12,8},{16,12},{20,16},{24,20},{28,24},{1,29},{... | collective-permute-start | bytes 798728 | tf_op jit(solution)/shard_map/ppermute | solution.py:22
  59.1 0.9 copy-start.1
  60.0 9.6 %collective-permute-start.6 = (bf16[1040,128]{1,0:T(8,128)(2,1)}, bf16[1040,128]{1,0:T(8,128)(2,1)S(1)}, u32[]{:S(2)}, u32[]{:S(2)}) collective-permute-start(bf16[1040,128]{1,0:T(8,128)(2,1)} %slice_bitcast_fusion.1), channel_id=1, source_target_pairs={{0,4},{4,8},{8,12},{12,16},{16,20},{20,24},{24,28},{28,0},{1,5},{5... | collective-permute-start | bytes 798728 | tf_op jit(solution)/shard_map/ppermute | solution.py:22

commit v8 on v6

--- a/solution.py
+++ b/solution.py
@@ -169,7 +169,7 @@
         functools.partial(product_kernel, first, start, half_rows, classes, matrix_rows),
         grid_spec=grid_spec,
         out_shape=out_shape,
-        compiler_params=pltpu.CompilerParams(vmem_limit_bytes=20 * 2**20),
+        compiler_params=pltpu.CompilerParams(vmem_limit_bytes=14 * 2**20),
         cost_estimate=pl.CostEstimate(
             flops=2 * rows * 32 * BS**3, bytes_accessed=12 * 2**20, transcendentals=0
         ),

time: 109 us -> 110 us (level)
  no operation moved by 1% of the time
where the time goes in v8:
time: 110 us; the launch traced here: 108 us
  starting transfers between devices  44.8 us (41%)
  blocking collectives  28.4 us (26%)
  waiting for transfers between devices  19.8 us (18%)
  Pallas kernels  12.2 us (11%)
  local copies, waits for them, and re-layouts  1.67 us (2%)
    all_to_all x1, blocking collectives, shards(): parts.append((mine, lax.all_to_all(coded, 'depth', 0, 0)))  28.4 us
    ppermute x8, starting transfers between devices, passed_along(): lax.ppermute(block, axis, [(i, (i + distance) % n) for i in range(n)])  27.4 us
    all_to_all x1, waiting for transfers between devices, shards(): lax.all_to_all(pieces, ('row', 'depth'), 0, 0, axis_index_groups=groups)  10.4 us
    ppermute x8, waiting for transfers between devices, passed_along(): lax.ppermute(block, axis, [(i, (i + distance) % n) for i in range(n)])  9.35 us
    all_to_all x1, starting transfers between devices, shards(): lax.all_to_all(pieces, ('row', 'depth'), 0, 0, axis_index_groups=groups)  8.35 us
    pallas_call x1, Pallas kernels, products(): pl.pallas_call(functools.partial(product_kernel, first, start, half_rows,...  8.21 us
    ppermute x1, starting transfers between devices, shards(): lax.ppermute(pair, 'row', [(i, (i + (2 if i % 2 == 0 else -2)) % n_panels...  7.15 us
  transfers between devices with their start and end apart: 11, of which 4 were waited for; matrix products, arithmetic and copies ran while one was open for 2% of the time, Pallas kernels for 1%

profile of v8, /device:TPU:1, one launch (start us, length us, event | category | flops | bytes accessed | tf_op | source)
XLA Modules:
  0.0 108.0 jit_solution(12677978462187997931)
XLA Ops:
  0.0 1.1 shard_map.28.payload_ref.refs_0_.refs_9_
  1.1 5.9 %collective-permute-start.1 = (bf16[2,1040,128]{2,1,0:T(8,128)(2,1)S(1)}, bf16[2,1040,128]{2,1,0:T(8,128)(2,1)S(1)}, u32[]{:S(2)}, u32[]{:S(2)}) collective-permute-start(bf16[2,1040,128]{2,1,0:T(8,128)(2,1)S(1)} %shard_map.28.payload_ref.refs_0_.refs_9_), channel_id=1, source_target_pairs={{0,28},{4,0},{8,4},{12,8},{16,12},{20,16},{24,20},{28,24},{1,29},{... | collective-permute-start | bytes 1597448 | tf_op jit(solution)/shard_map/ppermute | solution.py:22
  7.0 1.9 %collective-permute-start = (bf16[2,1040,128]{2,1,0:T(8,128)(2,1)S(1)}, bf16[2,1040,128]{2,1,0:T(8,128)(2,1)}, u32[]{:S(2)}, u32[]{:S(2)}) collective-permute-start(bf16[2,1040,128]{2,1,0:T(8,128)(2,1)S(1)} %shard_map.28.payload_ref.refs_0_.refs_9_), channel_id=1, source_target_pairs={{0,4},{4,8},{8,12},{12,16},{16,20},{20,24},{24,28},{28,0},{1,5},{5... | collective-permute-start | bytes 1597448 | tf_op jit(solution)/shard_map/ppermute | solution.py:22
  8.9 1.1 %shard_map.29 = bf16[8,528,128]{2,1,0:T(8,128)(2,1)} custom-call(bf16[2,1040,128]{2,1,0:T(8,128)(2,1)S(1)} %shard_map.28.payload_ref.refs_0_.refs_9_), custom_call_target="tpu_custom_call" | custom-call | tf_op jit(solution)/shard_map/pallas_call | solution.py:273
  10.1 8.4 %all-to-all-start = ((bf16[8,528,128]{2,1,0:T(8,128)(2,1)}), bf16[8,528,128]{2,1,0:T(8,128)(2,1)S(1)}, u32[]{:S(2)}, u32[]{:S(2)}) async-start(bf16[8,528,128]{2,1,0:T(8,128)(2,1)} %shard_map.29), calls=%async_computation | async-start | bytes 2162688 | tf_op jit(solution)/shard_map/all_to_all | solution.py:304
  18.4 0.0 collective-permute-done.1.refs_2_.refs_11_
  18.4 2.9 %collective-permute-start.3 = (bf16[2,1040,128]{2,1,0:T(8,128)(2,1)S(1)}, bf16[2,1040,128]{2,1,0:T(8,128)(2,1)}, u32[]{:S(2)}, u32[]{:S(2)}) collective-permute-start(bf16[2,1040,128]{2,1,0:T(8,128)(2,1)S(1)} %collective-permute-done.1.refs_2_.refs_11_), channel_id=1, source_target_pairs={{0,28},{4,0},{8,4},{12,8},{16,12},{20,16},{24,20},{28,24},{1,29},{... | collective-permute-start | bytes 1597448 | tf_op jit(solution)/shard_map/ppermute | solution.py:22
  21.3 0.0 collective-permute-done.refs_1_.refs_10_
  21.3 2.4 %collective-permute-start.2 = (bf16[2,1040,128]{2,1,0:T(8,128)(2,1)}, bf16[2,1040,128]{2,1,0:T(8,128)(2,1)}, u32[]{:S(2)}, u32[]{:S(2)}) collective-permute-start(bf16[2,1040,128]{2,1,0:T(8,128)(2,1)} %collective-permute-done.refs_1_.refs_10_), channel_id=1, source_target_pairs={{0,4},{4,8},{8,12},{12,16},{16,20},{20,24},{24,28},{28,0},{1,5},{5... | collective-permute-start | bytes 1597448 | tf_op jit(solution)/shard_map/ppermute | solution.py:22
  23.8 10.4 %all-to-all-done = bf16[8,528,128]{2,1,0:T(8,128)(2,1)S(1)} async-done(((bf16[8,528,128]{2,1,0:T(8,128)(2,1)}), bf16[8,528,128]{2,1,0:T(8,128)(2,1)S(1)}, u32[]{:S(2)}, u32[]{:S(2)}) %all-to-all-start) | async-done | bytes 1081376 | tf_op jit(solution)/shard_map/all_to_all | solution.py:304
  34.2 7.2 %collective-permute-start.8 = (bf16[4224,128]{1,0:T(8,128)(2,1)S(1)}, bf16[4224,128]{1,0:T(8,128)(2,1)S(1)}, u32[]{:S(2)}, u32[]{:S(2)}) collective-permute-start(bf16[4224,128]{1,0:T(8,128)(2,1)S(1)} %bitcast.16), channel_id=1, source_target_pairs={{0,64},{32,480},{64,128},{96,32},{128,192},{160,96},{192,256},{224... | collective-permute-start | bytes 3244040 | tf_op jit(solution)/shard_map/ppermute | solution.py:307
  41.3 0.0 collective-permute-done.3.refs_4_.refs_13_
  41.3 5.3 %collective-permute-start.5 = (bf16[2,1040,128]{2,1,0:T(8,128)(2,1)}, bf16[2,1040,128]{2,1,0:T(8,128)(2,1)S(1)}, u32[]{:S(2)}, u32[]{:S(2)}) collective-permute-start(bf16[2,1040,128]{2,1,0:T(8,128)(2,1)} %collective-permute-done.3.refs_4_.refs_13_), channel_id=1, source_target_pairs={{0,28},{4,0},{8,4},{12,8},{16,12},{20,16},{24,20},{28,24},{1,29},{... | collective-permute-start | bytes 1597448 | tf_op jit(solution)/shard_map/ppermute | solution.py:22
  46.6 0.0 collective-permute-done.2.refs_3_.refs_12_
  46.6 1.9 %collective-permute-start.4 = (bf16[2,1040,128]{2,1,0:T(8,128)(2,1)}, bf16[2,1040,128]{2,1,0:T(8,128)(2,1)S(1)}, u32[]{:S(2)}, u32[]{:S(2)}) collective-permute-start(bf16[2,1040,128]{2,1,0:T(8,128)(2,1)} %collective-permute-done.2.refs_3_.refs_12_), channel_id=1, source_target_pairs={{0,4},{4,8},{8,12},{12,16},{16,20},{20,24},{24,28},{28,0},{1,5},{5... | collective-permute-start | bytes 1597448 | tf_op jit(solution)/shard_map/ppermute | solution.py:22
  48.6 0.9 slice_select_fusion
  49.4 1.9 %collective-permute-start.9 = (bf16[2112,128]{1,0:T(8,128)(2,1)}, bf16[2112,128]{1,0:T(8,128)(2,1)S(1)}, u32[]{:S(2)}, u32[]{:S(2)}) collective-permute-start(bf16[2112,128]{1,0:T(8,128)(2,1)} %slice_select_fusion), channel_id=1, source_target_pairs={{0,448},{32,96},{64,0},{96,160},{128,64},{160,224},{192,128},{224,... | collective-permute-start | bytes 1622024 | tf_op jit(solution)/shard_map/ppermute | solution.py:310
  51.3 1.8 %collective-permute-done.5.refs_6_.refs_15_ = bf16[2,1040,128]{2,1,0:T(8,128)(2,1)S(1)} collective-permute-done((bf16[2,1040,128]{2,1,0:T(8,128)(2,1)}, bf16[2,1040,128]{2,1,0:T(8,128)(2,1)S(1)}, u32[]{:S(2)}, u32[]{:S(2)}) %collective-permute-start.5) | collective-permute-done | bytes 532512 | tf_op jit(solution)/shard_map/ppermute | solution.py:22
  53.1 0.8 slice_bitcast_fusion
  53.9 5.2 %collective-permute-start.7 = (bf16[1040,128]{1,0:T(8,128)(2,1)}, bf16[1040,128]{1,0:T(8,128)(2,1)}, u32[]{:S(2)}, u32[]{:S(2)}) collective-permute-start(bf16[1040,128]{1,0:T(8,128)(2,1)} %slice_bitcast_fusion), channel_id=1, source_target_pairs={{0,28},{4,0},{8,4},{12,8},{16,12},{20,16},{24,20},{28,24},{1,29},{... | collective-permute-start | bytes 798728 | tf_op jit(solution)/shard_map/ppermute | solution.py:22
  59.1 0.0 collective-permute-done.4.refs_5_.refs_14_
  59.1 0.8 slice_bitcast_fusion.1
  59.9 0.1 copy-done.1
  60.0 1.9 %collective-permute-start.6 = (bf16[1040,128]{1,0:T(8,128)(2,1)}, bf16[1040,128]{1,0:T(8,128)(2,1)S(1)}, u32[]{:S(2)}, u32[]{:S(2)}) collective-permute-start(bf16[1040,128]{1,0:T(8,128)(2,1)} %slice_bitcast_fusion.1), channel_id=1, source_target_pairs={{0,4},{4,8},{8,12},{12,16},{16,20},{20,24},{24,28},{28,0},{1,5},{5... | collective-permute-start | bytes 798728 | tf_op jit(solution)/shard_map/ppermute | solution.py:22
  61.9 0.1 pad_add_fusion.here_ref
  62.0 0.0 collective-permute-done.9.refs_22_
  62.0 1.7 %collective-permute-done.7.refs_8_ = bf16[1040,128]{1,0:T(8,128)(2,1)} collective-permute-done((bf16[1040,128]{1,0:T(8,128)(2,1)}, bf16[1040,128]{1,0:T(8,128)(2,1)}, u32[]{:S(2)}, u32[]{:S(2)}) %collective-permute-start.7) | collective-permute-done | bytes 266272 | tf_op jit(solution)/shard_map/ppermute | solution.py:22
  63.7 5.8 %collective-permute-done.6.refs_7_.refs_16_ = bf16[1040,128]{1,0:T(8,128)(2,1)S(1)} collective-permute-done((bf16[1040,128]{1,0:T(8,128)(2,1)}, bf16[1040,128]{1,0:T(8,128)(2,1)S(1)}, u32[]{:S(2)}, u32[]{:S(2)}) %collective-permute-start.6) | collective-permute-done | bytes 266272 | tf_op jit(solution)/shard_map/ppermute | solution.py:22
  69.6 0.0 collective-permute-done.8.refs_21_
  69.6 8.2 %shard_map.30 = (s16[4,2,1040,128]{3,2,1,0:T(8,128)(2,1)S(1)}, f32[2048,128]{1,0:T(8,128)S(1)}, s32[32,128]{1,0:T(8,128)}) custom-call(s32[3]{0:T(128)S(1)} %pad_add_fusion.here_ref, bf16[2,1040,128]{2,1,0:T(8,128)(2,1)S(1)} %shard_map.28.payload_ref.refs_0_.refs_9_, bf16[2,1040,128]{2,1,0:T(8,128)(2,1)} %collective-permute-done.refs_1_.refs_10_, ...), custom_call_target="tpu_custom_call" | custom-call | flops 2147483648 | bytes 12582912 | tf_op jit(solution)/shard_map/pallas_call | solution.py:168
  77.8 28.4 %all_to_all.10.refs_1_.refs_2_.refs_3_ = s16[4,2,1040,128]{3,2,1,0:T(8,128)(2,1)S(1)} all-to-all(s16[4,2,1040,128]{3,2,1,0:T(8,128)(2,1)S(1)} %get-tuple-element.10), channel_id=1, replica_groups=mesh['row'=16,'col'=8,'depth'=4] {'depth'}, dimensions={0} | all-to-all | bytes 4259840 | tf_op jit(solution)/shard_map/all_to_all | solution.py:320
  106.2 1.8 %shard_map.31 = bf16[2048,128]{1,0:T(8,128)(2,1)} custom-call(s32[3]{0:T(128)S(1)} %pad_add_fusion.here_ref, f32[2048,128]{1,0:T(8,128)S(1)} %get-tuple-element.9.refs_0_, s16[4,2,1040,128]{3,2,1,0:T(8,128)(2,1)S(1)} %all_to_all.10.refs_1_.refs_2_.refs_3_, s16[4,2,1040,128]{3,2,1,0:T(8,128)(2,1)S(1)} %all_to_all.10.refs_1_.refs_2_.refs_3_, ...), custom_call_target="tpu_custom_call" | custom-call | tf_op jit(solution)/shard_map/pallas_call | solution.py:221
  (5 shorter events, 0.0 us)
Async XLA Ops:
  1.1 17.4 %collective-permute-start.1 = (bf16[2,1040,128]{2,1,0:T(8,128)(2,1)S(1)}, bf16[2,1040,128]{2,1,0:T(8,128)(2,1)S(1)}, u32[]{:S(2)}, u32[]{:S(2)}) collective-permute-start(bf16[2,1040,128]{2,1,0:T(8,128)(2,1)S(1)} %shard_map.28.payload_ref.refs_0_.refs_9_), channel_id=1, source_target_pairs={{0,28},{4,0},{8,4},{12,8},{16,12},{20,16},{24,20},{28,24},{1,29},{... | collective-permute-start | bytes 1597448 | tf_op jit(solution)/shard_map/ppermute | solution.py:22
  7.0 14.3 %collective-permute-start = (bf16[2,1040,128]{2,1,0:T(8,128)(2,1)S(1)}, bf16[2,1040,128]{2,1,0:T(8,128)(2,1)}, u32[]{:S(2)}, u32[]{:S(2)}) collective-permute-start(bf16[2,1040,128]{2,1,0:T(8,128)(2,1)S(1)} %shard_map.28.payload_ref.refs_0_.refs_9_), channel_id=1, source_target_pairs={{0,4},{4,8},{8,12},{12,16},{16,20},{20,24},{24,28},{28,0},{1,5},{5... | collective-permute-start | bytes 1597448 | tf_op jit(solution)/shard_map/ppermute | solution.py:22
  10.1 24.1 %all-to-all-start = ((bf16[8,528,128]{2,1,0:T(8,128)(2,1)}), bf16[8,528,128]{2,1,0:T(8,128)(2,1)S(1)}, u32[]{:S(2)}, u32[]{:S(2)}) async-start(bf16[8,528,128]{2,1,0:T(8,128)(2,1)} %shard_map.29), calls=%async_computation | async-start | bytes 2162688 | tf_op jit(solution)/shard_map/all_to_all | solution.py:304
  18.4 30.1 %copy-start.2 = (bf16[2,1040,128]{2,1,0:T(8,128)(2,1)}, bf16[2,1040,128]{2,1,0:T(8,128)(2,1)S(1)}, u32[]{:S(2)}) copy-start(bf16[2,1040,128]{2,1,0:T(8,128)(2,1)S(1)} %collective-permute-done.1.refs_2_.refs_11_) | copy-start | bytes 1597444
  18.4 22.9 %collective-permute-start.3 = (bf16[2,1040,128]{2,1,0:T(8,128)(2,1)S(1)}, bf16[2,1040,128]{2,1,0:T(8,128)(2,1)}, u32[]{:S(2)}, u32[]{:S(2)}) collective-permute-start(bf16[2,1040,128]{2,1,0:T(8,128)(2,1)S(1)} %collective-permute-done.1.refs_2_.refs_11_), channel_id=1, source_target_pairs={{0,28},{4,0},{8,4},{12,8},{16,12},{20,16},{24,20},{28,24},{1,29},{... | collective-permute-start | bytes 1597448 | tf_op jit(solution)/shard_map/ppermute | solution.py:22
  21.3 25.3 %collective-permute-start.2 = (bf16[2,1040,128]{2,1,0:T(8,128)(2,1)}, bf16[2,1040,128]{2,1,0:T(8,128)(2,1)}, u32[]{:S(2)}, u32[]{:S(2)}) collective-permute-start(bf16[2,1040,128]{2,1,0:T(8,128)(2,1)} %collective-permute-done.refs_1_.refs_10_), channel_id=1, source_target_pairs={{0,4},{4,8},{8,12},{12,16},{16,20},{20,24},{24,28},{28,0},{1,5},{5... | collective-permute-start | bytes 1597448 | tf_op jit(solution)/shard_map/ppermute | solution.py:22
  34.2 35.4 %collective-permute-start.8 = (bf16[4224,128]{1,0:T(8,128)(2,1)S(1)}, bf16[4224,128]{1,0:T(8,128)(2,1)S(1)}, u32[]{:S(2)}, u32[]{:S(2)}) collective-permute-start(bf16[4224,128]{1,0:T(8,128)(2,1)S(1)} %bitcast.16), channel_id=1, source_target_pairs={{0,64},{32,480},{64,128},{96,32},{128,192},{160,96},{192,256},{224... | collective-permute-start | bytes 3244040 | tf_op jit(solution)/shard_map/ppermute | solution.py:307
  41.3 11.8 %collective-permute-start.5 = (bf16[2,1040,128]{2,1,0:T(8,128)(2,1)}, bf16[2,1040,128]{2,1,0:T(8,128)(2,1)S(1)}, u32[]{:S(2)}, u32[]{:S(2)}) collective-permute-start(bf16[2,1040,128]{2,1,0:T(8,128)(2,1)} %collective-permute-done.3.refs_4_.refs_13_), channel_id=1, source_target_pairs={{0,28},{4,0},{8,4},{12,8},{16,12},{20,16},{24,20},{28,24},{1,29},{... | collective-permute-start | bytes 1597448 | tf_op jit(solution)/shard_map/ppermute | solution.py:22
  46.6 12.5 %collective-permute-start.4 = (bf16[2,1040,128]{2,1,0:T(8,128)(2,1)}, bf16[2,1040,128]{2,1,0:T(8,128)(2,1)S(1)}, u32[]{:S(2)}, u32[]{:S(2)}) collective-permute-start(bf16[2,1040,128]{2,1,0:T(8,128)(2,1)} %collective-permute-done.2.refs_3_.refs_12_), channel_id=1, source_target_pairs={{0,4},{4,8},{8,12},{12,16},{16,20},{20,24},{24,28},{28,0},{1,5},{5... | collective-permute-start | bytes 1597448 | tf_op jit(solution)/shard_map/ppermute | solution.py:22
  49.4 12.6 %collective-permute-start.9 = (bf16[2112,128]{1,0:T(8,128)(2,1)}, bf16[2112,128]{1,0:T(8,128)(2,1)S(1)}, u32[]{:S(2)}, u32[]{:S(2)}) collective-permute-start(bf16[2112,128]{1,0:T(8,128)(2,1)} %slice_select_fusion), channel_id=1, source_target_pairs={{0,448},{32,96},{64,0},{96,160},{128,64},{160,224},{192,128},{224,... | collective-permute-start | bytes 1622024 | tf_op jit(solution)/shard_map/ppermute | solution.py:310
  53.1 6.0 %copy-start = (bf16[2,1040,128]{2,1,0:T(8,128)(2,1)}, bf16[2,1040,128]{2,1,0:T(8,128)(2,1)S(1)}, u32[]{:S(2)}) copy-start(bf16[2,1040,128]{2,1,0:T(8,128)(2,1)S(1)} %collective-permute-done.5.refs_6_.refs_15_) | copy-start | bytes 1597444
  53.9 9.8 %collective-permute-start.7 = (bf16[1040,128]{1,0:T(8,128)(2,1)}, bf16[1040,128]{1,0:T(8,128)(2,1)}, u32[]{:S(2)}, u32[]{:S(2)}) collective-permute-start(bf16[1040,128]{1,0:T(8,128)(2,1)} %slice_bitcast_fusion), channel_id=1, source_target_pairs={{0,28},{4,0},{8,4},{12,8},{16,12},{20,16},{24,20},{28,24},{1,29},{... | collective-permute-start | bytes 798728 | tf_op jit(solution)/shard_map/ppermute | solution.py:22
  59.1 0.9 copy-start.1
  60.0 9.6 %collective-permute-start.6 = (bf16[1040,128]{1,0:T(8,128)(2,1)}, bf16[1040,128]{1,0:T(8,128)(2,1)S(1)}, u32[]{:S(2)}, u32[]{:S(2)}) collective-permute-start(bf16[1040,128]{1,0:T(8,128)(2,1)} %slice_bitcast_fusion.1), channel_id=1, source_target_pairs={{0,4},{4,8},{8,12},{12,16},{16,20},{20,24},{24,28},{28,0},{1,5},{5... | collective-permute-start | bytes 798728 | tf_op jit(solution)/shard_map/ppermute | solution.py:22
